TPU v7x, 256 devices: a whole 4x4x8 slice. The times are simulated.
256 devices in a mesh: ctx: 16 (over y_lo, z), head: 16 (over y_hi, x, core).
Axes of the slice: x: 4, y: 4 (y_hi: 2, y_lo: 2; y = y_hi * 2 + y_lo), z: 8, core: 2. Of those that a mesh axis runs over, the one named last changes fastest.
Arguments:
- q_nope: bfloat16 [2, 1024, 16384], P(None, 'ctx', 'head'), may hold values from -6 to 6
- q_rope: bfloat16 [2, 1024, 8192], P(None, 'ctx', 'head'), may hold values from -8 to 8
- cache_latent: bfloat16 [2, 1024, 576], P(None, 'ctx'), may hold values from -8 to 8
- stretch_latent: bfloat16 [2, 1024, 576], P(None, 'ctx'), may hold values from -6 to 6
- w_uk: bfloat16 [512, 16384], P(None, 'head'), may hold values from -0.25 to 0.25
- w_uv: bfloat16 [512, 16384], P(None, 'head'), may hold values from -0.25 to 0.25
- w_o: bfloat16 [16384, 7168], P('head', 'ctx'), may hold values from -1.1953125 to 1.1953125
- stretch_start: int32 [2], replicated, may hold values from 256 to 1024, as said below
- prompt_len: int32 [2], replicated, may hold values from 512 to 2048, as said below
Outputs:
- mixed: bfloat16 [2, 1024, 7168], P(None, 'head', 'ctx')
Inputs may be any that keep to these rules, and one draw needn't show every extreme that they name: `stretch_start`: cached positions before the stretch; some sequence has exactly 1024. `prompt_len`: stretch_start plus the sequence's live stretch positions, which lie between 256 and 1024; some sequence fills both its cache and its stretch.
All inputs are finite; a program needn't handle non-finite values.
Results may differ from a plain program's by a relative error of at most 0.02.
Values may be sent and summed in bfloat16 or wider, within the bound.
No kernel may reach another device: no remote copies, remote signals or barrier semaphores. Data moves between devices by JAX's collectives and lax.ppermute only.
A program may use at most 128 MiB of HBM per device.

v0:
```python
import jax
import jax.numpy as jnp
from jax import lax
from jax.sharding import PartitionSpec as P

LATENT = 512
ROPE = 64
NOPE = 128


neg_fill = -1e30


def online(state_in, scores, visible, values_fn):
    running_max, weight_sum, weighted = state_in
    scores = jnp.where(visible, scores, neg_fill)
    new_max = jnp.maximum(running_max, jnp.max(scores, axis=-1))
    factor = jnp.exp(running_max - new_max)
    weights = jnp.where(visible, jnp.exp(scores - new_max[..., None]), 0.0)
    weight_sum = weight_sum * factor + jnp.sum(weights, axis=-1)
    rounded = weights.astype(jnp.bfloat16)
    weighted = weighted * factor[..., None] + values_fn(rounded)
    return (new_max, weight_sum, weighted)


def local(q_nope, q_rope, cache_latent, stretch_latent, w_uk, w_uv, w_o, stretch_start, prompt_len):
    highest = lax.Precision.HIGHEST
    batch_seqs, query_rows, feature_width = q_nope.shape
    groups = feature_width // NOPE
    score_scale = (NOPE + ROPE) ** (-0.5)
    query_position = lax.axis_index("ctx") * query_rows + jnp.arange(query_rows, dtype=jnp.int32)
    queries = q_nope.reshape(batch_seqs, query_rows, groups, NOPE)
    query_rope = q_rope.reshape(batch_seqs, query_rows, groups, ROPE).astype(jnp.float32)
    query_wide = queries.astype(jnp.float32)
    value_width = NOPE

    def scorer(block_in):
        compressed = block_in[..., :LATENT]
        rope_keys = block_in[..., LATENT:].astype(jnp.float32)
        count_rows = block_in.shape[1]
        key_block = jnp.einsum("srl,lf->srf", compressed, w_uk, preferred_element_type=jnp.float32)
        key_block = key_block.reshape(batch_seqs, count_rows, groups, NOPE)
        value_block = jnp.einsum(
            "srl,lf->srf", compressed, w_uv, preferred_element_type=jnp.float32
        )
        value_block = value_block.reshape(batch_seqs, count_rows, groups, NOPE)
        scores = jnp.einsum("sqgd,srgd->sgqr", query_wide, key_block, precision=highest)
        scores = scores + jnp.einsum("sqge,sre->sgqr", query_rope, rope_keys, precision=highest)

        def values_fn(rounded):
            widened = lax.optimization_barrier(rounded).astype(jnp.float32)
            return jnp.einsum("sgqr,srgd->sgqd", widened, value_block, precision=highest)

        return (scores * score_scale, values_fn)

    def advance(state_in, block_in, visible):
        scores, values_fn = scorer(block_in)
        return online(state_in, scores, visible, values_fn)

    initial = (
        jnp.full((batch_seqs, groups, query_rows), neg_fill, jnp.float32),
        jnp.zeros((batch_seqs, groups, query_rows), jnp.float32),
        jnp.zeros((batch_seqs, groups, query_rows, value_width), jnp.float32),
    )
    block_in = lax.all_gather(cache_latent, "ctx", axis=1, tiled=True)
    key_position = jnp.arange(block_in.shape[1], dtype=jnp.int32)
    visible = (key_position[None, :] < stretch_start[:, None])[:, None, None, :]
    state_out = advance(initial, block_in, visible)
    block_in = lax.all_gather(stretch_latent, "ctx", axis=1, tiled=True)
    key_position = jnp.arange(block_in.shape[1], dtype=jnp.int32)
    visible = (key_position[None, :] <= query_position[:, None])[None, None, :, :]
    state_out = advance(state_out, block_in, visible)
    running_max, weight_sum, weighted = state_out
    normed = weighted / weight_sum[..., None]
    live_rows = query_position[None, :] < (prompt_len - stretch_start)[:, None]
    attention = jnp.where(
        live_rows[..., None],
        normed.transpose(0, 2, 1, 3).reshape(batch_seqs, query_rows, groups * NOPE),
        0.0,
    ).astype(jnp.bfloat16)
    partial_value = jnp.einsum(
        "sqf,fd->sqd",
        lax.all_gather(attention, "ctx", axis=1, tiled=True),
        w_o,
        preferred_element_type=jnp.float32,
    )
    return lax.psum_scatter(
        partial_value.astype(jnp.bfloat16), "head", scatter_dimension=1, tiled=True
    )


def solution(mesh):
    placed = (
        P(None, "ctx", "head"),
        P(None, "ctx", "head"),
        P(None, "ctx", None),
        P(None, "ctx", None),
        P(None, "head"),
        P(None, "head"),
        P("head", "ctx"),
        P(),
        P(),
    )
    return jax.shard_map(
        local, mesh=mesh, in_specs=placed, out_specs=P(None, "head", "ctx"), check_vma=False
    )
```

profile of v0, /device:TPU:8, one launch (start us, length us, event | category | flops | bytes accessed | tf_op | source)
XLA Modules:
  0.0 349.0 jit_solution(9522165260028953713)
XLA Ops:
  6.5 0.0 copy-start
  6.5 0.0 all-gather.4.cloned.1.call-start
  6.5 0.7 all-gather.4.cloned.1.call-update
  7.3 0.0 all-gather.6.cloned.1.call-start
  7.3 0.7 all-gather.6.cloned.1.call-update
  8.0 0.0 all-gather.8.cloned.1.call-start
  8.1 1.1 reshape.125
  9.2 0.7 sub.43
  9.8 0.1 broadcast_compare_fusion
  9.9 0.7 iota_compare_fusion.1
  10.7 0.1 iota_compare_fusion
  10.8 0.0 copy-start.3
  10.8 73.4 %all-gather.4.cloned.1.call-done = bf16[2,1024,576]{2,1,0:T(8,128)(2,1)} async-done(((bf16[2,64,576]{2,1,0:T(8,128)(2,1)}), bf16[2,1024,576]{2,1,0:T(8,128)(2,1)}) %all-gather.4.cloned.1.call-update) | async-done | bytes 2359312 | tf_op jit(solution)/shard_map/all_gather | solution.py:65
  84.2 0.0 copy-done
  84.2 4.0 %fusion.14 = f32[2,1024,1024]{1,2,0:T(8,128)S(1)} fusion(bf16[2,1024,576]{2,1,0:T(8,128)(2,1)} %all-gather.4.cloned.1.call-done, bf16[512,1024]{1,0:T(8,128)(2,1)S(1)} %copy-done), kind=kOutput, calls=%fused_computation.19 | convolution fusion | flops 2147483648 | bytes 11534336 | tf_op jit(solution)/shard_map/srl,lf->srf/dot_general | solution.py:41
  88.2 0.0 copy-done.3
  88.2 4.9 %fusion.29 = f32[2,8,1024,64]{2,3,1,0:T(8,128)} fusion(f32[2,1024,8,128]{1,3,2,0:T(8,128)S(1)} %bitcast.111, bf16[2,64,1024]{2,1,0:T(8,128)(2,1)S(1)} %copy-done.3), kind=kOutput, calls=%fused_computation.39 | convolution fusion | flops 1610612736 | bytes 12845056 | tf_op jit(solution)/shard_map/sqgd,srgd->sgqr/dot_general | solution.py:47
  93.1 63.8 %all-gather.6.cloned.1.call-done = bf16[2,1024,576]{2,1,0:T(8,128)(2,1)} async-done(((bf16[2,64,576]{2,1,0:T(8,128)(2,1)}), bf16[2,1024,576]{2,1,0:T(8,128)(2,1)}) %all-gather.6.cloned.1.call-update) | async-done | bytes 2359312 | tf_op jit(solution)/shard_map/all_gather | solution.py:69
  156.9 4.0 %fusion.10 = f32[2,1024,1024]{1,2,0:T(8,128)S(1)} fusion(bf16[2,1024,576]{2,1,0:T(8,128)(2,1)} %all-gather.6.cloned.1.call-done, bf16[512,1024]{1,0:T(8,128)(2,1)S(1)} %copy-done), kind=kOutput, calls=%fused_computation.15 | convolution fusion | flops 2147483648 | bytes 11534336 | tf_op jit(solution)/shard_map/srl,lf->srf/dot_general | solution.py:41
  160.9 0.0 copy-start.2
  160.9 0.0 copy-start.4
  160.9 3.4 fusion.27
  164.3 0.0 copy-done.2
  164.3 0.0 copy-done.4
  164.3 0.0 copy-start.5
  164.3 0.9 fusion.41
  165.3 0.8 copy-done.5
  166.1 1.0 fusion.42
  167.1 0.0 copy-start.6
  167.1 2.3 fusion.4
  169.5 0.0 copy-done.6
  169.5 2.4 fusion.8
  171.9 4.9 %convolution_bitcast_fusion = f32[2,64,8,128]{3,1,2,0:T(8,128)S(1)} fusion(bf16[2,8,64,1024]{3,2,1,0:T(8,128)(2,1)S(1)} %get-tuple-element.18, f32[2,1024,8,128]{1,3,2,0:T(8,128)S(1)} %bitcast.110), kind=kOutput, calls=%fused_computation.21 | convolution fusion | flops 1610612736 | bytes 11010048 | tf_op jit(solution)/shard_map/sgqr,srgd->sgqd/dot_general | solution.py:52
  176.8 2.4 fusion.12
  179.2 0.0 copy-start.7
  179.2 5.2 %fusion.20 = bf16[2,8,8,8,128]{4,3,2,1,0:T(8,128)(2,1)S(1)} fusion(f32[2,64,8,128]{3,1,2,0:T(8,128)S(1)} %convolution_bitcast_fusion, bf16[2,8,64,1024]{3,2,1,0:T(8,128)(2,1)S(1)} %get-tuple-element.10, f32[2,1024,8,128]{1,3,2,0:T(8,128)S(1)} %bitcast.109, f32[2,64,8]{1,2,0:T(8,128)S(1)} %get-tuple-element.5, f32[2,64,8]{1,2,0:T(8,128)S(1)} %get-tuple-element.6, ...), kind=kOutput, calls=%fused_computation.27 | convolution fusion | flops 1611268096 | bytes 11284480 | tf_op jit(solution)/shard_map/sgqr,srgd->sgqd/dot_general | solution.py:52
  184.4 0.8 fusion.26
  185.2 0.0 all-gather.8.cloned.1.call-update
  185.2 0.0 reduce-scatter.2.cloned.1.call-start
  185.3 74.8 %all-gather.8.cloned.1.call-done = bf16[2,1024,1024]{2,1,0:T(8,128)(2,1)} async-done(((bf16[2,64,1024]{2,1,0:T(8,128)(2,1)}), bf16[2,1024,1024]{2,1,0:T(8,128)(2,1)}) %all-gather.8.cloned.1.call-update) | async-done | bytes 4194320 | tf_op jit(solution)/shard_map/all_gather | solution.py:83
  260.1 0.0 copy-done.7
  260.1 0.0 copy-start.1
  260.1 6.0 %convolution_convert_fusion = bf16[2,1024,448]{2,1,0:T(8,128)(2,1)} fusion(bf16[2,1024,1024]{2,1,0:T(8,128)(2,1)} %all-gather.8.cloned.1.call-done, bf16[1024,448]{0,1:T(8,128)(2,1)S(1)} %copy-done.7), kind=kOutput, calls=%fused_computation.12 | convolution fusion | flops 1879965696 | bytes 6946816 | tf_op jit(solution)/shard_map/sqf,fd->sqd/dot_general | solution.py:81
  266.1 0.0 reduce-scatter.2.cloned.1.call-update
  266.1 76.4 %reduce-scatter.2.cloned.1.call-done = bf16[2,64,448]{2,1,0:T(8,128)(2,1)} async-done(((bf16[2,1024,448]{2,1,0:T(8,128)(2,1)}), bf16[2,64,448]{2,1,0:T(8,128)(2,1)}) %reduce-scatter.2.cloned.1.call-update) | async-done | bytes 114704 | tf_op jit(solution)/shard_map/reduce_scatter | solution.py:87
  342.5 0.0 copy-done.1
  (3 shorter events, 0.0 us)
Async XLA Ops:
  6.5 77.7 %copy-start = (bf16[512,1024]{1,0:T(8,128)(2,1)S(1)}, bf16[512,1024]{1,0:T(8,128)(2,1)}, u32[]{:S(2)}) copy-start(bf16[512,1024]{1,0:T(8,128)(2,1)} %param.13) | copy-start | bytes 3145732
  6.5 77.7 %all-gather.4.cloned.1.call-start = ((), (), s32[]{:S(2)}) async-start(), calls=%async_computation.1 | async-start | bytes 2785280 | tf_op jit(solution)/shard_map/all_gather | solution.py:65
  7.3 149.7 %all-gather.6.cloned.1.call-start = ((), (), s32[]{:S(2)}) async-start(), calls=%async_computation.2 | async-start | bytes 2785280 | tf_op jit(solution)/shard_map/all_gather | solution.py:69
  8.0 252.1 %all-gather.8.cloned.1.call-start = ((), (), s32[]{:S(2)}) async-start(), calls=%async_computation.3 | async-start | bytes 4456448 | tf_op jit(solution)/shard_map/all_gather | solution.py:83
  10.8 77.4 %copy-start.3 = (bf16[2,64,1024]{2,1,0:T(8,128)(2,1)S(1)}, bf16[2,64,1024]{2,1,0:T(8,128)(2,1)}, u32[]{:S(2)}) copy-start(bf16[2,64,1024]{2,1,0:T(8,128)(2,1)} %param.9) | copy-start | bytes 786436
  160.9 3.4 copy-start.2
  160.9 3.4 copy-start.4
  164.3 1.7 copy-start.5
  167.1 2.4 copy-start.6
  179.2 80.9 %copy-start.7 = (bf16[1024,448]{0,1:T(8,128)(2,1)S(1)}, bf16[1024,448]{0,1:T(8,128)(2,1)}, u32[]{:S(2)}) copy-start(bf16[1024,448]{0,1:T(8,128)(2,1)} %param.15) | copy-start | bytes 2752516
  185.2 157.3 %reduce-scatter.2.cloned.1.call-start = ((), (), s32[]{:S(2)}) async-start(), calls=%async_computation.4 | async-start | bytes 2228224 | tf_op jit(solution)/shard_map/reduce_scatter | solution.py:87
  260.1 82.4 %copy-start.1 = (bf16[512,1024]{1,0:T(8,128)(2,1)S(1)}, bf16[512,1024]{1,0:T(8,128)(2,1)}, u32[]{:S(2)}) copy-start(bf16[512,1024]{1,0:T(8,128)(2,1)} %param.13) | copy-start | bytes 3145732
Sparse Core Ops, SparseCore 0:
  9.2 75.0 all-gather.3
  86.0 70.8 all-gather.5
  185.4 74.7 all-gather.7
  266.2 76.2 reduce-scatter.1
where the time goes:
time: 350 us; the launch traced here: 349 us
  waiting for transfers between devices  290 us (83%)
  matrix products  39 us (11%)
  between operations  13.3 us (4%)
  other arithmetic  4.77 us (1%)
    reduce_scatter x1, waiting for transfers between devices, local(): lax.psum_scatter(partial_value.astype(jnp.bfloat16), 'head', scatter_dime...  76.4 us
    all_gather x1, waiting for transfers between devices, local(): lax.all_gather(attention, 'ctx', axis=1, tiled=True)  74.8 us
    all_gather x1, waiting for transfers between devices, local(): block_in = lax.all_gather(cache_latent, 'ctx', axis=1, tiled=True)  73.4 us
    all_gather x1, waiting for transfers between devices, local(): block_in = lax.all_gather(stretch_latent, 'ctx', axis=1, tiled=True)  63.8 us
    dot_general x2, matrix products, values_fn(): jnp.einsum('sgqr,srgd->sgqd', widened, value_block, precision=highest)  10.1 us
    dot_general x2, matrix products, scorer(): jnp.einsum('sqgd,srgd->sgqr', query_wide, key_block, precision=highest)  8.29 us
    dot_general x2, matrix products, scorer(): jnp.einsum('srl,lf->srf', compressed, w_uk, preferred_element_type=jnp.fl...  7.94 us
  transfers between devices with their start and end apart: 4, of which 4 were waited for; matrix products, arithmetic and copies ran while one was open for 3% of the time, Pallas kernels for 0%

commit v1 on v0

v1 whole, which is shorter than its diff:
```python
import functools

import jax
import jax.numpy as jnp
from jax import lax
from jax.experimental import pallas as pl
from jax.experimental.pallas import tpu as pltpu
from jax.sharding import Mesh, PartitionSpec as P

LATENT = 512
ROPE = 64
NOPE = 128
LOG2E = 1.4426950408889634
HIDDEN = -1e30
GROUP = 4
VMEM_LIMIT = 56 * 1024 * 1024

f32 = jnp.float32
bf16 = jnp.bfloat16


def nt(a, b):
    return lax.dot_general(a, b, (((1,), (1,)), ((), ())), preferred_element_type=f32)


def nn(a, b):
    return jnp.dot(a, b, preferred_element_type=f32)


def attention_kernel(rows, heads, half, scale, *refs):
    info, qn0, qr0, qn1, qr1, wuk, wuv = refs[:7]
    pieces = refs[7:16]
    own, own_lse, message = refs[16:19]
    keys, bias, qaug = refs[19:]
    start, y, z = info[0], info[1], info[2]
    step = 2 * rows
    count = 8 * step
    for d in range(8):
        for part in range(2):
            at = d * step + part * rows
            if d == 4:
                piece = pieces[7 + part][...]
            else:
                piece = pieces[d if d < 4 else d - 1][part * rows : (part + 1) * rows, :]
            keys[at : at + rows, :LATENT] = piece[:, :LATENT]
            rope = piece[:, LATENT:]
            keys[at : at + rows, LATENT:] = jnp.concatenate([rope, rope], axis=1)

    row = lax.broadcasted_iota(jnp.int32, (2 * rows, count), 0)
    col = lax.broadcasted_iota(jnp.int32, (2 * rows, count), 1)
    partner = (row >= rows).astype(jnp.int32)
    q_y = y + partner * (1 - 2 * y)
    q_pos = q_y * half + z * rows + row - partner * rows
    slot = col // step
    k_z = (z - slot) & 7
    inner = col - slot * step
    in_cache = inner < rows
    k_pos = y * half + k_z * rows + jnp.where(in_cache, inner, inner - rows)
    limit = jnp.where(in_cache, start, q_pos + 1)
    bias[...] = jnp.where(k_pos < limit, 0.0, HIDDEN).astype(f32)

    c = scale * LOG2E
    lane = lax.broadcasted_iota(jnp.int32, (2 * rows, 2 * ROPE), 1)
    low = lane < ROPE
    out_lane = lax.broadcasted_iota(jnp.int32, (2 * rows, 128), 1)
    lse_all = jnp.zeros((2 * rows, 128), f32)
    for g in range(heads // GROUP):
        for j in range(GROUP):
            h = g * GROUP + j
            at = h * NOPE
            q = jnp.concatenate([qn0[:, at : at + NOPE], qn1[:, at : at + NOPE]], axis=0)
            r0 = (h // 2) * 2 * ROPE
            r = jnp.concatenate([qr0[:, r0 : r0 + 2 * ROPE], qr1[:, r0 : r0 + 2 * ROPE]], axis=0)
            keep = low if h % 2 == 0 else jnp.logical_not(low)
            base = j * 2 * rows
            qaug[g % 2, base : base + 2 * rows, :LATENT] = nt(q, wuk[:, at : at + NOPE]).astype(bf16)
            qaug[g % 2, base : base + 2 * rows, LATENT:] = jnp.where(keep, r, jnp.zeros_like(r))
        s = nt(qaug[g % 2], keys[...])
        s = (s.reshape(GROUP, 2 * rows, count) + bias[...][None]).reshape(GROUP * 2 * rows, count)
        m = jnp.max(s, axis=-1, keepdims=True)
        p = jnp.exp2((s - m) * c)
        total = jnp.sum(p, axis=-1, keepdims=True)
        acc = nn(p.astype(bf16), keys[:, :LATENT])
        mixed = (acc / total).astype(bf16)
        lse = m * c + jnp.log2(total)
        for j in range(GROUP):
            h = g * GROUP + j
            at = h * NOPE
            base = j * 2 * rows
            o = nn(mixed[base : base + 2 * rows], wuv[:, at : at + NOPE])
            own[:, at : at + NOPE] = o[:rows]
            message[:, at : at + NOPE] = o[rows:].astype(bf16)
            lse_all = jnp.where(out_lane == h, lse[base : base + 2 * rows], lse_all)
    own_lse[...] = lse_all[:rows]
    rest = lse_all[rows:]
    hi = rest.astype(bf16)
    rest = rest - hi.astype(f32)
    mid = rest.astype(bf16)
    low_part = (rest - mid.astype(f32)).astype(bf16)
    wide = heads * NOPE
    message[:, wide : wide + 128] = hi
    message[:, wide + 128 : wide + 256] = mid
    message[:, wide + 256 : wide + 384] = low_part


def attention_part(info, q0, q1, wuk, wuv, pieces, half):
    rows = pieces[0].shape[0] // 2
    heads = wuk.shape[1] // NOPE
    wide = heads * NOPE
    vmem = pl.BlockSpec(memory_space=pltpu.VMEM)
    smem = pl.BlockSpec(memory_space=pltpu.SMEM)
    scale = (NOPE + ROPE) ** -0.5
    return pl.pallas_call(
        functools.partial(attention_kernel, rows, heads, half, scale),
        out_shape=(
            jax.ShapeDtypeStruct((rows, wide), f32),
            jax.ShapeDtypeStruct((rows, 128), f32),
            jax.ShapeDtypeStruct((rows, wide + 384), bf16),
        ),
        in_specs=[smem] + [vmem] * 15,
        out_specs=(vmem, vmem, vmem),
        scratch_shapes=[
            pltpu.VMEM((16 * rows, LATENT + 2 * ROPE), bf16),
            pltpu.VMEM((2 * rows, 16 * rows), f32),
            pltpu.VMEM((2, GROUP * 2 * rows, LATENT + 2 * ROPE), bf16),
        ],
        compiler_params=pltpu.CompilerParams(vmem_limit_bytes=VMEM_LIMIT),
    )(info, q0[0], q0[1], q1[0], q1[1], wuk, wuv, *pieces)


def combine_kernel(rows, heads, info, own_a, lse_a, got_a, own_b, lse_b, got_b, out):
    live = info[3]
    base = info[4]
    wide = heads * NOPE
    alive = base + lax.broadcasted_iota(jnp.int32, (rows, 1), 0) < live
    for part, (own, lse, got) in enumerate(((own_a, lse_a, got_a), (own_b, lse_b, got_b))):
        there = (
            got[:, wide : wide + 128].astype(f32)
            + got[:, wide + 128 : wide + 256].astype(f32)
            + got[:, wide + 256 : wide + 384].astype(f32)
        )
        share = 1.0 / (1.0 + jnp.exp2(there - lse[...]))
        for h in range(heads):
            at = h * NOPE
            w = share[:, h : h + 1]
            o = own[:, at : at + NOPE] * w + got[:, at : at + NOPE].astype(f32) * (1.0 - w)
            out[:, part * wide + at : part * wide + at + NOPE] = jnp.where(alive, o, 0.0).astype(bf16)


def combine(info, a, got_a, b, got_b):
    rows, wide = a[0].shape
    vmem = pl.BlockSpec(memory_space=pltpu.VMEM)
    smem = pl.BlockSpec(memory_space=pltpu.SMEM)
    return pl.pallas_call(
        functools.partial(combine_kernel, rows, wide // NOPE),
        out_shape=jax.ShapeDtypeStruct((rows, 2 * wide), bf16),
        in_specs=[smem] + [vmem] * 6,
        out_specs=vmem,
        compiler_params=pltpu.CompilerParams(vmem_limit_bytes=VMEM_LIMIT),
    )(info, a[0], a[1], got_a, b[0], b[1], got_b)


def project_kernel(rows, info, *refs):
    pieces = refs[:9]
    w00, w01, w10, w11, out, held = refs[9:]
    z = info[2]
    depth = w00.shape[0]
    for d in range(8):
        if d == 4:
            held[d * rows : d * rows + rows // 2, :] = pieces[7][...]
            held[d * rows + rows // 2 : (d + 1) * rows, :] = pieces[8][...]
        else:
            held[d * rows : (d + 1) * rows, :] = pieces[d if d < 4 else d - 1][...]
    left = held[:, :depth]
    right = held[:, depth:]
    first = nn(left, w00[...]) + nn(right, w10[...])
    second = nn(left, w01[...]) + nn(right, w11[...])
    both = jnp.concatenate([first, second], axis=1).astype(bf16)
    for d in range(8):
        out[(z - d) & 7] = both[d * rows : (d + 1) * rows]


def project(info, pieces, w00, w01, w10, w11):
    rows, wide = pieces[0].shape
    vmem = pl.BlockSpec(memory_space=pltpu.VMEM)
    smem = pl.BlockSpec(memory_space=pltpu.SMEM)
    return pl.pallas_call(
        functools.partial(project_kernel, rows),
        out_shape=jax.ShapeDtypeStruct((8, rows, 2 * w00.shape[1]), bf16),
        in_specs=[smem] + [vmem] * 13,
        out_specs=vmem,
        scratch_shapes=[pltpu.VMEM((8 * rows, wide), bf16)],
        compiler_params=pltpu.CompilerParams(vmem_limit_bytes=VMEM_LIMIT),
    )(info, *pieces, w00, w01, w10, w11)


def swap(x, axis):
    return lax.ppermute(x, axis, [(0, 1), (1, 0)])


def ring(x):
    up = [(i, (i + 1) % 8) for i in range(8)]
    down = [(i, (i - 1) % 8) for i in range(8)]
    a = b = x
    ups, downs = [], []
    for _ in range(3):
        a = lax.ppermute(a, "z", up)
        b = lax.ppermute(b, "z", down)
        ups.append(a)
        downs.append(b)
    cut = x.shape[0] // 2
    first = lax.ppermute(a[:cut], "z", up)
    second = lax.ppermute(b[cut:], "z", down)
    return [x] + ups + downs[::-1] + [first, second]


def local(q_nope, q_rope, cache_latent, stretch_latent, w_uk, w_uv, w_o, stretch_start, prompt_len):
    rows = q_nope.shape[1]
    core = lax.axis_index("core")
    y = lax.axis_index("yl")
    yh = lax.axis_index("yh")
    z = lax.axis_index("z")
    half = 8 * rows
    wide_q = q_nope.shape[2]

    def mine(x):
        return lax.dynamic_index_in_dim(x, core, 0, keepdims=False)

    def other(x):
        return lax.dynamic_index_in_dim(x, 1 - core, 0, keepdims=False)

    info = jnp.stack(
        [mine(stretch_start), y, z, mine(prompt_len) - mine(stretch_start), y * half + z * rows]
    ).astype(jnp.int32)

    pieces = ring(jnp.concatenate([mine(cache_latent), mine(stretch_latent)], axis=0))

    q_own = jnp.concatenate([mine(q_nope), mine(q_rope)], axis=1)
    q_sent = jnp.concatenate([other(q_nope), other(q_rope)], axis=1)
    q_here = jnp.stack([q_own, swap(q_sent, "core")])
    q_there = swap(q_here, "yl")
    w_uk2 = swap(w_uk, "core")
    w_uv2 = swap(w_uv, "core")
    w_o_y = swap(w_o, "yl")
    w_o_c = swap(w_o, "core")
    w_o_cy = swap(w_o_y, "core")

    def split(x):
        return (x[:, :wide_q], x[:, wide_q:])

    a = attention_part(info, split(q_here[0]), split(q_there[0]), w_uk, w_uv, pieces, half)
    got_a = swap(a[2], "yl")
    b = attention_part(info, split(q_here[1]), split(q_there[1]), w_uk2, w_uv2, pieces, half)
    got_b = swap(b[2], "yl")
    attention = combine(info, a, got_a, b, got_b)

    partial = project(info, ring(attention), w_o, w_o_y, w_o_c, w_o_cy)
    parts = lax.all_to_all(partial, ("x", "core"), 0, 0, tiled=True)
    cols = w_o.shape[1]
    summed = jnp.sum(parts.reshape(4, 2, rows, 2 * cols).astype(f32), axis=0).astype(bf16)
    by_col = (summed[:, :, :cols], summed[:, :, cols:])
    same = yh == y
    keep = jnp.where(same, by_col[0], by_col[1])
    move = jnp.where(same, by_col[1], by_col[0])
    got = lax.ppermute(keep, ("yl", "yh"), [(0, 0), (1, 2), (2, 1), (3, 3)])
    got2 = lax.ppermute(move, ("yl", "yh"), [(0, 2), (2, 3), (1, 0), (3, 1)])
    return (got.astype(f32) + got2.astype(f32)).astype(bf16)


def solution(mesh):
    fine = Mesh(mesh.devices.reshape(2, 8, 2, 4, 2), ("yl", "z", "yh", "x", "core"))
    ctx = ("yl", "z")
    head = ("yh", "x", "core")
    placed = (
        P(None, ctx, head),
        P(None, ctx, head),
        P(None, ctx, None),
        P(None, ctx, None),
        P(None, head),
        P(None, head),
        P(head, ctx),
        P(),
        P(),
    )
    return jax.shard_map(
        local, mesh=fine, in_specs=placed, out_specs=P(None, head, ctx), check_vma=False
    )
```

time: 350 us -> 142 us (0.41)
  waiting for transfers between devices: 290 us -> 49.1 us
  starting transfers between devices: 0.12 us -> 40.4 us
  matrix products: 39 us -> 0 us
  local copies, waits for them, and re-layouts: 1.93 us -> 25.8 us
  Pallas kernels: 0 us -> 22.7 us
  between operations: 13.3 us -> 1.57 us
    all_gather x3 -> x0, waiting for transfers between devices: 212 us -> none  [the longest x1 74.8 us: local(): lax.all_gather(attention, 'ctx', axis=1, tiled=True)]
    reduce_scatter x1 -> x0, waiting for transfers between devices: 76.4 us -> none  [local(): lax.psum_scatter(partial_value.astype(jnp.bfloat16), 'head', scatter_dime...]
    dot_general x11 -> x0, matrix products: 39 us -> none  [the longest x2 10.1 us: values_fn(): jnp.einsum('sgqr,srgd->sgqd', widened, value_block, precision=highest)]
    ppermute x0 -> x27, starting transfers between devices: none -> 36.1 us  [the longest x6 17 us: ring(): b = lax.ppermute(b, 'z', down)]
    ppermute x0 -> x27, waiting for transfers between devices: none -> 34.5 us  [the longest x6 17.5 us: ring(): a = lax.ppermute(a, 'z', up)]
    pallas_call x0 -> x4, Pallas kernels: none -> 22.7 us  [the longest x2 14.2 us: attention_part(): pl.pallas_call(functools.partial(attention_kernel, rows, heads, half, sca...]
    all_to_all x0 -> x1, waiting for transfers between devices: none -> 14.6 us  [local(): parts = lax.all_to_all(partial, ('x', 'core'), 0, 0, tiled=True)]
    unnamed x16 -> x51, local copies, waits for them, and re-layouts: 0.82 us -> 8.23 us
  transfers between devices with their start and end apart: 4 -> 28, of which waited for: 4 -> 13; matrix products, arithmetic and copies ran while one was open for 3% -> 14% of each run, Pallas kernels for 0% -> 12%
where the time goes in v1:
time: 142 us; the launch traced here: 141 us
  waiting for transfers between devices  49.1 us (35%)
  starting transfers between devices  40.4 us (28%)
  local copies, waits for them, and re-layouts  25.8 us (18%)
  Pallas kernels  22.7 us (16%)
  other arithmetic  1.81 us (1%)
  between operations  1.57 us (1%)
    ppermute x6, waiting for transfers between devices, ring(): a = lax.ppermute(a, 'z', up)  17.5 us
    ppermute x6, starting transfers between devices, ring(): b = lax.ppermute(b, 'z', down)  17 us
    all_to_all x1, waiting for transfers between devices, local(): parts = lax.all_to_all(partial, ('x', 'core'), 0, 0, tiled=True)  14.6 us
    pallas_call x2, Pallas kernels, attention_part(): pl.pallas_call(functools.partial(attention_kernel, rows, heads, half, sca...  14.2 us
    ppermute x6, waiting for transfers between devices, ring(): b = lax.ppermute(b, 'z', down)  8.31 us
    unnamed x51, local copies, waits for them, and re-layouts  8.23 us
    pallas_call x1, Pallas kernels, project(): pl.pallas_call(functools.partial(project_kernel, rows), out_shape=jax.Sha...  6.17 us
    slice x6, local copies, waits for them, and re-layouts, split(): return (x[:, :wide_q], x[:, wide_q:])  5.62 us
  transfers between devices with their start and end apart: 28, of which 13 were waited for; matrix products, arithmetic and copies ran while one was open for 14% of the time, Pallas kernels for 12%

profile of v1, /device:TPU:8, one launch (start us, length us, event | category | flops | bytes accessed | tf_op | source)
XLA Modules:
  0.0 141.3 jit_solution(10030589927970938537)
XLA Ops:
  0.0 1.0 dynamic-slice_bitcast_fusion.2
  1.1 2.0 %collective-permute-start.2 = (bf16[128,576]{1,0:T(8,128)(2,1)S(1)}, bf16[128,576]{1,0:T(8,128)(2,1)S(1)}, u32[]{:S(2)}, u32[]{:S(2)}) collective-permute-start(bf16[128,576]{1,0:T(8,128)(2,1)S(1)} %pad_maximum_fusion.2.refs_7_), channel_id=1, source_target_pairs={{0,16},{16,32},{32,48},{48,64},{64,80},{80,96},{96,112},{112,0},{1... | collective-permute-start | bytes 442376 | tf_op jit(solution)/shard_map/ppermute | solution.py:207
  3.1 4.0 %collective-permute-start.5 = (bf16[128,576]{1,0:T(8,128)(2,1)S(1)}, bf16[128,576]{1,0:T(8,128)(2,1)}, u32[]{:S(2)}, u32[]{:S(2)}) collective-permute-start(bf16[128,576]{1,0:T(8,128)(2,1)S(1)} %pad_maximum_fusion.2.refs_7_), channel_id=1, source_target_pairs={{0,112},{16,0},{32,16},{48,32},{64,48},{80,64},{96,80},{112,96},{1... | collective-permute-start | bytes 442376 | tf_op jit(solution)/shard_map/ppermute | solution.py:208
  7.1 1.0 dynamic-slice_bitcast_fusion
  8.3 0.5 collective-permute-start.11
  8.9 2.3 %collective-permute-done.2.refs_8_ = bf16[128,576]{1,0:T(8,128)(2,1)S(1)} collective-permute-done((bf16[128,576]{1,0:T(8,128)(2,1)S(1)}, bf16[128,576]{1,0:T(8,128)(2,1)S(1)}, u32[]{:S(2)}, u32[]{:S(2)}) %collective-permute-start.2) | collective-permute-done | bytes 147488 | tf_op jit(solution)/shard_map/ppermute | solution.py:207
  11.2 3.2 %collective-permute-start.6 = (bf16[128,576]{1,0:T(8,128)(2,1)}, bf16[128,576]{1,0:T(8,128)(2,1)}, u32[]{:S(2)}, u32[]{:S(2)}) collective-permute-start(bf16[128,576]{1,0:T(8,128)(2,1)} %collective-permute-done.5.refs_13_), channel_id=1, source_target_pairs={{0,112},{16,0},{32,16},{48,32},{64,48},{80,64},{96,80},{112,96},{1... | collective-permute-start | bytes 442376 | tf_op jit(solution)/shard_map/ppermute | solution.py:208
  14.5 0.8 pad_maximum_fusion
  15.3 0.5 collective-permute-start.1
  15.7 2.1 %collective-permute-done.3.refs_9_ = bf16[128,576]{1,0:T(8,128)(2,1)S(1)} collective-permute-done((bf16[128,576]{1,0:T(8,128)(2,1)S(1)}, bf16[128,576]{1,0:T(8,128)(2,1)S(1)}, u32[]{:S(2)}, u32[]{:S(2)}) %collective-permute-start.3) | collective-permute-done | bytes 147488 | tf_op jit(solution)/shard_map/ppermute | solution.py:207
  17.8 0.5 collective-permute-start.22
  18.4 6.0 %collective-permute-done.4.refs_10_ = bf16[128,576]{1,0:T(8,128)(2,1)S(1)} collective-permute-done((bf16[128,576]{1,0:T(8,128)(2,1)S(1)}, bf16[128,576]{1,0:T(8,128)(2,1)S(1)}, u32[]{:S(2)}, u32[]{:S(2)}) %collective-permute-start.4) | collective-permute-done | bytes 147488 | tf_op jit(solution)/shard_map/ppermute | solution.py:207
  24.4 0.7 copy-done.23
  25.0 0.6 dynamic_slice.29
  25.7 0.7 copy-done.24
  26.3 0.7 dynamic_slice.30
  28.3 1.3 stack.26.refs_0_.info
  29.6 1.6 %slice.61.refs_1_ = bf16[64,1024]{1,0:T(8,128)(2,1)} slice(bf16[64,1536]{1,0:T(8,128)(2,1)} %copy-done.7), slice={[0:64], [0:1024]} | slice | bytes 262144 | tf_op jit(solution)/shard_map/slice | solution.py:249
  31.2 1.5 %slice.62.refs_2_ = bf16[64,512]{1,0:T(8,128)(2,1)} slice(bf16[64,1536]{1,0:T(8,128)(2,1)} %copy-done.7), slice={[0:64], [1024:1536]} | slice | bytes 131072 | tf_op jit(solution)/shard_map/slice | solution.py:249
  32.7 2.1 %collective-permute-start.8 = (bf16[64,576]{1,0:T(8,128)(2,1)S(1)}, bf16[64,576]{1,0:T(8,128)(2,1)S(1)}, u32[]{:S(2)}, u32[]{:S(2)}) collective-permute-start(bf16[64,576]{1,0:T(8,128)(2,1)S(1)} %slice.59), channel_id=1, source_target_pairs={{0,16},{16,32},{32,48},{48,64},{64,80},{80,96},{96,112},{112,0},{1... | collective-permute-start | bytes 221192 | tf_op jit(solution)/shard_map/ppermute | solution.py:212
  34.7 1.5 %collective-permute-start.9 = (bf16[64,576]{1,0:T(8,128)(2,1)S(1)}, bf16[64,576]{1,0:T(8,128)(2,1)S(1)}, u32[]{:S(2)}, u32[]{:S(2)}) collective-permute-start(bf16[64,576]{1,0:T(8,128)(2,1)S(1)} %slice.60), channel_id=1, source_target_pairs={{0,112},{16,0},{32,16},{48,32},{64,48},{80,64},{96,80},{112,96},{1... | collective-permute-start | bytes 221192 | tf_op jit(solution)/shard_map/ppermute | solution.py:213
  36.3 1.0 slice_bitcast_fusion
  37.3 0.7 slice.57.refs_3_
  38.0 0.6 slice.58.refs_4_
  38.6 0.7 slice.64.refs_3_
  39.3 0.6 slice.65.refs_4_
  39.9 0.6 copy-done.13
  40.5 0.6 copy-done.14
  41.2 7.1 %shard_map.91 = (f32[64,1024]{1,0:T(8,128)}, f32[64,128]{1,0:T(8,128)}, bf16[64,1408]{1,0:T(8,128)(2,1)}) custom-call(s32[5]{0:T(128)} %stack.26.refs_0_.info, bf16[64,1024]{1,0:T(8,128)(2,1)} %copy-done.1, bf16[64,512]{1,0:T(8,128)(2,1)} %copy-done.12, bf16[64,1024]{1,0:T(8,128)(2,1)} %slice.57.refs_3_, bf16[64,512]{1,0:T(8,128)(2,1)} %slice.58.refs_4_, ...), custom_call_target="tpu_custom_call" | custom-call | tf_op jit(solution)/shard_map/pallas_call | solution.py:113
  48.3 0.4 collective-permute-start.10
  48.7 1.0 copy-done.3
  49.8 1.0 copy-done.4
  50.7 7.1 %shard_map.92 = (f32[64,1024]{1,0:T(8,128)}, f32[64,128]{1,0:T(8,128)}, bf16[64,1408]{1,0:T(8,128)(2,1)}) custom-call(s32[5]{0:T(128)} %stack.26.refs_0_.info, bf16[64,1024]{1,0:T(8,128)(2,1)} %slice.61.refs_1_, bf16[64,512]{1,0:T(8,128)(2,1)} %slice.62.refs_2_, bf16[64,1024]{1,0:T(8,128)(2,1)} %slice.64.refs_3_, bf16[64,512]{1,0:T(8,128)(2,1)} %slice.65.refs_4_, ...), custom_call_target="tpu_custom_call" | custom-call | tf_op jit(solution)/shard_map/pallas_call | solution.py:113
  57.8 1.6 %collective-permute-start.13 = (bf16[64,1408]{1,0:T(8,128)(2,1)}, bf16[64,1408]{1,0:T(8,128)(2,1)S(1)}, u32[]{:S(2)}, u32[]{:S(2)}) collective-permute-start(bf16[64,1408]{1,0:T(8,128)(2,1)} %get-tuple-element.16), channel_id=1, source_target_pairs={{0,128},{128,0},{1,129},{129,1},{2,130},{130,2},{3,131},{131,3},{4... | collective-permute-start | bytes 540680 | tf_op jit(solution)/shard_map/ppermute | solution.py:198
  59.4 4.1 %collective-permute-done.13.got_b = bf16[64,1408]{1,0:T(8,128)(2,1)S(1)} collective-permute-done((bf16[64,1408]{1,0:T(8,128)(2,1)}, bf16[64,1408]{1,0:T(8,128)(2,1)S(1)}, u32[]{:S(2)}, u32[]{:S(2)}) %collective-permute-start.13) | collective-permute-done | bytes 180256 | tf_op jit(solution)/shard_map/ppermute | solution.py:198
  63.5 0.7 copy-done.20
  64.2 2.3 %shard_map.93.refs_0_ = bf16[64,2048]{1,0:T(8,128)(2,1)} custom-call(s32[5]{0:T(128)} %stack.26.refs_0_.info, f32[64,1024]{1,0:T(8,128)} %get-tuple-element.11.own_a, f32[64,128]{1,0:T(8,128)} %get-tuple-element.12.lse_a, bf16[64,1408]{1,0:T(8,128)(2,1)} %copy-done.19, f32[64,1024]{1,0:T(8,128)} %get-tuple-element.14.own_b, ...), custom_call_target="tpu_custom_call" | custom-call | tf_op jit(solution)/shard_map/pallas_call | solution.py:154
  66.5 0.8 collective-permute-start.14
  67.3 2.5 %collective-permute-start.17 = (bf16[64,2048]{1,0:T(8,128)(2,1)}, bf16[64,2048]{1,0:T(8,128)(2,1)S(1)}, u32[]{:S(2)}, u32[]{:S(2)}) collective-permute-start(bf16[64,2048]{1,0:T(8,128)(2,1)} %shard_map.93.refs_0_), channel_id=1, source_target_pairs={{0,112},{16,0},{32,16},{48,32},{64,48},{80,64},{96,80},{112,96},{1... | collective-permute-start | bytes 786440 | tf_op jit(solution)/shard_map/ppermute | solution.py:208
  69.7 0.2 collective-permute-start.24
  70.0 4.5 %collective-permute-done.14.refs_1_ = bf16[64,2048]{1,0:T(8,128)(2,1)S(1)} collective-permute-done((bf16[64,2048]{1,0:T(8,128)(2,1)}, bf16[64,2048]{1,0:T(8,128)(2,1)S(1)}, u32[]{:S(2)}, u32[]{:S(2)}) %collective-permute-start.14) | collective-permute-done | bytes 262176 | tf_op jit(solution)/shard_map/ppermute | solution.py:207
  74.5 1.8 %collective-permute-done.17.refs_6_ = bf16[64,2048]{1,0:T(8,128)(2,1)S(1)} collective-permute-done((bf16[64,2048]{1,0:T(8,128)(2,1)}, bf16[64,2048]{1,0:T(8,128)(2,1)S(1)}, u32[]{:S(2)}, u32[]{:S(2)}) %collective-permute-start.17) | collective-permute-done | bytes 262176 | tf_op jit(solution)/shard_map/ppermute | solution.py:208
  76.3 3.6 %collective-permute-start.18 = (bf16[64,2048]{1,0:T(8,128)(2,1)S(1)}, bf16[64,2048]{1,0:T(8,128)(2,1)S(1)}, u32[]{:S(2)}, u32[]{:S(2)}) collective-permute-start(bf16[64,2048]{1,0:T(8,128)(2,1)S(1)} %collective-permute-done.17.refs_6_), channel_id=1, source_target_pairs={{0,112},{16,0},{32,16},{48,32},{64,48},{80,64},{96,80},{112,96},{1... | collective-permute-start | bytes 786440 | tf_op jit(solution)/shard_map/ppermute | solution.py:208
  79.9 2.2 %collective-permute-done.15.refs_2_ = bf16[64,2048]{1,0:T(8,128)(2,1)S(1)} collective-permute-done((bf16[64,2048]{1,0:T(8,128)(2,1)S(1)}, bf16[64,2048]{1,0:T(8,128)(2,1)S(1)}, u32[]{:S(2)}, u32[]{:S(2)}) %collective-permute-start.15) | collective-permute-done | bytes 262176 | tf_op jit(solution)/shard_map/ppermute | solution.py:207
  82.0 3.3 %collective-permute-done.18.refs_5_ = bf16[64,2048]{1,0:T(8,128)(2,1)S(1)} collective-permute-done((bf16[64,2048]{1,0:T(8,128)(2,1)S(1)}, bf16[64,2048]{1,0:T(8,128)(2,1)S(1)}, u32[]{:S(2)}, u32[]{:S(2)}) %collective-permute-start.18) | collective-permute-done | bytes 262176 | tf_op jit(solution)/shard_map/ppermute | solution.py:208
  85.3 3.7 %collective-permute-start.19 = (bf16[64,2048]{1,0:T(8,128)(2,1)S(1)}, bf16[64,2048]{1,0:T(8,128)(2,1)S(1)}, u32[]{:S(2)}, u32[]{:S(2)}) collective-permute-start(bf16[64,2048]{1,0:T(8,128)(2,1)S(1)} %collective-permute-done.18.refs_5_), channel_id=1, source_target_pairs={{0,112},{16,0},{32,16},{48,32},{64,48},{80,64},{96,80},{112,96},{1... | collective-permute-start | bytes 786440 | tf_op jit(solution)/shard_map/ppermute | solution.py:208
  89.0 0.6 collective-permute-done.16.refs_3_
  89.6 0.7 slice.66
  90.3 3.3 %collective-permute-done.19.refs_4_ = bf16[64,2048]{1,0:T(8,128)(2,1)S(1)} collective-permute-done((bf16[64,2048]{1,0:T(8,128)(2,1)S(1)}, bf16[64,2048]{1,0:T(8,128)(2,1)S(1)}, u32[]{:S(2)}, u32[]{:S(2)}) %collective-permute-start.19) | collective-permute-done | bytes 262176 | tf_op jit(solution)/shard_map/ppermute | solution.py:208
  93.6 0.7 slice.67
  94.3 3.7 %collective-permute-start.21 = (bf16[32,2048]{1,0:T(8,128)(2,1)}, bf16[32,2048]{1,0:T(8,128)(2,1)}, u32[]{:S(2)}, u32[]{:S(2)}) collective-permute-start(bf16[32,2048]{1,0:T(8,128)(2,1)} %slice.67), channel_id=1, source_target_pairs={{0,112},{16,0},{32,16},{48,32},{64,48},{80,64},{96,80},{112,96},{1... | collective-permute-start | bytes 393224 | tf_op jit(solution)/shard_map/ppermute | solution.py:213
  98.0 2.3 %copy.13.refs_9_ = bf16[1024,448]{1,0:T(8,128)(2,1)} copy(bf16[1024,448]{0,1:T(8,128)(2,1)} %param.15) | data formatting | bytes 1835008 | tf_op args[6]
  100.3 2.3 %copy.14.refs_10_ = bf16[1024,448]{1,0:T(8,128)(2,1)} copy(bf16[1024,448]{0,1:T(8,128)(2,1)} %collective-permute-done.22) | data formatting | bytes 1835008 | tf_op jit(solution)/shard_map/ppermute | solution.py:198
  102.5 1.3 copy.15.refs_11_
  103.8 1.3 copy.16.refs_12_
  105.2 0.6 copy-done.21
  105.8 6.2 %shard_map.94 = bf16[8,64,896]{2,1,0:T(8,128)(2,1)} custom-call(s32[5]{0:T(128)} %stack.26.refs_0_.info, bf16[64,2048]{1,0:T(8,128)(2,1)} %shard_map.93.refs_0_, bf16[64,2048]{1,0:T(8,128)(2,1)} %copy-done.15, bf16[64,2048]{1,0:T(8,128)(2,1)} %copy-done.17, bf16[64,2048]{1,0:T(8,128)(2,1)} %copy-done.10, bf16[64,2048]{1,0:T(8,128)(2,1)} %copy-done.11, ...), custom_call_target="tpu_custom_call" | custom-call | tf_op jit(solution)/shard_map/pallas_call | solution.py:187
  112.0 4.3 %all-to-all-start = ((bf16[8,64,896]{2,1,0:T(8,128)(2,1)}), bf16[8,64,896]{2,1,0:T(8,128)(2,1)S(1)}, u32[]{:S(2)}, u32[]{:S(2)}) async-start(bf16[8,64,896]{2,1,0:T(8,128)(2,1)} %shard_map.94), calls=%async_computation | async-start | bytes 1835008 | tf_op jit(solution)/shard_map/all_to_all | solution.py:258
  116.3 14.6 %all-to-all-done = bf16[8,64,896]{2,1,0:T(8,128)(2,1)S(1)} async-done(((bf16[8,64,896]{2,1,0:T(8,128)(2,1)}), bf16[8,64,896]{2,1,0:T(8,128)(2,1)S(1)}, u32[]{:S(2)}, u32[]{:S(2)}) %all-to-all-start) | async-done | bytes 917536 | tf_op jit(solution)/shard_map/all_to_all | solution.py:258
  131.1 2.7 %collective-permute-start.26 = (bf16[2,64,448]{2,1,0:T(8,128)(2,1)S(1)}, bf16[2,64,448]{2,1,0:T(8,128)(2,1)S(1)}, u32[]{:S(2)}, u32[]{:S(2)}) collective-permute-start(bf16[2,64,448]{2,1,0:T(8,128)(2,1)S(1)} %get-tuple-element.22), channel_id=1, source_target_pairs={{0,128},{128,136},{8,0},{136,8},{1,129},{129,137},{9,1},{137,9},{2... | collective-permute-start | bytes 344072 | tf_op jit(solution)/shard_map/ppermute | solution.py:266
  133.8 2.3 %collective-permute-start.25 = (bf16[2,64,448]{2,1,0:T(8,128)(2,1)S(1)}, bf16[2,64,448]{2,1,0:T(8,128)(2,1)S(1)}, u32[]{:S(2)}, u32[]{:S(2)}) collective-permute-start(bf16[2,64,448]{2,1,0:T(8,128)(2,1)S(1)} %get-tuple-element.21), channel_id=1, source_target_pairs={{0,0},{8,128},{128,8},{136,136},{1,1},{9,129},{129,9},{137,137},{2... | collective-permute-start | bytes 344072 | tf_op jit(solution)/shard_map/ppermute | solution.py:265
  136.1 0.2 collective-permute-done.26
  136.3 4.3 %collective-permute-done.25 = bf16[2,64,448]{2,1,0:T(8,128)(2,1)S(1)} collective-permute-done((bf16[2,64,448]{2,1,0:T(8,128)(2,1)S(1)}, bf16[2,64,448]{2,1,0:T(8,128)(2,1)S(1)}, u32[]{:S(2)}, u32[]{:S(2)}) %collective-permute-start.25) | collective-permute-done | bytes 114720 | tf_op jit(solution)/shard_map/ppermute | solution.py:265
  140.6 0.7 add_convert_fusion
  (74 shorter events, 0.7 us)
Async XLA Ops:
  0.0 8.3 %copy-start.2 = (bf16[512,1024]{1,0:T(8,128)(2,1)S(1)}, bf16[512,1024]{1,0:T(8,128)(2,1)}, u32[]{:S(2)}) copy-start(bf16[512,1024]{1,0:T(8,128)(2,1)} %refs_5_.1) | copy-start | bytes 3145732
  1.1 7.1 %copy-start = (bf16[128,576]{1,0:T(8,128)(2,1)}, bf16[128,576]{1,0:T(8,128)(2,1)S(1)}, u32[]{:S(2)}) copy-start(bf16[128,576]{1,0:T(8,128)(2,1)S(1)} %pad_maximum_fusion.2.refs_7_) | copy-start | bytes 442372
  1.1 10.1 %collective-permute-start.2 = (bf16[128,576]{1,0:T(8,128)(2,1)S(1)}, bf16[128,576]{1,0:T(8,128)(2,1)S(1)}, u32[]{:S(2)}, u32[]{:S(2)}) collective-permute-start(bf16[128,576]{1,0:T(8,128)(2,1)S(1)} %pad_maximum_fusion.2.refs_7_), channel_id=1, source_target_pairs={{0,16},{16,32},{32,48},{48,64},{64,80},{80,96},{96,112},{112,0},{1... | collective-permute-start | bytes 442376 | tf_op jit(solution)/shard_map/ppermute | solution.py:207
  3.1 8.1 %collective-permute-start.5 = (bf16[128,576]{1,0:T(8,128)(2,1)S(1)}, bf16[128,576]{1,0:T(8,128)(2,1)}, u32[]{:S(2)}, u32[]{:S(2)}) collective-permute-start(bf16[128,576]{1,0:T(8,128)(2,1)S(1)} %pad_maximum_fusion.2.refs_7_), channel_id=1, source_target_pairs={{0,112},{16,0},{32,16},{48,32},{64,48},{80,64},{96,80},{112,96},{1... | collective-permute-start | bytes 442376 | tf_op jit(solution)/shard_map/ppermute | solution.py:208
  7.1 1.0 copy-start.22
  8.1 0.8 copy-start.1
  8.2 0.7 copy-start.12
  8.2 6.2 %collective-permute-start = (bf16[64,1536]{1,0:T(8,128)(2,1)S(1)}, bf16[64,1536]{1,0:T(8,128)(2,1)S(1)}, u32[]{:S(2)}, u32[]{:S(2)}) collective-permute-start(bf16[64,1536]{1,0:T(8,128)(2,1)S(1)} %pad_maximum_fusion.1), channel_id=1, source_target_pairs={{0,1},{1,0},{2,3},{3,2},{4,5},{5,4},{6,7},{7,6},{8,9},{9,8},{10,11... | collective-permute-start | bytes 589832 | tf_op jit(solution)/shard_map/ppermute | solution.py:198
  8.3 40.4 %collective-permute-start.11 = (bf16[512,1024]{1,0:T(8,128)(2,1)S(1)}, bf16[512,1024]{1,0:T(8,128)(2,1)S(1)}, u32[]{:S(2)}, u32[]{:S(2)}) collective-permute-start(bf16[512,1024]{1,0:T(8,128)(2,1)S(1)} %copy-done.2), channel_id=1, source_target_pairs={{0,1},{1,0},{2,3},{3,2},{4,5},{5,4},{6,7},{7,6},{8,9},{9,8},{10,11... | collective-permute-start | bytes 3145736 | tf_op jit(solution)/shard_map/ppermute | solution.py:198
  8.8 39.9 %collective-permute-start.12 = (bf16[512,1024]{1,0:T(8,128)(2,1)}, bf16[512,1024]{1,0:T(8,128)(2,1)S(1)}, u32[]{:S(2)}, u32[]{:S(2)}) collective-permute-start(bf16[512,1024]{1,0:T(8,128)(2,1)} %refs_6_.1), channel_id=1, source_target_pairs={{0,1},{1,0},{2,3},{3,2},{4,5},{5,4},{6,7},{7,6},{8,9},{9,8},{10,11... | collective-permute-start | bytes 3145736 | tf_op jit(solution)/shard_map/ppermute | solution.py:198
  11.2 4.1 %copy-start.8 = (bf16[128,576]{1,0:T(8,128)(2,1)}, bf16[128,576]{1,0:T(8,128)(2,1)S(1)}, u32[]{:S(2)}) copy-start(bf16[128,576]{1,0:T(8,128)(2,1)S(1)} %collective-permute-done.2.refs_8_) | copy-start | bytes 442372
  11.2 6.6 %collective-permute-start.3 = (bf16[128,576]{1,0:T(8,128)(2,1)S(1)}, bf16[128,576]{1,0:T(8,128)(2,1)S(1)}, u32[]{:S(2)}, u32[]{:S(2)}) collective-permute-start(bf16[128,576]{1,0:T(8,128)(2,1)S(1)} %collective-permute-done.2.refs_8_), channel_id=1, source_target_pairs={{0,16},{16,32},{32,48},{48,64},{64,80},{80,96},{96,112},{112,0},{1... | collective-permute-start | bytes 442376 | tf_op jit(solution)/shard_map/ppermute | solution.py:207
  11.2 6.6 %collective-permute-start.6 = (bf16[128,576]{1,0:T(8,128)(2,1)}, bf16[128,576]{1,0:T(8,128)(2,1)}, u32[]{:S(2)}, u32[]{:S(2)}) collective-permute-start(bf16[128,576]{1,0:T(8,128)(2,1)} %collective-permute-done.5.refs_13_), channel_id=1, source_target_pairs={{0,112},{16,0},{32,16},{48,32},{64,48},{80,64},{96,80},{112,96},{1... | collective-permute-start | bytes 442376 | tf_op jit(solution)/shard_map/ppermute | solution.py:208
  14.5 0.8 copy-start.7
  15.3 19.5 %collective-permute-start.1 = (bf16[2,64,1536]{2,1,0:T(8,128)(2,1)}, bf16[2,64,1536]{2,1,0:T(8,128)(2,1)}, u32[]{:S(2)}, u32[]{:S(2)}) collective-permute-start(bf16[2,64,1536]{2,1,0:T(8,128)(2,1)} %pad_maximum_fusion), channel_id=1, source_target_pairs={{0,128},{128,0},{1,129},{129,1},{2,130},{130,2},{3,131},{131,3},{4... | collective-permute-start | bytes 1179656 | tf_op jit(solution)/shard_map/ppermute | solution.py:198
  17.8 6.5 %copy-start.9 = (bf16[128,576]{1,0:T(8,128)(2,1)}, bf16[128,576]{1,0:T(8,128)(2,1)S(1)}, u32[]{:S(2)}) copy-start(bf16[128,576]{1,0:T(8,128)(2,1)S(1)} %collective-permute-done.3.refs_9_) | copy-start | bytes 442372
  17.8 6.5 %collective-permute-start.4 = (bf16[128,576]{1,0:T(8,128)(2,1)S(1)}, bf16[128,576]{1,0:T(8,128)(2,1)S(1)}, u32[]{:S(2)}, u32[]{:S(2)}) collective-permute-start(bf16[128,576]{1,0:T(8,128)(2,1)S(1)} %collective-permute-done.3.refs_9_), channel_id=1, source_target_pairs={{0,16},{16,32},{32,48},{48,64},{64,80},{80,96},{96,112},{112,0},{1... | collective-permute-start | bytes 442376 | tf_op jit(solution)/shard_map/ppermute | solution.py:207
  17.8 51.9 %collective-permute-start.22 = (bf16[1024,448]{0,1:T(8,128)(2,1)}, bf16[1024,448]{0,1:T(8,128)(2,1)}, u32[]{:S(2)}, u32[]{:S(2)}) collective-permute-start(bf16[1024,448]{0,1:T(8,128)(2,1)} %param.15), channel_id=1, source_target_pairs={{0,128},{128,0},{1,129},{129,1},{2,130},{130,2},{3,131},{131,3},{4... | collective-permute-start | bytes 2752520 | tf_op jit(solution)/shard_map/ppermute | solution.py:198
  24.3 8.3 %copy-start.5 = (bf16[128,576]{1,0:T(8,128)(2,1)}, bf16[128,576]{1,0:T(8,128)(2,1)S(1)}, u32[]{:S(2)}) copy-start(bf16[128,576]{1,0:T(8,128)(2,1)S(1)} %collective-permute-done.4.refs_10_) | copy-start | bytes 442372
  24.3 8.3 %collective-permute-start.7 = (bf16[128,576]{1,0:T(8,128)(2,1)}, bf16[128,576]{1,0:T(8,128)(2,1)S(1)}, u32[]{:S(2)}, u32[]{:S(2)}) collective-permute-start(bf16[128,576]{1,0:T(8,128)(2,1)} %collective-permute-done.6.refs_12_), channel_id=1, source_target_pairs={{0,112},{16,0},{32,16},{48,32},{64,48},{80,64},{96,80},{112,96},{1... | collective-permute-start | bytes 442376 | tf_op jit(solution)/shard_map/ppermute | solution.py:208
  24.4 0.7 copy-start.23
  25.7 0.7 copy-start.24
  32.7 4.7 %copy-start.6 = (bf16[128,576]{1,0:T(8,128)(2,1)}, bf16[128,576]{1,0:T(8,128)(2,1)S(1)}, u32[]{:S(2)}) copy-start(bf16[128,576]{1,0:T(8,128)(2,1)S(1)} %collective-permute-done.7.refs_11_) | copy-start | bytes 442372
  32.7 7.2 %collective-permute-start.8 = (bf16[64,576]{1,0:T(8,128)(2,1)S(1)}, bf16[64,576]{1,0:T(8,128)(2,1)S(1)}, u32[]{:S(2)}, u32[]{:S(2)}) collective-permute-start(bf16[64,576]{1,0:T(8,128)(2,1)S(1)} %slice.59), channel_id=1, source_target_pairs={{0,16},{16,32},{32,48},{48,64},{64,80},{80,96},{96,112},{112,0},{1... | collective-permute-start | bytes 221192 | tf_op jit(solution)/shard_map/ppermute | solution.py:212
  34.7 5.2 %collective-permute-start.9 = (bf16[64,576]{1,0:T(8,128)(2,1)S(1)}, bf16[64,576]{1,0:T(8,128)(2,1)S(1)}, u32[]{:S(2)}, u32[]{:S(2)}) collective-permute-start(bf16[64,576]{1,0:T(8,128)(2,1)S(1)} %slice.60), channel_id=1, source_target_pairs={{0,112},{16,0},{32,16},{48,32},{64,48},{80,64},{96,80},{112,96},{1... | collective-permute-start | bytes 221192 | tf_op jit(solution)/shard_map/ppermute | solution.py:213
  39.9 0.6 copy-start.13
  40.5 0.6 copy-start.14
  48.3 11.1 %collective-permute-start.10 = (bf16[64,1408]{1,0:T(8,128)(2,1)}, bf16[64,1408]{1,0:T(8,128)(2,1)S(1)}, u32[]{:S(2)}, u32[]{:S(2)}) collective-permute-start(bf16[64,1408]{1,0:T(8,128)(2,1)} %get-tuple-element.13), channel_id=1, source_target_pairs={{0,128},{128,0},{1,129},{129,1},{2,130},{130,2},{3,131},{131,3},{4... | collective-permute-start | bytes 540680 | tf_op jit(solution)/shard_map/ppermute | solution.py:198
  48.7 1.0 copy-start.3
  49.8 1.0 copy-start.4
  57.8 5.7 %collective-permute-start.13 = (bf16[64,1408]{1,0:T(8,128)(2,1)}, bf16[64,1408]{1,0:T(8,128)(2,1)S(1)}, u32[]{:S(2)}, u32[]{:S(2)}) collective-permute-start(bf16[64,1408]{1,0:T(8,128)(2,1)} %get-tuple-element.16), channel_id=1, source_target_pairs={{0,128},{128,0},{1,129},{129,1},{2,130},{130,2},{3,131},{131,3},{4... | collective-permute-start | bytes 540680 | tf_op jit(solution)/shard_map/ppermute | solution.py:198
  59.4 4.1 %copy-start.19 = (bf16[64,1408]{1,0:T(8,128)(2,1)}, bf16[64,1408]{1,0:T(8,128)(2,1)S(1)}, u32[]{:S(2)}) copy-start(bf16[64,1408]{1,0:T(8,128)(2,1)S(1)} %collective-permute-done.10.got_a) | copy-start | bytes 540676
  63.5 0.7 copy-start.20
  66.5 8.0 %collective-permute-start.14 = (bf16[64,2048]{1,0:T(8,128)(2,1)}, bf16[64,2048]{1,0:T(8,128)(2,1)S(1)}, u32[]{:S(2)}, u32[]{:S(2)}) collective-permute-start(bf16[64,2048]{1,0:T(8,128)(2,1)} %shard_map.93.refs_0_), channel_id=1, source_target_pairs={{0,16},{16,32},{32,48},{48,64},{64,80},{80,96},{96,112},{112,0},{1... | collective-permute-start | bytes 786440 | tf_op jit(solution)/shard_map/ppermute | solution.py:207
  67.3 35.3 %collective-permute-start.23 = (bf16[1024,448]{0,1:T(8,128)(2,1)}, bf16[1024,448]{0,1:T(8,128)(2,1)S(1)}, u32[]{:S(2)}, u32[]{:S(2)}) collective-permute-start(bf16[1024,448]{0,1:T(8,128)(2,1)} %param.15), channel_id=1, source_target_pairs={{0,1},{1,0},{2,3},{3,2},{4,5},{5,4},{6,7},{7,6},{8,9},{9,8},{10,11... | collective-permute-start | bytes 2752520 | tf_op jit(solution)/shard_map/ppermute | solution.py:198
  67.3 9.0 %collective-permute-start.17 = (bf16[64,2048]{1,0:T(8,128)(2,1)}, bf16[64,2048]{1,0:T(8,128)(2,1)S(1)}, u32[]{:S(2)}, u32[]{:S(2)}) collective-permute-start(bf16[64,2048]{1,0:T(8,128)(2,1)} %shard_map.93.refs_0_), channel_id=1, source_target_pairs={{0,112},{16,0},{32,16},{48,32},{64,48},{80,64},{96,80},{112,96},{1... | collective-permute-start | bytes 786440 | tf_op jit(solution)/shard_map/ppermute | solution.py:208
  69.7 34.1 %collective-permute-start.24 = (bf16[1024,448]{0,1:T(8,128)(2,1)}, bf16[1024,448]{0,1:T(8,128)(2,1)S(1)}, u32[]{:S(2)}, u32[]{:S(2)}) collective-permute-start(bf16[1024,448]{0,1:T(8,128)(2,1)} %collective-permute-done.22), channel_id=1, source_target_pairs={{0,1},{1,0},{2,3},{3,2},{4,5},{5,4},{6,7},{7,6},{8,9},{9,8},{10,11... | collective-permute-start | bytes 2752520 | tf_op jit(solution)/shard_map/ppermute | solution.py:198
  74.4 19.8 %copy-start.15 = (bf16[64,2048]{1,0:T(8,128)(2,1)}, bf16[64,2048]{1,0:T(8,128)(2,1)S(1)}, u32[]{:S(2)}) copy-start(bf16[64,2048]{1,0:T(8,128)(2,1)S(1)} %collective-permute-done.14.refs_1_) | copy-start | bytes 786436
  74.4 7.6 %collective-permute-start.15 = (bf16[64,2048]{1,0:T(8,128)(2,1)S(1)}, bf16[64,2048]{1,0:T(8,128)(2,1)S(1)}, u32[]{:S(2)}, u32[]{:S(2)}) collective-permute-start(bf16[64,2048]{1,0:T(8,128)(2,1)S(1)} %collective-permute-done.14.refs_1_), channel_id=1, source_target_pairs={{0,16},{16,32},{32,48},{48,64},{64,80},{80,96},{96,112},{112,0},{1... | collective-permute-start | bytes 786440 | tf_op jit(solution)/shard_map/ppermute | solution.py:207
  76.3 24.0 %copy-start.16 = (bf16[64,2048]{1,0:T(8,128)(2,1)}, bf16[64,2048]{1,0:T(8,128)(2,1)S(1)}, u32[]{:S(2)}) copy-start(bf16[64,2048]{1,0:T(8,128)(2,1)S(1)} %collective-permute-done.17.refs_6_) | copy-start | bytes 786436
  76.3 9.0 %collective-permute-start.18 = (bf16[64,2048]{1,0:T(8,128)(2,1)S(1)}, bf16[64,2048]{1,0:T(8,128)(2,1)S(1)}, u32[]{:S(2)}, u32[]{:S(2)}) collective-permute-start(bf16[64,2048]{1,0:T(8,128)(2,1)S(1)} %collective-permute-done.17.refs_6_), channel_id=1, source_target_pairs={{0,112},{16,0},{32,16},{48,32},{64,48},{80,64},{96,80},{112,96},{1... | collective-permute-start | bytes 786440 | tf_op jit(solution)/shard_map/ppermute | solution.py:208
  82.0 18.2 %copy-start.17 = (bf16[64,2048]{1,0:T(8,128)(2,1)}, bf16[64,2048]{1,0:T(8,128)(2,1)S(1)}, u32[]{:S(2)}) copy-start(bf16[64,2048]{1,0:T(8,128)(2,1)S(1)} %collective-permute-done.15.refs_2_) | copy-start | bytes 786436
  82.0 7.6 %collective-permute-start.16 = (bf16[64,2048]{1,0:T(8,128)(2,1)S(1)}, bf16[64,2048]{1,0:T(8,128)(2,1)S(1)}, u32[]{:S(2)}, u32[]{:S(2)}) collective-permute-start(bf16[64,2048]{1,0:T(8,128)(2,1)S(1)} %collective-permute-done.15.refs_2_), channel_id=1, source_target_pairs={{0,16},{16,32},{32,48},{48,64},{64,80},{80,96},{96,112},{112,0},{1... | collective-permute-start | bytes 786440 | tf_op jit(solution)/shard_map/ppermute | solution.py:207
  85.3 14.9 %copy-start.18 = (bf16[64,2048]{1,0:T(8,128)(2,1)}, bf16[64,2048]{1,0:T(8,128)(2,1)S(1)}, u32[]{:S(2)}) copy-start(bf16[64,2048]{1,0:T(8,128)(2,1)S(1)} %collective-permute-done.18.refs_5_) | copy-start | bytes 786436
  85.3 8.3 %collective-permute-start.19 = (bf16[64,2048]{1,0:T(8,128)(2,1)S(1)}, bf16[64,2048]{1,0:T(8,128)(2,1)S(1)}, u32[]{:S(2)}, u32[]{:S(2)}) collective-permute-start(bf16[64,2048]{1,0:T(8,128)(2,1)S(1)} %collective-permute-done.18.refs_5_), channel_id=1, source_target_pairs={{0,112},{16,0},{32,16},{48,32},{64,48},{80,64},{96,80},{112,96},{1... | collective-permute-start | bytes 786440 | tf_op jit(solution)/shard_map/ppermute | solution.py:208
  89.6 4.7 %copy-start.10 = (bf16[64,2048]{1,0:T(8,128)(2,1)}, bf16[64,2048]{1,0:T(8,128)(2,1)S(1)}, u32[]{:S(2)}) copy-start(bf16[64,2048]{1,0:T(8,128)(2,1)S(1)} %collective-permute-done.16.refs_3_) | copy-start | bytes 786436
  90.3 14.8 %collective-permute-start.20 = (bf16[32,2048]{1,0:T(8,128)(2,1)}, bf16[32,2048]{1,0:T(8,128)(2,1)S(1)}, u32[]{:S(2)}, u32[]{:S(2)}) collective-permute-start(bf16[32,2048]{1,0:T(8,128)(2,1)} %slice.66), channel_id=1, source_target_pairs={{0,16},{16,32},{32,48},{48,64},{64,80},{80,96},{96,112},{112,0},{1... | collective-permute-start | bytes 393224 | tf_op jit(solution)/shard_map/ppermute | solution.py:212
  93.6 6.7 %copy-start.11 = (bf16[64,2048]{1,0:T(8,128)(2,1)}, bf16[64,2048]{1,0:T(8,128)(2,1)S(1)}, u32[]{:S(2)}) copy-start(bf16[64,2048]{1,0:T(8,128)(2,1)S(1)} %collective-permute-done.19.refs_4_) | copy-start | bytes 786436
  94.3 10.9 %collective-permute-start.21 = (bf16[32,2048]{1,0:T(8,128)(2,1)}, bf16[32,2048]{1,0:T(8,128)(2,1)}, u32[]{:S(2)}, u32[]{:S(2)}) collective-permute-start(bf16[32,2048]{1,0:T(8,128)(2,1)} %slice.67), channel_id=1, source_target_pairs={{0,112},{16,0},{32,16},{48,32},{64,48},{80,64},{96,80},{112,96},{1... | collective-permute-start | bytes 393224 | tf_op jit(solution)/shard_map/ppermute | solution.py:213
  105.2 0.7 copy-start.21
  112.0 18.9 %all-to-all-start = ((bf16[8,64,896]{2,1,0:T(8,128)(2,1)}), bf16[8,64,896]{2,1,0:T(8,128)(2,1)S(1)}, u32[]{:S(2)}, u32[]{:S(2)}) async-start(bf16[8,64,896]{2,1,0:T(8,128)(2,1)} %shard_map.94), calls=%async_computation | async-start | bytes 1835008 | tf_op jit(solution)/shard_map/all_to_all | solution.py:258
  131.1 5.2 %collective-permute-start.26 = (bf16[2,64,448]{2,1,0:T(8,128)(2,1)S(1)}, bf16[2,64,448]{2,1,0:T(8,128)(2,1)S(1)}, u32[]{:S(2)}, u32[]{:S(2)}) collective-permute-start(bf16[2,64,448]{2,1,0:T(8,128)(2,1)S(1)} %get-tuple-element.22), channel_id=1, source_target_pairs={{0,128},{128,136},{8,0},{136,8},{1,129},{129,137},{9,1},{137,9},{2... | collective-permute-start | bytes 344072 | tf_op jit(solution)/shard_map/ppermute | solution.py:266
  133.8 6.8 %collective-permute-start.25 = (bf16[2,64,448]{2,1,0:T(8,128)(2,1)S(1)}, bf16[2,64,448]{2,1,0:T(8,128)(2,1)S(1)}, u32[]{:S(2)}, u32[]{:S(2)}) collective-permute-start(bf16[2,64,448]{2,1,0:T(8,128)(2,1)S(1)} %get-tuple-element.21), channel_id=1, source_target_pairs={{0,0},{8,128},{128,8},{136,136},{1,1},{9,129},{129,9},{137,137},{2... | collective-permute-start | bytes 344072 | tf_op jit(solution)/shard_map/ppermute | solution.py:265

commit v2 on v1

v2 whole, which is shorter than its diff:
```python
import functools

import jax
import jax.numpy as jnp
from jax import lax
from jax.experimental import pallas as pl
from jax.experimental.pallas import tpu as pltpu
from jax.sharding import Mesh, PartitionSpec as P

LATENT = 512
ROPE = 64
NOPE = 128
LOG2E = 1.4426950408889634
HIDDEN = -1e30
GROUP = 4
MIB = 1024 * 1024

f32 = jnp.float32
bf16 = jnp.bfloat16


def nt(a, b):
    return lax.dot_general(a, b, (((1,), (1,)), ((), ())), preferred_element_type=f32)


def nn(a, b):
    return jnp.dot(a, b, preferred_element_type=f32)


def attention_kernel(rows, heads, half, scale, *refs):
    coords, starts, q0, q1, wuk, wuv = refs[:6]
    pieces = refs[6:15]
    own, own_lse, message = refs[16:19]
    keys, bias, qaug = refs[19:]
    y, z, core = coords[0], coords[1], coords[2]
    start = starts[core]
    step = 2 * rows
    count = 8 * step
    wide = heads * NOPE
    for d in range(8):
        for part in range(2):
            at = d * step + part * rows
            if d == 4:
                piece = pieces[7 + part][...]
            else:
                piece = pieces[d if d < 4 else d - 1][part * rows : (part + 1) * rows, :]
            keys[at : at + rows, :LATENT] = piece[:, :LATENT]
            rope = piece[:, LATENT:]
            keys[at : at + rows, LATENT:] = jnp.concatenate([rope, rope], axis=1)

    row = lax.broadcasted_iota(jnp.int32, (2 * rows, count), 0)
    col = lax.broadcasted_iota(jnp.int32, (2 * rows, count), 1)
    partner = (row >= rows).astype(jnp.int32)
    q_y = y + partner * (1 - 2 * y)
    q_pos = q_y * half + z * rows + row - partner * rows
    slot = col // step
    k_z = (z - slot) & 7
    inner = col - slot * step
    in_cache = inner < rows
    k_pos = y * half + k_z * rows + jnp.where(in_cache, inner, inner - rows)
    limit = jnp.where(in_cache, start, q_pos + 1)
    bias[...] = jnp.where(k_pos < limit, 0.0, HIDDEN).astype(f32)

    c = scale * LOG2E
    lane = lax.broadcasted_iota(jnp.int32, (2 * rows, 2 * ROPE), 1)
    low = lane < ROPE
    out_lane = lax.broadcasted_iota(jnp.int32, (2 * rows, 128), 1)
    lse_all = jnp.zeros((2 * rows, 128), f32)
    for g in range(heads // GROUP):
        for j in range(GROUP):
            h = g * GROUP + j
            at = h * NOPE
            q = jnp.concatenate([q0[:, at : at + NOPE], q1[:, at : at + NOPE]], axis=0)
            r0 = wide + (h // 2) * 2 * ROPE
            r = jnp.concatenate([q0[:, r0 : r0 + 2 * ROPE], q1[:, r0 : r0 + 2 * ROPE]], axis=0)
            keep = low if h % 2 == 0 else jnp.logical_not(low)
            base = j * 2 * rows
            qaug[g % 2, base : base + 2 * rows, :LATENT] = nt(q, wuk[:, at : at + NOPE]).astype(bf16)
            qaug[g % 2, base : base + 2 * rows, LATENT:] = jnp.where(keep, r, jnp.zeros_like(r))
        s = nt(qaug[g % 2], keys[...])
        s = (s.reshape(GROUP, 2 * rows, count) + bias[...][None]).reshape(GROUP * 2 * rows, count)
        m = jnp.max(s, axis=-1, keepdims=True)
        p = jnp.exp2((s - m) * c)
        total = jnp.sum(p, axis=-1, keepdims=True)
        acc = nn(p.astype(bf16), keys[:, :LATENT])
        mixed = (acc / total).astype(bf16)
        lse = m * c + jnp.log2(total)
        for j in range(GROUP):
            h = g * GROUP + j
            at = h * NOPE
            base = j * 2 * rows
            o = nn(mixed[base : base + 2 * rows], wuv[:, at : at + NOPE])
            own[:, at : at + NOPE] = o[:rows]
            message[:, at : at + NOPE] = o[rows:].astype(bf16)
            lse_all = jnp.where(out_lane == h, lse[base : base + 2 * rows], lse_all)
    own_lse[...] = lse_all[:rows]
    rest = lse_all[rows:]
    hi = rest.astype(bf16)
    rest = rest - hi.astype(f32)
    mid = rest.astype(bf16)
    last = (rest - mid.astype(f32)).astype(bf16)
    message[:, wide : wide + 128] = hi
    message[:, wide + 128 : wide + 256] = mid
    message[:, wide + 256 : wide + 384] = last


VMEM = pl.BlockSpec(memory_space=pltpu.VMEM)
SMEM = pl.BlockSpec(memory_space=pltpu.SMEM)
ANY = pl.BlockSpec(memory_space=pl.ANY)


def params(mib):
    return pltpu.CompilerParams(vmem_limit_bytes=mib * MIB)


def held_in_vmem(*arrays):
    return tuple(pltpu.with_memory_space_constraint(x, pltpu.VMEM) for x in arrays)


def cost(flops, exps=0):
    return pl.CostEstimate(flops=flops, transcendentals=exps, bytes_accessed=4 * MIB)


def attention_part(coords, starts, q0, q1, wuk, wuv, pieces, half, earlier):
    rows = pieces[0].shape[0] // 2
    heads = wuk.shape[1] // NOPE
    wide = heads * NOPE
    scale = (NOPE + ROPE) ** -0.5
    return pl.pallas_call(
        functools.partial(attention_kernel, rows, heads, half, scale),
        out_shape=(
            pltpu.VMEM((rows, wide), f32),
            pltpu.VMEM((rows, 128), f32),
            pltpu.VMEM((rows, wide + 384), bf16),
        ),
        in_specs=[SMEM, SMEM] + [VMEM] * 13 + [ANY],
        out_specs=(VMEM, VMEM, VMEM),
        scratch_shapes=[
            pltpu.VMEM((16 * rows, LATENT + 2 * ROPE), bf16),
            pltpu.VMEM((2 * rows, 16 * rows), f32),
            pltpu.VMEM((2, GROUP * 2 * rows, LATENT + 2 * ROPE), bf16),
        ],
        compiler_params=params(24),
        cost_estimate=cost(
            2 * heads * 2 * rows * 16 * rows * (2 * LATENT + 2 * ROPE), heads * 32 * rows * rows
        ),
    )(coords, starts, *held_in_vmem(q0, q1, wuk, wuv, *pieces, earlier))


def combine_kernel(rows, heads, half, coords, starts, lens, *refs):
    weights, out, copied, sem = refs[6:]
    moving = pltpu.make_async_copy(weights, copied, sem)
    moving.start()
    y, z, core = coords[0], coords[1], coords[2]
    live = lens[core] - starts[core]
    base = y * half + z * rows
    wide = heads * NOPE
    alive = base + lax.broadcasted_iota(jnp.int32, (rows, 1), 0) < live
    for part in range(2):
        own, lse, got = refs[3 * part : 3 * part + 3]
        there = (
            got[:, wide : wide + 128].astype(f32)
            + got[:, wide + 128 : wide + 256].astype(f32)
            + got[:, wide + 256 : wide + 384].astype(f32)
        )
        share = 1.0 / (1.0 + jnp.exp2(there - lse[...]))
        for h in range(heads):
            at = h * NOPE
            w = share[:, h : h + 1]
            o = own[:, at : at + NOPE] * w + got[:, at : at + NOPE].astype(f32) * (1.0 - w)
            at = part * wide + h * NOPE
            out[:, at : at + NOPE] = jnp.where(alive, o, 0.0).astype(bf16)
    moving.wait()


def combine(coords, starts, lens, parts, weights, half):
    rows, wide = parts[0].shape
    return pl.pallas_call(
        functools.partial(combine_kernel, rows, wide // NOPE, half),
        out_shape=(
            pltpu.VMEM((rows, 2 * wide), bf16),
            pltpu.VMEM(weights.shape, weights.dtype),
        ),
        in_specs=[SMEM, SMEM, SMEM] + [VMEM] * 6 + [ANY],
        out_specs=(VMEM, ANY),
        scratch_shapes=[pltpu.SemaphoreType.DMA(())],
        compiler_params=params(4),
    )(coords, starts, lens, *held_in_vmem(*parts), weights)


def project_kernel(rows, at, extra, *refs):
    coords = refs[0]
    count = len(at)
    pieces = refs[1 : 1 + count]
    w00, w01, w10, w11 = refs[1 + count : 5 + count]
    out, held = refs[5 + count + extra :]
    z, same = coords[1], coords[3]
    depth = w00.shape[1]
    place, slots = 0, []
    for piece, slot in zip(pieces, at):
        held[place : place + piece.shape[0], :] = piece[...]
        if slot is not None:
            slots.append((slot, place))
        place += piece.shape[0]
    left = held[:, :depth]
    right = held[:, depth:]
    mine = nt(left, w00[...]) + nt(right, w10[...])
    other = nt(left, w01[...]) + nt(right, w11[...])
    swapped = same == 0
    both = jnp.concatenate(
        [jnp.where(swapped, other, mine), jnp.where(swapped, mine, other)], axis=1
    ).astype(bf16)
    for slot, place in slots:
        out[(z - slot) & 7] = both[place : place + rows]


def project(coords, rows, pieces, at, weights, before=None):
    wide = pieces[0].shape[1]
    cols = weights[0].shape[0]
    total = sum(p.shape[0] for p in pieces)
    extra = 0 if before is None else 1
    inputs = held_in_vmem(*pieces, *weights)
    if extra:
        inputs += held_in_vmem(before)
    return pl.pallas_call(
        functools.partial(project_kernel, rows, at, extra),
        out_shape=pltpu.VMEM((8, rows, 2 * cols), bf16),
        in_specs=[SMEM] + [VMEM] * (len(pieces) + 4) + [ANY] * extra,
        out_specs=VMEM,
        scratch_shapes=[pltpu.VMEM((total, wide), bf16)],
        input_output_aliases={5 + len(pieces): 0} if extra else {},
        compiler_params=params(12),
        cost_estimate=cost(4 * total * wide * cols),
    )(coords, *inputs)


def level_kernel(*refs):
    pass


def level(arrays, earlier=()):
    count = len(arrays)
    return pl.pallas_call(
        level_kernel,
        out_shape=tuple(pltpu.VMEM(x.shape, x.dtype) for x in arrays),
        in_specs=[ANY] * (count + len(earlier)),
        out_specs=(ANY,) * count,
        input_output_aliases={i: i for i in range(count)},
        compiler_params=params(1),
    )(*held_in_vmem(*arrays, *earlier))


def swap(x, axis):
    return lax.ppermute(x, axis, [(0, 1), (1, 0)])


UP = [(i, (i + 1) % 8) for i in range(8)]
DOWN = [(i, (i - 1) % 8) for i in range(8)]


def step(a, b):
    return lax.ppermute(a, "z", UP), lax.ppermute(b, "z", DOWN)


def last(a, b):
    cut = a.shape[0] // 2
    return step(a[:cut], b[cut:])


def in_order(x, ups, downs, ends):
    return [x, *ups, *downs[::-1], *ends]


def local(q_nope, q_rope, cache_latent, stretch_latent, w_uk, w_uv, w_o, stretch_start, prompt_len):
    rows = q_nope.shape[1]
    core = lax.axis_index("core")
    y = lax.axis_index("yl")
    yh = lax.axis_index("yh")
    z = lax.axis_index("z")
    half = 8 * rows
    coords = jnp.stack([y, z, core, (yh == y).astype(jnp.int32)])

    def mine(x):
        return lax.dynamic_index_in_dim(x, core, 0, keepdims=False)

    def other(x):
        return lax.dynamic_index_in_dim(x, 1 - core, 0, keepdims=False)

    latent = jnp.concatenate([mine(cache_latent), mine(stretch_latent)], axis=0)
    q_own = jnp.concatenate([mine(q_nope), mine(q_rope)], axis=1)
    q_sent = jnp.concatenate([other(q_nope), other(q_rope)], axis=1)
    u1, d1 = level(step(latent, latent))
    q_own_y = swap(q_own, "yl")
    q_got = swap(q_sent, "core")
    u2, d2, q_got = level((*step(u1, d1), q_got), (q_own_y,))
    q_got_y = swap(q_got, "yl")
    w_uk2 = swap(w_uk, "core")
    w_uv2 = swap(w_uv, "core")
    u3, d3 = level(step(u2, d2), (q_got_y, w_uk2, w_uv2))
    pieces = in_order(latent, (u1, u2, u3), (d1, d2, d3), last(u3, d3))

    a = attention_part(
        coords, stretch_start, q_own, q_own_y, w_uk, w_uv, pieces, half, u1
    )
    b = attention_part(coords, stretch_start, q_got, q_got_y, w_uk2, w_uv2, pieces, half, a[1])
    parts = (*a[:2], swap(a[2], "yl"), *b[:2], swap(b[2], "yl"))
    attention, w_t = combine(coords, stretch_start, prompt_len, parts, w_o.T, half)
    u1, d1 = level(step(attention, attention))
    w_t_c = swap(w_t, "core")
    w_t_y = swap(w_t, "yl")
    u2, d2 = level(step(u1, d1), (w_t_c,))
    u3, d3, w_t_y = level((*step(u2, d2), w_t_y))
    w_t_cy = swap(w_t_y, "core")
    rounds = in_order(attention, (u1, u2, u3), (d1, d2, d3), last(u3, d3))
    weights = (w_t, w_t_y, w_t_c, w_t_cy)

    early, late = (0, 1, 2, 6, 7), (3, 5, 4, None)
    before = project(coords, rows, [rounds[i if i < 4 else i - 1] for i in early], early, weights)
    partial = project(
        coords, rows, [rounds[3], rounds[4], rounds[7], rounds[8]], late, weights, before
    )
    parts = lax.all_to_all(partial, ("x", "core"), 0, 0, tiled=True)
    cols = w_o.shape[1]
    summed = jnp.sum(parts.reshape(4, 2, rows, 2 * cols).astype(f32), axis=0).astype(bf16)
    got = lax.ppermute(summed[:, :, :cols], ("yl", "yh"), [(0, 0), (1, 2), (2, 1), (3, 3)])
    got2 = lax.ppermute(summed[:, :, cols:], ("yl", "yh"), [(0, 2), (2, 3), (1, 0), (3, 1)])
    return (got.astype(f32) + got2.astype(f32)).astype(bf16)


def solution(mesh):
    fine = Mesh(mesh.devices.reshape(2, 8, 2, 4, 2), ("yl", "z", "yh", "x", "core"))
    ctx = ("yl", "z")
    head = ("yh", "x", "core")
    placed = (
        P(None, ctx, head),
        P(None, ctx, head),
        P(None, ctx, None),
        P(None, ctx, None),
        P(None, head),
        P(None, head),
        P(head, ctx),
        P(),
        P(),
    )
    return jax.shard_map(
        local, mesh=fine, in_specs=placed, out_specs=P(None, head, ctx), check_vma=False
    )
```

time: 142 us -> 121 us (0.85)
  local copies, waits for them, and re-layouts: 25.8 us -> 1.84 us
  blocking collectives: 0 us -> 18.7 us
  Pallas kernels: 22.7 us -> 15.9 us
  starting transfers between devices: 40.4 us -> 37 us
  waiting for transfers between devices: 49.1 us -> 45.8 us
    all_to_all x0 -> x1, blocking collectives: none -> 18.7 us  [local(): parts = lax.all_to_all(partial, ('x', 'core'), 0, 0, tiled=True)]
    all_to_all x1 -> x0, waiting for transfers between devices: 14.6 us -> none  [local(): parts = lax.all_to_all(partial, ('x', 'core'), 0, 0, tiled=True)]
    unnamed x51 -> x18, local copies, waits for them, and re-layouts: 8.23 us -> 0.69 us
    slice x10 -> x5, local copies, waits for them, and re-layouts: 7.05 us -> 0.14 us  [the longest x1 0.1 us: local(): summed[:, :, :cols]]
    ppermute x18, waiting for transfers between devices: 30.4 us -> 37.1 us  [the longest x16 32.2 us: step(): return (lax.ppermute(a, 'z', UP), lax.ppermute(b, 'z', DOWN))]
    ppermute x3 -> x0, local copies, waits for them, and re-layouts: 4.87 us -> none  [swap(): return lax.ppermute(x, axis, [(0, 1), (1, 0)])]
    ppermute x9 -> x10, waiting for transfers between devices: 4.14 us -> 8.69 us  [swap(): return lax.ppermute(x, axis, [(0, 1), (1, 0)])]
    all_to_all x1 -> x0, starting transfers between devices: 4.3 us -> none  [local(): parts = lax.all_to_all(partial, ('x', 'core'), 0, 0, tiled=True)]
  transfers between devices with their start and end apart: 28 -> 28, of which waited for: 13 -> 17; matrix products, arithmetic and copies ran while one was open for 14% -> 0% of each run, Pallas kernels for 12% -> 2%
where the time goes in v2:
time: 121 us; the launch traced here: 120 us
  waiting for transfers between devices  45.8 us (38%)
  starting transfers between devices  37 us (31%)
  blocking collectives  18.7 us (15%)
  Pallas kernels  15.9 us (13%)
  local copies, waits for them, and re-layouts  1.84 us (2%)
    ppermute x16, waiting for transfers between devices, step(): return (lax.ppermute(a, 'z', UP), lax.ppermute(b, 'z', DOWN))  32.2 us
    ppermute x16, starting transfers between devices, step(): return (lax.ppermute(a, 'z', UP), lax.ppermute(b, 'z', DOWN))  28 us
    all_to_all x1, blocking collectives, local(): parts = lax.all_to_all(partial, ('x', 'core'), 0, 0, tiled=True)  18.7 us
    pallas_call x2, Pallas kernels, attention_part(): pl.pallas_call(functools.partial(attention_kernel, rows, heads, half, sca...  10.8 us
    ppermute x10, waiting for transfers between devices, swap(): return lax.ppermute(x, axis, [(0, 1), (1, 0)])  8.69 us
    ppermute x10, starting transfers between devices, swap(): return lax.ppermute(x, axis, [(0, 1), (1, 0)])  5.37 us
    pallas_call x2, Pallas kernels, project(): pl.pallas_call(functools.partial(project_kernel, rows, at, extra), out_sh...  3.96 us
    ppermute x1, starting transfers between devices, local(): lax.ppermute(summed[:, :, :cols], ('yl', 'yh'), [(0, 0), (1, 2), (2, 1),...  3.49 us
  transfers between devices with their start and end apart: 28, of which 17 were waited for; matrix products, arithmetic and copies ran while one was open for 0% of the time, Pallas kernels for 2%

profile of v2, /device:TPU:8, one launch (start us, length us, event | category | flops | bytes accessed | tf_op | source)
XLA Modules:
  0.0 120.4 jit_solution(315825183344676007)
XLA Ops:
  0.0 1.0 dynamic-slice_bitcast_fusion.2
  1.0 0.0 copy-start.7
  1.0 2.0 %collective-permute-start.1 = (bf16[128,576]{1,0:T(8,128)(2,1)S(1)}, bf16[128,576]{1,0:T(8,128)(2,1)S(1)}, u32[]{:S(2)}, u32[]{:S(2)}) collective-permute-start(bf16[128,576]{1,0:T(8,128)(2,1)S(1)} %pad_maximum_fusion.2.refs_6_), channel_id=1, source_target_pairs={{0,16},{16,32},{32,48},{48,64},{64,80},{80,96},{96,112},{112,0},{1... | collective-permute-start | bytes 442376 | tf_op jit(solution)/shard_map/ppermute | solution.py:262
  3.0 4.0 %collective-permute-start.2 = (bf16[128,576]{1,0:T(8,128)(2,1)S(1)}, bf16[128,576]{1,0:T(8,128)(2,1)S(1)}, u32[]{:S(2)}, u32[]{:S(2)}) collective-permute-start(bf16[128,576]{1,0:T(8,128)(2,1)S(1)} %pad_maximum_fusion.2.refs_6_), channel_id=1, source_target_pairs={{0,112},{16,0},{32,16},{48,32},{64,48},{80,64},{96,80},{112,96},{1... | collective-permute-start | bytes 442376 | tf_op jit(solution)/shard_map/ppermute | solution.py:262
  7.0 0.0 collective-permute-start.10
  7.0 0.5 collective-permute-start.9
  7.6 0.5 collective-permute-start
  8.2 3.0 %collective-permute-done.1.refs_0_ = bf16[128,576]{1,0:T(8,128)(2,1)S(1)} collective-permute-done((bf16[128,576]{1,0:T(8,128)(2,1)S(1)}, bf16[128,576]{1,0:T(8,128)(2,1)S(1)}, u32[]{:S(2)}, u32[]{:S(2)}) %collective-permute-start.1) | collective-permute-done | bytes 147488 | tf_op jit(solution)/shard_map/ppermute | solution.py:262
  11.2 0.0 collective-permute-start.5
  11.2 0.1 collective-permute-start.3
  11.3 3.3 %collective-permute-done.refs_3_ = bf16[64,1536]{1,0:T(8,128)(2,1)S(1)} collective-permute-done((bf16[64,1536]{1,0:T(8,128)(2,1)S(1)}, bf16[64,1536]{1,0:T(8,128)(2,1)S(1)}, u32[]{:S(2)}, u32[]{:S(2)}) %collective-permute-start) | collective-permute-done | bytes 196640 | tf_op jit(solution)/shard_map/ppermute | solution.py:254
  14.5 1.9 %collective-permute-start.4 = (bf16[128,576]{1,0:T(8,128)(2,1)S(1)}, bf16[128,576]{1,0:T(8,128)(2,1)}, u32[]{:S(2)}, u32[]{:S(2)}) collective-permute-start(bf16[128,576]{1,0:T(8,128)(2,1)S(1)} %get-tuple-element.28.refs_12_), channel_id=1, source_target_pairs={{0,112},{16,0},{32,16},{48,32},{64,48},{80,64},{96,80},{112,96},{1... | collective-permute-start | bytes 442376 | tf_op jit(solution)/shard_map/ppermute | solution.py:262
  16.5 2.6 %collective-permute-done.3.refs_0_ = bf16[128,576]{1,0:T(8,128)(2,1)} collective-permute-done((bf16[128,576]{1,0:T(8,128)(2,1)S(1)}, bf16[128,576]{1,0:T(8,128)(2,1)}, u32[]{:S(2)}, u32[]{:S(2)}) %collective-permute-start.3) | collective-permute-done | bytes 147488 | tf_op jit(solution)/shard_map/ppermute | solution.py:262
  19.1 0.9 collective-permute-done.4.refs_1_
  20.0 0.5 collective-permute-start.8
  20.4 0.3 collective-permute-start.6
  20.7 2.9 %collective-permute-start.7 = (bf16[128,576]{1,0:T(8,128)(2,1)}, bf16[128,576]{1,0:T(8,128)(2,1)S(1)}, u32[]{:S(2)}, u32[]{:S(2)}) collective-permute-start(bf16[128,576]{1,0:T(8,128)(2,1)} %get-tuple-element.30.refs_11_), channel_id=1, source_target_pairs={{0,112},{16,0},{32,16},{48,32},{64,48},{80,64},{96,80},{112,96},{1... | collective-permute-start | bytes 442376 | tf_op jit(solution)/shard_map/ppermute | solution.py:262
  23.7 3.5 %collective-permute-done.6.refs_0_ = bf16[128,576]{1,0:T(8,128)(2,1)S(1)} collective-permute-done((bf16[128,576]{1,0:T(8,128)(2,1)}, bf16[128,576]{1,0:T(8,128)(2,1)S(1)}, u32[]{:S(2)}, u32[]{:S(2)}) %collective-permute-start.6) | collective-permute-done | bytes 147488 | tf_op jit(solution)/shard_map/ppermute | solution.py:262
  27.2 0.0 collective-permute-done.8.refs_2_.refs_3_
  27.2 0.0 collective-permute-done.10.refs_4_.refs_5_
  27.2 0.0 collective-permute-done.9.refs_3_.refs_4_
  27.2 1.7 %collective-permute-start.11 = (bf16[64,576]{1,0:T(8,128)(2,1)S(1)}, bf16[64,576]{1,0:T(8,128)(2,1)S(1)}, u32[]{:S(2)}, u32[]{:S(2)}) collective-permute-start(bf16[64,576]{1,0:T(8,128)(2,1)S(1)} %slice.18), channel_id=1, source_target_pairs={{0,16},{16,32},{32,48},{48,64},{64,80},{80,96},{96,112},{112,0},{1... | collective-permute-start | bytes 221192 | tf_op jit(solution)/shard_map/ppermute | solution.py:262
  28.9 1.9 %collective-permute-start.12 = (bf16[64,576]{1,0:T(8,128)(2,1)S(1)}, bf16[64,576]{1,0:T(8,128)(2,1)S(1)}, u32[]{:S(2)}, u32[]{:S(2)}) collective-permute-start(bf16[64,576]{1,0:T(8,128)(2,1)S(1)} %slice.19), channel_id=1, source_target_pairs={{0,112},{16,0},{32,16},{48,32},{64,48},{80,64},{96,80},{112,96},{1... | collective-permute-start | bytes 221192 | tf_op jit(solution)/shard_map/ppermute | solution.py:262
  30.8 0.1 pad_add_fusion.refs_0_.coords
  30.9 2.1 %collective-permute-done.11.refs_13_ = bf16[64,576]{1,0:T(8,128)(2,1)S(1)} collective-permute-done((bf16[64,576]{1,0:T(8,128)(2,1)S(1)}, bf16[64,576]{1,0:T(8,128)(2,1)S(1)}, u32[]{:S(2)}, u32[]{:S(2)}) %collective-permute-start.11) | collective-permute-done | bytes 73760 | tf_op jit(solution)/shard_map/ppermute | solution.py:262
  32.9 0.7 collective-permute-done.12.refs_14_
  33.6 5.4 %shard_map.94 = (f32[64,1024]{1,0:T(8,128)S(1)}, f32[64,128]{1,0:T(8,128)S(1)}, bf16[64,1408]{1,0:T(8,128)(2,1)S(1)}) custom-call(s32[4]{0:T(128)S(1)} %pad_add_fusion.refs_0_.coords, s32[2]{0:T(128)S(1)} %copy-done.3, bf16[64,1536]{1,0:T(8,128)(2,1)S(1)} %pad_maximum_fusion.refs_2_, bf16[64,1536]{1,0:T(8,128)(2,1)S(1)} %collective-permute-done.refs_3_, ...), custom_call_target="tpu_custom_call" | custom-call | flops 2415919104 | bytes 4194304 | tf_op jit(solution)/shard_map/pallas_call | solution.py:129
  39.0 0.0 copy-start
  39.0 5.4 %shard_map.95 = (f32[64,1024]{1,0:T(8,128)S(1)}, f32[64,128]{1,0:T(8,128)S(1)}, bf16[64,1408]{1,0:T(8,128)(2,1)S(1)}) custom-call(s32[4]{0:T(128)S(1)} %pad_add_fusion.refs_0_.coords, s32[2]{0:T(128)S(1)} %copy-done.3, bf16[64,1536]{1,0:T(8,128)(2,1)S(1)} %get-tuple-element.31.refs_2_, bf16[64,1536]{1,0:T(8,128)(2,1)S(1)} %collective-permute-done.8.refs_2_.refs_3_, ...), custom_call_target="tpu_custom_call" | custom-call | flops 2415919104 | bytes 4194304 | tf_op jit(solution)/shard_map/pallas_call | solution.py:129
  44.4 1.7 %collective-permute-start.14 = (bf16[64,1408]{1,0:T(8,128)(2,1)S(1)}, bf16[64,1408]{1,0:T(8,128)(2,1)S(1)}, u32[]{:S(2)}, u32[]{:S(2)}) collective-permute-start(bf16[64,1408]{1,0:T(8,128)(2,1)S(1)} %get-tuple-element.39), channel_id=1, source_target_pairs={{0,128},{128,0},{1,129},{129,1},{2,130},{130,2},{3,131},{131,3},{4... | collective-permute-start | bytes 540680 | tf_op jit(solution)/shard_map/ppermute | solution.py:254
  46.1 0.4 collective-permute-start.13
  46.5 3.5 %collective-permute-done.14.refs_5_ = bf16[64,1408]{1,0:T(8,128)(2,1)S(1)} collective-permute-done((bf16[64,1408]{1,0:T(8,128)(2,1)S(1)}, bf16[64,1408]{1,0:T(8,128)(2,1)S(1)}, u32[]{:S(2)}, u32[]{:S(2)}) %collective-permute-start.14) | collective-permute-done | bytes 180256 | tf_op jit(solution)/shard_map/ppermute | solution.py:254
  50.0 1.9 %collective-permute-done.13.refs_2_ = bf16[64,1408]{1,0:T(8,128)(2,1)S(1)} collective-permute-done((bf16[64,1408]{1,0:T(8,128)(2,1)S(1)}, bf16[64,1408]{1,0:T(8,128)(2,1)S(1)}, u32[]{:S(2)}, u32[]{:S(2)}) %collective-permute-start.13) | collective-permute-done | bytes 180256 | tf_op jit(solution)/shard_map/ppermute | solution.py:254
  51.9 0.7 copy-done.4
  52.6 1.2 shard_map.96
  53.8 0.1 collective-permute-start.19
  53.9 1.7 %collective-permute-start.22 = (bf16[448,1024]{1,0:T(8,128)(2,1)S(1)}, bf16[448,1024]{1,0:T(8,128)(2,1)S(1)}, u32[]{:S(2)}, u32[]{:S(2)}) collective-permute-start(bf16[448,1024]{1,0:T(8,128)(2,1)S(1)} %get-tuple-element.43.refs_6_.refs_5_), channel_id=1, source_target_pairs={{0,128},{128,0},{1,129},{129,1},{2,130},{130,2},{3,131},{131,3},{4... | collective-permute-start | bytes 2752520 | tf_op jit(solution)/shard_map/ppermute | solution.py:254
  55.5 2.5 %collective-permute-start.15 = (bf16[64,2048]{1,0:T(8,128)(2,1)S(1)}, bf16[64,2048]{1,0:T(8,128)(2,1)S(1)}, u32[]{:S(2)}, u32[]{:S(2)}) collective-permute-start(bf16[64,2048]{1,0:T(8,128)(2,1)S(1)} %get-tuple-element.40.refs_1_), channel_id=1, source_target_pairs={{0,16},{16,32},{32,48},{48,64},{64,80},{80,96},{96,112},{112,0},{1... | collective-permute-start | bytes 786440 | tf_op jit(solution)/shard_map/ppermute | solution.py:262
  58.1 0.7 collective-permute-start.16
  58.8 6.3 %collective-permute-done.15.refs_0_ = bf16[64,2048]{1,0:T(8,128)(2,1)S(1)} collective-permute-done((bf16[64,2048]{1,0:T(8,128)(2,1)S(1)}, bf16[64,2048]{1,0:T(8,128)(2,1)S(1)}, u32[]{:S(2)}, u32[]{:S(2)}) %collective-permute-start.15) | collective-permute-done | bytes 262176 | tf_op jit(solution)/shard_map/ppermute | solution.py:262
  65.1 1.3 %collective-permute-done.16.refs_1_ = bf16[64,2048]{1,0:T(8,128)(2,1)S(1)} collective-permute-done((bf16[64,2048]{1,0:T(8,128)(2,1)S(1)}, bf16[64,2048]{1,0:T(8,128)(2,1)S(1)}, u32[]{:S(2)}, u32[]{:S(2)}) %collective-permute-start.16) | collective-permute-done | bytes 262176 | tf_op jit(solution)/shard_map/ppermute | solution.py:262
  66.4 1.7 %collective-permute-start.17 = (bf16[64,2048]{1,0:T(8,128)(2,1)S(1)}, bf16[64,2048]{1,0:T(8,128)(2,1)S(1)}, u32[]{:S(2)}, u32[]{:S(2)}) collective-permute-start(bf16[64,2048]{1,0:T(8,128)(2,1)S(1)} %get-tuple-element.41.refs_2_), channel_id=1, source_target_pairs={{0,16},{16,32},{32,48},{48,64},{64,80},{80,96},{96,112},{112,0},{1... | collective-permute-start | bytes 786440 | tf_op jit(solution)/shard_map/ppermute | solution.py:262
  68.2 1.5 %collective-permute-start.18 = (bf16[64,2048]{1,0:T(8,128)(2,1)S(1)}, bf16[64,2048]{1,0:T(8,128)(2,1)S(1)}, u32[]{:S(2)}, u32[]{:S(2)}) collective-permute-start(bf16[64,2048]{1,0:T(8,128)(2,1)S(1)} %get-tuple-element.42.refs_5_), channel_id=1, source_target_pairs={{0,112},{16,0},{32,16},{48,32},{64,48},{80,64},{96,80},{112,96},{1... | collective-permute-start | bytes 786440 | tf_op jit(solution)/shard_map/ppermute | solution.py:262
  69.7 5.5 %collective-permute-done.17.refs_0_ = bf16[64,2048]{1,0:T(8,128)(2,1)S(1)} collective-permute-done((bf16[64,2048]{1,0:T(8,128)(2,1)S(1)}, bf16[64,2048]{1,0:T(8,128)(2,1)S(1)}, u32[]{:S(2)}, u32[]{:S(2)}) %collective-permute-start.17) | collective-permute-done | bytes 262176 | tf_op jit(solution)/shard_map/ppermute | solution.py:262
  75.1 0.0 collective-permute-done.18.refs_1_
  75.2 0.0 collective-permute-done.19.refs_2_.refs_8_.refs_7_
  75.2 1.2 %collective-permute-start.20 = (bf16[64,2048]{1,0:T(8,128)(2,1)S(1)}, bf16[64,2048]{1,0:T(8,128)(2,1)S(1)}, u32[]{:S(2)}, u32[]{:S(2)}) collective-permute-start(bf16[64,2048]{1,0:T(8,128)(2,1)S(1)} %get-tuple-element.44.refs_3_), channel_id=1, source_target_pairs={{0,16},{16,32},{32,48},{48,64},{64,80},{80,96},{96,112},{112,0},{1... | collective-permute-start | bytes 786440 | tf_op jit(solution)/shard_map/ppermute | solution.py:262
  76.4 2.1 %collective-permute-start.21 = (bf16[64,2048]{1,0:T(8,128)(2,1)S(1)}, bf16[64,2048]{1,0:T(8,128)(2,1)S(1)}, u32[]{:S(2)}, u32[]{:S(2)}) collective-permute-start(bf16[64,2048]{1,0:T(8,128)(2,1)S(1)} %get-tuple-element.45.refs_4_), channel_id=1, source_target_pairs={{0,112},{16,0},{32,16},{48,32},{64,48},{80,64},{96,80},{112,96},{1... | collective-permute-start | bytes 786440 | tf_op jit(solution)/shard_map/ppermute | solution.py:262
  78.5 0.0 collective-permute-done.22.refs_2_
  78.5 4.6 %collective-permute-done.20.refs_0_ = bf16[64,2048]{1,0:T(8,128)(2,1)S(1)} collective-permute-done((bf16[64,2048]{1,0:T(8,128)(2,1)S(1)}, bf16[64,2048]{1,0:T(8,128)(2,1)S(1)}, u32[]{:S(2)}, u32[]{:S(2)}) %collective-permute-start.20) | collective-permute-done | bytes 262176 | tf_op jit(solution)/shard_map/ppermute | solution.py:262
  83.1 1.6 %collective-permute-start.23 = (bf16[32,2048]{1,0:T(8,128)(2,1)S(1)}, bf16[32,2048]{1,0:T(8,128)(2,1)S(1)}, u32[]{:S(2)}, u32[]{:S(2)}) collective-permute-start(bf16[32,2048]{1,0:T(8,128)(2,1)S(1)} %slice.20), channel_id=1, source_target_pairs={{0,16},{16,32},{32,48},{48,64},{64,80},{80,96},{96,112},{112,0},{1... | collective-permute-start | bytes 393224 | tf_op jit(solution)/shard_map/ppermute | solution.py:262
  84.7 1.8 %collective-permute-start.24 = (bf16[32,2048]{1,0:T(8,128)(2,1)S(1)}, bf16[32,2048]{1,0:T(8,128)(2,1)S(1)}, u32[]{:S(2)}, u32[]{:S(2)}) collective-permute-start(bf16[32,2048]{1,0:T(8,128)(2,1)S(1)} %slice.21), channel_id=1, source_target_pairs={{0,112},{16,0},{32,16},{48,32},{64,48},{80,64},{96,80},{112,96},{1... | collective-permute-start | bytes 393224 | tf_op jit(solution)/shard_map/ppermute | solution.py:262
  86.5 2.2 %shard_map.100.refs_9_ = bf16[8,64,896]{2,1,0:T(8,128)(2,1)S(1)} custom-call(s32[4]{0:T(128)S(1)} %pad_add_fusion.refs_0_.coords, bf16[64,2048]{1,0:T(8,128)(2,1)S(1)} %get-tuple-element.40.refs_1_, bf16[64,2048]{1,0:T(8,128)(2,1)S(1)} %get-tuple-element.41.refs_2_, bf16[64,2048]{1,0:T(8,128)(2,1)S(1)} %get-tuple-element.44.refs_3_, ...), custom_call_target="tpu_custom_call" | custom-call | flops 1174405120 | bytes 4194304 | tf_op jit(solution)/shard_map/pallas_call | solution.py:225
  88.6 1.7 %collective-permute-done.23.refs_3_ = bf16[32,2048]{1,0:T(8,128)(2,1)S(1)} collective-permute-done((bf16[32,2048]{1,0:T(8,128)(2,1)S(1)}, bf16[32,2048]{1,0:T(8,128)(2,1)S(1)}, u32[]{:S(2)}, u32[]{:S(2)}) %collective-permute-start.23) | collective-permute-done | bytes 131104 | tf_op jit(solution)/shard_map/ppermute | solution.py:262
  90.3 0.1 collective-permute-done.24.refs_4_
  90.4 1.8 %shard_map.101 = bf16[8,64,896]{2,1,0:T(8,128)(2,1)S(1)} custom-call(s32[4]{0:T(128)S(1)} %pad_add_fusion.refs_0_.coords, bf16[64,2048]{1,0:T(8,128)(2,1)S(1)} %get-tuple-element.46.refs_1_, bf16[64,2048]{1,0:T(8,128)(2,1)S(1)} %get-tuple-element.47.refs_2_, bf16[32,2048]{1,0:T(8,128)(2,1)S(1)} %collective-permute-done.23.refs_3_, ...), custom_call_target="tpu_custom_call", output_to_operand_aliasing={{}: (9, {})} | custom-call | flops 704643072 | bytes 4194304 | tf_op jit(solution)/shard_map/pallas_call | solution.py:225
  92.2 18.7 %all_to_all.5 = bf16[8,64,896]{2,1,0:T(8,128)(2,1)S(1)} all-to-all(bf16[8,64,896]{2,1,0:T(8,128)(2,1)S(1)} %shard_map.101), channel_id=1, replica_groups=mesh['yl'=2,'z'=8,'yh'=2,'x'=4,'core'=2] {'x','core'}, dimensions={0} | all-to-all | bytes 1835008 | tf_op jit(solution)/shard_map/all_to_all | solution.py:322
  111.0 0.1 reduce_sum.12
  111.1 0.1 fusion
  111.2 3.5 %collective-permute-start.26 = (bf16[2,64,448]{2,1,0:T(8,128)(2,1)S(1)}, bf16[2,64,448]{2,1,0:T(8,128)(2,1)S(1)}, u32[]{:S(2)}, u32[]{:S(2)}) collective-permute-start(bf16[2,64,448]{2,1,0:T(8,128)(2,1)S(1)} %get-tuple-element.51), channel_id=1, source_target_pairs={{0,0},{8,128},{128,8},{136,136},{1,1},{9,129},{129,9},{137,137},{2... | collective-permute-start | bytes 344072 | tf_op jit(solution)/shard_map/ppermute | solution.py:325
  114.7 0.1 collective-permute-start.27
  114.8 3.4 %collective-permute-done.26 = bf16[2,64,448]{2,1,0:T(8,128)(2,1)S(1)} collective-permute-done((bf16[2,64,448]{2,1,0:T(8,128)(2,1)S(1)}, bf16[2,64,448]{2,1,0:T(8,128)(2,1)S(1)}, u32[]{:S(2)}, u32[]{:S(2)}) %collective-permute-start.26) | collective-permute-done | bytes 114720 | tf_op jit(solution)/shard_map/ppermute | solution.py:325
  118.2 1.6 %collective-permute-done.27 = bf16[2,64,448]{2,1,0:T(8,128)(2,1)S(1)} collective-permute-done((bf16[2,64,448]{2,1,0:T(8,128)(2,1)S(1)}, bf16[2,64,448]{2,1,0:T(8,128)(2,1)S(1)}, u32[]{:S(2)}, u32[]{:S(2)}) %collective-permute-start.27) | collective-permute-done | bytes 114720 | tf_op jit(solution)/shard_map/ppermute | solution.py:326
  119.8 0.7 add_convert_fusion
  (36 shorter events, 0.2 us)
Async XLA Ops:
  0.0 7.6 %copy-start.8 = (bf16[2,64,512]{2,1,0:T(8,128)(2,1)S(1)}, bf16[2,64,512]{2,1,0:T(8,128)(2,1)}, u32[]{:S(2)}) copy-start(bf16[2,64,512]{2,1,0:T(8,128)(2,1)} %param.10) | copy-start | bytes 393220
  1.0 6.6 %copy-start.7 = (bf16[2,64,1024]{2,1,0:T(8,128)(2,1)S(1)}, bf16[2,64,1024]{2,1,0:T(8,128)(2,1)}, u32[]{:S(2)}) copy-start(bf16[2,64,1024]{2,1,0:T(8,128)(2,1)} %param.9) | copy-start | bytes 786436
  1.0 10.1 %collective-permute-start.1 = (bf16[128,576]{1,0:T(8,128)(2,1)S(1)}, bf16[128,576]{1,0:T(8,128)(2,1)S(1)}, u32[]{:S(2)}, u32[]{:S(2)}) collective-permute-start(bf16[128,576]{1,0:T(8,128)(2,1)S(1)} %pad_maximum_fusion.2.refs_6_), channel_id=1, source_target_pairs={{0,16},{16,32},{32,48},{48,64},{64,80},{80,96},{96,112},{112,0},{1... | collective-permute-start | bytes 442376 | tf_op jit(solution)/shard_map/ppermute | solution.py:262
  3.0 8.1 %collective-permute-start.2 = (bf16[128,576]{1,0:T(8,128)(2,1)S(1)}, bf16[128,576]{1,0:T(8,128)(2,1)S(1)}, u32[]{:S(2)}, u32[]{:S(2)}) collective-permute-start(bf16[128,576]{1,0:T(8,128)(2,1)S(1)} %pad_maximum_fusion.2.refs_6_), channel_id=1, source_target_pairs={{0,112},{16,0},{32,16},{48,32},{64,48},{80,64},{96,80},{112,96},{1... | collective-permute-start | bytes 442376 | tf_op jit(solution)/shard_map/ppermute | solution.py:262
  7.0 20.1 %collective-permute-start.10 = (bf16[512,1024]{1,0:T(8,128)(2,1)}, bf16[512,1024]{1,0:T(8,128)(2,1)S(1)}, u32[]{:S(2)}, u32[]{:S(2)}) collective-permute-start(bf16[512,1024]{1,0:T(8,128)(2,1)} %refs_5_.1), channel_id=1, source_target_pairs={{0,1},{1,0},{2,3},{3,2},{4,5},{5,4},{6,7},{7,6},{8,9},{9,8},{10,11... | collective-permute-start | bytes 3145736 | tf_op jit(solution)/shard_map/ppermute | solution.py:254
  7.0 20.1 %collective-permute-start.9 = (bf16[512,1024]{1,0:T(8,128)(2,1)}, bf16[512,1024]{1,0:T(8,128)(2,1)S(1)}, u32[]{:S(2)}, u32[]{:S(2)}) collective-permute-start(bf16[512,1024]{1,0:T(8,128)(2,1)} %refs_4_.1), channel_id=1, source_target_pairs={{0,1},{1,0},{2,3},{3,2},{4,5},{5,4},{6,7},{7,6},{8,9},{9,8},{10,11... | collective-permute-start | bytes 3145736 | tf_op jit(solution)/shard_map/ppermute | solution.py:254
  7.6 6.9 %collective-permute-start = (bf16[64,1536]{1,0:T(8,128)(2,1)S(1)}, bf16[64,1536]{1,0:T(8,128)(2,1)S(1)}, u32[]{:S(2)}, u32[]{:S(2)}) collective-permute-start(bf16[64,1536]{1,0:T(8,128)(2,1)S(1)} %pad_maximum_fusion.refs_2_), channel_id=1, source_target_pairs={{0,128},{128,0},{1,129},{129,1},{2,130},{130,2},{3,131},{131,3},{4... | collective-permute-start | bytes 589832 | tf_op jit(solution)/shard_map/ppermute | solution.py:254
  11.2 5.3 %collective-permute-start.5 = (bf16[64,1536]{1,0:T(8,128)(2,1)S(1)}, bf16[64,1536]{1,0:T(8,128)(2,1)S(1)}, u32[]{:S(2)}, u32[]{:S(2)}) collective-permute-start(bf16[64,1536]{1,0:T(8,128)(2,1)S(1)} %pad_maximum_fusion.1), channel_id=1, source_target_pairs={{0,1},{1,0},{2,3},{3,2},{4,5},{5,4},{6,7},{7,6},{8,9},{9,8},{10,11... | collective-permute-start | bytes 589832 | tf_op jit(solution)/shard_map/ppermute | solution.py:254
  11.2 8.8 %copy-start.1 = (bf16[128,576]{1,0:T(8,128)(2,1)}, bf16[128,576]{1,0:T(8,128)(2,1)S(1)}, u32[]{:S(2)}) copy-start(bf16[128,576]{1,0:T(8,128)(2,1)S(1)} %get-tuple-element.28.refs_12_) | copy-start | bytes 442372
  11.2 7.9 %collective-permute-start.3 = (bf16[128,576]{1,0:T(8,128)(2,1)S(1)}, bf16[128,576]{1,0:T(8,128)(2,1)}, u32[]{:S(2)}, u32[]{:S(2)}) collective-permute-start(bf16[128,576]{1,0:T(8,128)(2,1)S(1)} %get-tuple-element.27.refs_7_.refs_15_), channel_id=1, source_target_pairs={{0,16},{16,32},{32,48},{48,64},{64,80},{80,96},{96,112},{112,0},{1... | collective-permute-start | bytes 442376 | tf_op jit(solution)/shard_map/ppermute | solution.py:262
  14.5 5.4 %collective-permute-start.4 = (bf16[128,576]{1,0:T(8,128)(2,1)S(1)}, bf16[128,576]{1,0:T(8,128)(2,1)}, u32[]{:S(2)}, u32[]{:S(2)}) collective-permute-start(bf16[128,576]{1,0:T(8,128)(2,1)S(1)} %get-tuple-element.28.refs_12_), channel_id=1, source_target_pairs={{0,112},{16,0},{32,16},{48,32},{64,48},{80,64},{96,80},{112,96},{1... | collective-permute-start | bytes 442376 | tf_op jit(solution)/shard_map/ppermute | solution.py:262
  20.0 7.2 %collective-permute-start.8 = (bf16[64,1536]{1,0:T(8,128)(2,1)S(1)}, bf16[64,1536]{1,0:T(8,128)(2,1)S(1)}, u32[]{:S(2)}, u32[]{:S(2)}) collective-permute-start(bf16[64,1536]{1,0:T(8,128)(2,1)S(1)} %get-tuple-element.31.refs_2_), channel_id=1, source_target_pairs={{0,128},{128,0},{1,129},{129,1},{2,130},{130,2},{3,131},{131,3},{4... | collective-permute-start | bytes 589832 | tf_op jit(solution)/shard_map/ppermute | solution.py:254
  20.4 6.7 %collective-permute-start.6 = (bf16[128,576]{1,0:T(8,128)(2,1)}, bf16[128,576]{1,0:T(8,128)(2,1)S(1)}, u32[]{:S(2)}, u32[]{:S(2)}) collective-permute-start(bf16[128,576]{1,0:T(8,128)(2,1)} %get-tuple-element.29.refs_8_), channel_id=1, source_target_pairs={{0,16},{16,32},{32,48},{48,64},{64,80},{80,96},{96,112},{112,0},{1... | collective-permute-start | bytes 442376 | tf_op jit(solution)/shard_map/ppermute | solution.py:262
  20.7 6.4 %collective-permute-start.7 = (bf16[128,576]{1,0:T(8,128)(2,1)}, bf16[128,576]{1,0:T(8,128)(2,1)S(1)}, u32[]{:S(2)}, u32[]{:S(2)}) collective-permute-start(bf16[128,576]{1,0:T(8,128)(2,1)} %get-tuple-element.30.refs_11_), channel_id=1, source_target_pairs={{0,112},{16,0},{32,16},{48,32},{64,48},{80,64},{96,80},{112,96},{1... | collective-permute-start | bytes 442376 | tf_op jit(solution)/shard_map/ppermute | solution.py:262
  23.7 10.0 %copy-start.5 = (bf16[512,1024]{1,0:T(8,128)(2,1)S(1)}, bf16[512,1024]{1,0:T(8,128)(2,1)}, u32[]{:S(2)}) copy-start(bf16[512,1024]{1,0:T(8,128)(2,1)} %refs_4_.1) | copy-start | bytes 3145732
  23.7 10.0 %copy-start.6 = (bf16[512,1024]{1,0:T(8,128)(2,1)S(1)}, bf16[512,1024]{1,0:T(8,128)(2,1)}, u32[]{:S(2)}) copy-start(bf16[512,1024]{1,0:T(8,128)(2,1)} %refs_5_.1) | copy-start | bytes 3145732
  27.2 6.4 %copy-start.2 = (bf16[128,576]{1,0:T(8,128)(2,1)S(1)}, bf16[128,576]{1,0:T(8,128)(2,1)}, u32[]{:S(2)}) copy-start(bf16[128,576]{1,0:T(8,128)(2,1)} %copy-done.1) | copy-start | bytes 442372
  27.2 5.7 %collective-permute-start.11 = (bf16[64,576]{1,0:T(8,128)(2,1)S(1)}, bf16[64,576]{1,0:T(8,128)(2,1)S(1)}, u32[]{:S(2)}, u32[]{:S(2)}) collective-permute-start(bf16[64,576]{1,0:T(8,128)(2,1)S(1)} %slice.18), channel_id=1, source_target_pairs={{0,16},{16,32},{32,48},{48,64},{64,80},{80,96},{96,112},{112,0},{1... | collective-permute-start | bytes 221192 | tf_op jit(solution)/shard_map/ppermute | solution.py:262
  28.9 4.7 %collective-permute-start.12 = (bf16[64,576]{1,0:T(8,128)(2,1)S(1)}, bf16[64,576]{1,0:T(8,128)(2,1)S(1)}, u32[]{:S(2)}, u32[]{:S(2)}) collective-permute-start(bf16[64,576]{1,0:T(8,128)(2,1)S(1)} %slice.19), channel_id=1, source_target_pairs={{0,112},{16,0},{32,16},{48,32},{64,48},{80,64},{96,80},{112,96},{1... | collective-permute-start | bytes 221192 | tf_op jit(solution)/shard_map/ppermute | solution.py:262
  30.8 2.8 %copy-start.3 = (s32[2]{0:T(128)S(1)}, s32[2]{0:T(128)}, u32[]{:S(2)}) copy-start(s32[2]{0:T(128)} %starts.1) | copy-start | bytes 28
  39.0 12.9 %copy-start = (bf16[1024,448]{0,1:T(8,128)(2,1)S(1)}, bf16[1024,448]{0,1:T(8,128)(2,1)}, u32[]{:S(2)}) copy-start(bf16[1024,448]{0,1:T(8,128)(2,1)} %param.15) | copy-start | bytes 2752516
  44.4 5.6 %collective-permute-start.14 = (bf16[64,1408]{1,0:T(8,128)(2,1)S(1)}, bf16[64,1408]{1,0:T(8,128)(2,1)S(1)}, u32[]{:S(2)}, u32[]{:S(2)}) collective-permute-start(bf16[64,1408]{1,0:T(8,128)(2,1)S(1)} %get-tuple-element.39), channel_id=1, source_target_pairs={{0,128},{128,0},{1,129},{129,1},{2,130},{130,2},{3,131},{131,3},{4... | collective-permute-start | bytes 540680 | tf_op jit(solution)/shard_map/ppermute | solution.py:254
  46.1 5.8 %collective-permute-start.13 = (bf16[64,1408]{1,0:T(8,128)(2,1)S(1)}, bf16[64,1408]{1,0:T(8,128)(2,1)S(1)}, u32[]{:S(2)}, u32[]{:S(2)}) collective-permute-start(bf16[64,1408]{1,0:T(8,128)(2,1)S(1)} %get-tuple-element.36), channel_id=1, source_target_pairs={{0,128},{128,0},{1,129},{129,1},{2,130},{130,2},{3,131},{131,3},{4... | collective-permute-start | bytes 540680 | tf_op jit(solution)/shard_map/ppermute | solution.py:254
  51.9 0.7 copy-start.4
  53.8 21.4 %collective-permute-start.19 = (bf16[448,1024]{1,0:T(8,128)(2,1)S(1)}, bf16[448,1024]{1,0:T(8,128)(2,1)S(1)}, u32[]{:S(2)}, u32[]{:S(2)}) collective-permute-start(bf16[448,1024]{1,0:T(8,128)(2,1)S(1)} %get-tuple-element.43.refs_6_.refs_5_), channel_id=1, source_target_pairs={{0,1},{1,0},{2,3},{3,2},{4,5},{5,4},{6,7},{7,6},{8,9},{9,8},{10,11... | collective-permute-start | bytes 2752520 | tf_op jit(solution)/shard_map/ppermute | solution.py:254
  53.9 24.6 %collective-permute-start.22 = (bf16[448,1024]{1,0:T(8,128)(2,1)S(1)}, bf16[448,1024]{1,0:T(8,128)(2,1)S(1)}, u32[]{:S(2)}, u32[]{:S(2)}) collective-permute-start(bf16[448,1024]{1,0:T(8,128)(2,1)S(1)} %get-tuple-element.43.refs_6_.refs_5_), channel_id=1, source_target_pairs={{0,128},{128,0},{1,129},{129,1},{2,130},{130,2},{3,131},{131,3},{4... | collective-permute-start | bytes 2752520 | tf_op jit(solution)/shard_map/ppermute | solution.py:254
  55.5 9.6 %collective-permute-start.15 = (bf16[64,2048]{1,0:T(8,128)(2,1)S(1)}, bf16[64,2048]{1,0:T(8,128)(2,1)S(1)}, u32[]{:S(2)}, u32[]{:S(2)}) collective-permute-start(bf16[64,2048]{1,0:T(8,128)(2,1)S(1)} %get-tuple-element.40.refs_1_), channel_id=1, source_target_pairs={{0,16},{16,32},{32,48},{48,64},{64,80},{80,96},{96,112},{112,0},{1... | collective-permute-start | bytes 786440 | tf_op jit(solution)/shard_map/ppermute | solution.py:262
  58.1 8.4 %collective-permute-start.16 = (bf16[64,2048]{1,0:T(8,128)(2,1)S(1)}, bf16[64,2048]{1,0:T(8,128)(2,1)S(1)}, u32[]{:S(2)}, u32[]{:S(2)}) collective-permute-start(bf16[64,2048]{1,0:T(8,128)(2,1)S(1)} %get-tuple-element.40.refs_1_), channel_id=1, source_target_pairs={{0,112},{16,0},{32,16},{48,32},{64,48},{80,64},{96,80},{112,96},{1... | collective-permute-start | bytes 786440 | tf_op jit(solution)/shard_map/ppermute | solution.py:262
  66.4 8.7 %collective-permute-start.17 = (bf16[64,2048]{1,0:T(8,128)(2,1)S(1)}, bf16[64,2048]{1,0:T(8,128)(2,1)S(1)}, u32[]{:S(2)}, u32[]{:S(2)}) collective-permute-start(bf16[64,2048]{1,0:T(8,128)(2,1)S(1)} %get-tuple-element.41.refs_2_), channel_id=1, source_target_pairs={{0,16},{16,32},{32,48},{48,64},{64,80},{80,96},{96,112},{112,0},{1... | collective-permute-start | bytes 786440 | tf_op jit(solution)/shard_map/ppermute | solution.py:262
  68.2 7.0 %collective-permute-start.18 = (bf16[64,2048]{1,0:T(8,128)(2,1)S(1)}, bf16[64,2048]{1,0:T(8,128)(2,1)S(1)}, u32[]{:S(2)}, u32[]{:S(2)}) collective-permute-start(bf16[64,2048]{1,0:T(8,128)(2,1)S(1)} %get-tuple-element.42.refs_5_), channel_id=1, source_target_pairs={{0,112},{16,0},{32,16},{48,32},{64,48},{80,64},{96,80},{112,96},{1... | collective-permute-start | bytes 786440 | tf_op jit(solution)/shard_map/ppermute | solution.py:262
  75.2 7.9 %collective-permute-start.20 = (bf16[64,2048]{1,0:T(8,128)(2,1)S(1)}, bf16[64,2048]{1,0:T(8,128)(2,1)S(1)}, u32[]{:S(2)}, u32[]{:S(2)}) collective-permute-start(bf16[64,2048]{1,0:T(8,128)(2,1)S(1)} %get-tuple-element.44.refs_3_), channel_id=1, source_target_pairs={{0,16},{16,32},{32,48},{48,64},{64,80},{80,96},{96,112},{112,0},{1... | collective-permute-start | bytes 786440 | tf_op jit(solution)/shard_map/ppermute | solution.py:262
  76.4 6.6 %collective-permute-start.21 = (bf16[64,2048]{1,0:T(8,128)(2,1)S(1)}, bf16[64,2048]{1,0:T(8,128)(2,1)S(1)}, u32[]{:S(2)}, u32[]{:S(2)}) collective-permute-start(bf16[64,2048]{1,0:T(8,128)(2,1)S(1)} %get-tuple-element.45.refs_4_), channel_id=1, source_target_pairs={{0,112},{16,0},{32,16},{48,32},{64,48},{80,64},{96,80},{112,96},{1... | collective-permute-start | bytes 786440 | tf_op jit(solution)/shard_map/ppermute | solution.py:262
  83.0 3.4 %collective-permute-start.25 = (bf16[448,1024]{1,0:T(8,128)(2,1)S(1)}, bf16[448,1024]{1,0:T(8,128)(2,1)S(1)}, u32[]{:S(2)}, u32[]{:S(2)}) collective-permute-start(bf16[448,1024]{1,0:T(8,128)(2,1)S(1)} %get-tuple-element.48.refs_7_.refs_6_), channel_id=1, source_target_pairs={{0,1},{1,0},{2,3},{3,2},{4,5},{5,4},{6,7},{7,6},{8,9},{9,8},{10,11... | collective-permute-start | bytes 2752520 | tf_op jit(solution)/shard_map/ppermute | solution.py:254
  83.1 7.3 %collective-permute-start.23 = (bf16[32,2048]{1,0:T(8,128)(2,1)S(1)}, bf16[32,2048]{1,0:T(8,128)(2,1)S(1)}, u32[]{:S(2)}, u32[]{:S(2)}) collective-permute-start(bf16[32,2048]{1,0:T(8,128)(2,1)S(1)} %slice.20), channel_id=1, source_target_pairs={{0,16},{16,32},{32,48},{48,64},{64,80},{80,96},{96,112},{112,0},{1... | collective-permute-start | bytes 393224 | tf_op jit(solution)/shard_map/ppermute | solution.py:262
  84.7 5.7 %collective-permute-start.24 = (bf16[32,2048]{1,0:T(8,128)(2,1)S(1)}, bf16[32,2048]{1,0:T(8,128)(2,1)S(1)}, u32[]{:S(2)}, u32[]{:S(2)}) collective-permute-start(bf16[32,2048]{1,0:T(8,128)(2,1)S(1)} %slice.21), channel_id=1, source_target_pairs={{0,112},{16,0},{32,16},{48,32},{64,48},{80,64},{96,80},{112,96},{1... | collective-permute-start | bytes 393224 | tf_op jit(solution)/shard_map/ppermute | solution.py:262
  111.2 6.9 %collective-permute-start.26 = (bf16[2,64,448]{2,1,0:T(8,128)(2,1)S(1)}, bf16[2,64,448]{2,1,0:T(8,128)(2,1)S(1)}, u32[]{:S(2)}, u32[]{:S(2)}) collective-permute-start(bf16[2,64,448]{2,1,0:T(8,128)(2,1)S(1)} %get-tuple-element.51), channel_id=1, source_target_pairs={{0,0},{8,128},{128,8},{136,136},{1,1},{9,129},{129,9},{137,137},{2... | collective-permute-start | bytes 344072 | tf_op jit(solution)/shard_map/ppermute | solution.py:325
  114.7 5.0 %collective-permute-start.27 = (bf16[2,64,448]{2,1,0:T(8,128)(2,1)S(1)}, bf16[2,64,448]{2,1,0:T(8,128)(2,1)S(1)}, u32[]{:S(2)}, u32[]{:S(2)}) collective-permute-start(bf16[2,64,448]{2,1,0:T(8,128)(2,1)S(1)} %get-tuple-element.52), channel_id=1, source_target_pairs={{0,128},{128,136},{8,0},{136,8},{1,129},{129,137},{9,1},{137,9},{2... | collective-permute-start | bytes 344072 | tf_op jit(solution)/shard_map/ppermute | solution.py:326

commit v3 on v2

v3 whole, which is shorter than its diff:
```python
import functools

import jax
import jax.numpy as jnp
from jax import lax
from jax.experimental import pallas as pl
from jax.experimental.pallas import tpu as pltpu
from jax.sharding import Mesh, PartitionSpec as P

LATENT = 512
ROPE = 64
NOPE = 128
LOG2E = 1.4426950408889634
HIDDEN = -1e30
GROUP = 8
MIB = 1024 * 1024

f32 = jnp.float32
bf16 = jnp.bfloat16


def nt(a, b):
    return lax.dot_general(a, b, (((1,), (1,)), ((), ())), preferred_element_type=f32)


def nn(a, b):
    return jnp.dot(a, b, preferred_element_type=f32)


def load_keys(rows, slots, pieces, keys):
    place = 0
    for piece in pieces:
        height = piece.shape[0]
        value = piece[...]
        keys[place : place + height, :LATENT] = value[:, :LATENT]
        rope = value[:, LATENT:]
        keys[place : place + height, LATENT:] = jnp.concatenate([rope, rope], axis=1)
        place += height


def hidden_keys(rows, slots, half, starts):
    y, z = lax.axis_index("yl"), lax.axis_index("z")
    start = starts[lax.axis_index("core")]
    row = lax.broadcasted_iota(jnp.int32, (2 * rows, 2 * rows), 0)
    col = lax.broadcasted_iota(jnp.int32, (2 * rows, 2 * rows), 1)
    partner = (row >= rows).astype(jnp.int32)
    q_y = y + partner * (1 - 2 * y)
    q_pos = q_y * half + z * rows + row - partner * rows
    in_cache = col < rows
    limit = jnp.where(in_cache, start, q_pos + 1)
    inner = y * half + jnp.where(in_cache, col, col - rows)
    return jnp.concatenate(
        [
            jnp.where(inner + ((z - d) & 7) * rows < limit, 0.0, HIDDEN).astype(f32)
            for d in slots
        ],
        axis=1,
    )


def scores_of(q, keys, bias):
    s = nt(q, keys[...])
    height, count = bias.shape
    return (s.reshape(GROUP, height, count) + bias[...][None]).reshape(GROUP * height, count)


def tiled(x, like):
    return jnp.concatenate([x] * (like.shape[1] // 128), axis=1)


def first_kernel(rows, heads, half, slots, *refs):
    c = (NOPE + ROPE) ** -0.5 * LOG2E
    starts, q0, q1, wuk = refs[:4]
    pieces = refs[4 : 4 + len(slots)]
    qaug, acc, stats, keys, bias = refs[5 + len(slots) :]
    load_keys(rows, slots, pieces, keys)
    bias[...] = hidden_keys(rows, slots, half, starts)
    wide = heads * NOPE
    block = GROUP * 2 * rows
    low = lax.broadcasted_iota(jnp.int32, (2 * rows, 2 * ROPE), 1) < ROPE
    for g in range(heads // GROUP):
        for j in range(GROUP):
            h = g * GROUP + j
            at = h * NOPE
            q = jnp.concatenate([q0[:, at : at + NOPE], q1[:, at : at + NOPE]], axis=0)
            r0 = wide + (h // 2) * 2 * ROPE
            r = jnp.concatenate([q0[:, r0 : r0 + 2 * ROPE], q1[:, r0 : r0 + 2 * ROPE]], axis=0)
            keep = low if h % 2 == 0 else jnp.logical_not(low)
            base = h * 2 * rows
            qaug[base : base + 2 * rows, :LATENT] = nt(q, wuk[:, at : at + NOPE]).astype(bf16)
            qaug[base : base + 2 * rows, LATENT:] = jnp.where(keep, r, jnp.zeros_like(r))
        here = slice(g * block, (g + 1) * block)
        s = scores_of(qaug[here], keys, bias)
        m = jnp.broadcast_to(jnp.max(s, axis=-1, keepdims=True), (block, 128))
        p = jnp.exp2((s - tiled(m, s)) * c)
        acc[here] = nn(p.astype(bf16), keys[:, :LATENT])
        stats[here, :128] = m
        stats[here, 128:] = jnp.broadcast_to(jnp.sum(p, axis=-1, keepdims=True), (block, 128))


def second_kernel(rows, heads, half, slots, *refs):
    c = (NOPE + ROPE) ** -0.5 * LOG2E
    starts, qaug, acc, stats, wuv = refs[:5]
    count = len(refs) - 11
    pieces = refs[5 : 5 + count]
    own, own_lse, message, keys, bias = refs[6 + count :]
    load_keys(rows, slots, pieces, keys)
    bias[...] = hidden_keys(rows, slots, half, starts)
    wide = heads * NOPE
    block = GROUP * 2 * rows
    out_lane = lax.broadcasted_iota(jnp.int32, (rows, 128), 1)
    own_all = jnp.zeros((rows, 128), f32)
    sent_all = jnp.zeros((rows, 128), f32)
    for g in range(heads // GROUP):
        here = slice(g * block, (g + 1) * block)
        s = scores_of(qaug[here], keys, bias)
        m1 = stats[here, :128]
        m = jnp.maximum(m1, jnp.max(s, axis=-1, keepdims=True))
        factor = jnp.exp2((m1 - m) * c)
        p = jnp.exp2((s - tiled(m, s)) * c)
        total = stats[here, 128:] * factor + jnp.sum(p, axis=-1, keepdims=True)
        fresh = nn(p.astype(bf16), keys[:, :LATENT])
        inverse = 1.0 / total
        mixed = acc[here] * tiled(factor * inverse, fresh) + fresh * tiled(inverse, fresh)
        mixed = mixed.astype(bf16)
        lse = m * c + jnp.log2(total)
        for j in range(GROUP):
            h = g * GROUP + j
            at = h * NOPE
            base = j * 2 * rows
            o = nn(mixed[base : base + 2 * rows], wuv[:, at : at + NOPE])
            own[:, at : at + NOPE] = o[:rows]
            message[:, at : at + NOPE] = o[rows:].astype(bf16)
            own_all = jnp.where(out_lane == h, lse[base : base + rows], own_all)
            rest = lse[base + rows : base + 2 * rows]
            for term in range(3):
                part = rest.astype(bf16).astype(f32)
                sent_all = jnp.where(out_lane == term * heads + h, part, sent_all)
                rest = rest - part
    own_lse[...] = own_all
    message[:, wide : wide + 128] = sent_all.astype(bf16)


VMEM = pl.BlockSpec(memory_space=pltpu.VMEM)
SMEM = pl.BlockSpec(memory_space=pltpu.SMEM)
ANY = pl.BlockSpec(memory_space=pl.ANY)


def params(mib):
    return pltpu.CompilerParams(vmem_limit_bytes=mib * MIB)


def held_in_vmem(*arrays):
    return tuple(pltpu.with_memory_space_constraint(x, pltpu.VMEM) for x in arrays)


def in_hbm(*arrays):
    return tuple(pltpu.with_memory_space_constraint(x, pltpu.HBM) for x in arrays)


def cost(flops, exps=0):
    return pl.CostEstimate(flops=flops, transcendentals=exps, bytes_accessed=4 * MIB)


def attention_first(starts, q0, q1, wuk, pieces, slots, half, earlier):
    rows = q0.shape[0]
    heads = wuk.shape[1] // NOPE
    height = heads * 2 * rows
    count = 2 * rows * len(slots)
    return pl.pallas_call(
        functools.partial(first_kernel, rows, heads, half, slots),
        out_shape=(
            pltpu.VMEM((height, LATENT + 2 * ROPE), bf16),
            pltpu.VMEM((height, LATENT), f32),
            pltpu.VMEM((height, 256), f32),
        ),
        in_specs=[SMEM] + [VMEM] * (3 + len(pieces)) + [ANY],
        out_specs=(VMEM, VMEM, VMEM),
        scratch_shapes=[
            pltpu.VMEM((count, LATENT + 2 * ROPE), bf16),
            pltpu.VMEM((2 * rows, count), f32),
        ],
        compiler_params=params(16),
        cost_estimate=cost(2 * height * count * (2 * LATENT + 2 * ROPE), height * count),
    )(starts, *held_in_vmem(q0, q1, wuk, *pieces, earlier))


def attention_second(starts, state, wuv, pieces, slots, half, earlier):
    heads = wuv.shape[1] // NOPE
    height = state[0].shape[0]
    rows = height // heads // 2
    count = 2 * rows * len(slots)
    wide = heads * NOPE
    return pl.pallas_call(
        functools.partial(second_kernel, rows, heads, half, slots),
        out_shape=(
            pltpu.VMEM((rows, wide), f32),
            pltpu.VMEM((rows, 128), f32),
            pltpu.VMEM((rows, wide + 128), bf16),
        ),
        in_specs=[SMEM] + [VMEM] * (4 + len(pieces)) + [ANY],
        out_specs=(VMEM, VMEM, VMEM),
        scratch_shapes=[
            pltpu.VMEM((count, LATENT + 2 * ROPE), bf16),
            pltpu.VMEM((2 * rows, count), f32),
        ],
        compiler_params=params(16),
        cost_estimate=cost(2 * height * count * (2 * LATENT + 2 * ROPE), height * count),
    )(starts, *held_in_vmem(*state, wuv, *pieces, earlier))


def combine_kernel(rows, heads, half, part, starts, lens, own, lse, got, *refs):
    out = refs[-1 - 2 * part]
    if part:
        weights, (copied, sem) = refs[-4], refs[-2:]
        moving = pltpu.make_async_copy(weights, copied, sem)
        moving.start()
    core = lax.axis_index("core")
    live = lens[core] - starts[core]
    base = lax.axis_index("yl") * half + lax.axis_index("z") * rows
    wide = heads * NOPE
    alive = base + lax.broadcasted_iota(jnp.int32, (rows, 1), 0) < live
    terms = got[:, wide : wide + 128].astype(f32)
    for h in range(heads):
        at = h * NOPE
        there = (
            terms[:, h : h + 1]
            + terms[:, heads + h : heads + h + 1]
            + terms[:, 2 * heads + h : 2 * heads + h + 1]
        )
        w = 1.0 / (1.0 + jnp.exp2(there - lse[:, h : h + 1]))
        o = own[:, at : at + NOPE] * w + got[:, at : at + NOPE].astype(f32) * (1.0 - w)
        at = part * wide + h * NOPE
        out[:, at : at + NOPE] = jnp.where(alive, o, 0.0).astype(bf16)
    if part:
        moving.wait()


def combine_first(starts, lens, own, lse, got, half, earlier):
    rows, wide = own.shape
    return pl.pallas_call(
        functools.partial(combine_kernel, rows, wide // NOPE, half, 0),
        out_shape=pltpu.VMEM((rows, 2 * wide), bf16),
        in_specs=[SMEM, SMEM] + [VMEM] * 3 + [ANY],
        out_specs=VMEM,
        compiler_params=params(2),
        cost_estimate=cost(8 * rows * wide),
    )(starts, lens, *held_in_vmem(own, lse, got, earlier))


def combine_second(starts, lens, own, lse, got, half, before, weights):
    rows, wide = own.shape
    return pl.pallas_call(
        functools.partial(combine_kernel, rows, wide // NOPE, half, 1),
        out_shape=(
            pltpu.VMEM((rows, 2 * wide), bf16),
            pltpu.VMEM(weights.shape, weights.dtype),
        ),
        in_specs=[SMEM, SMEM] + [VMEM] * 4 + [ANY],
        out_specs=(VMEM, ANY),
        scratch_shapes=[pltpu.SemaphoreType.DMA(())],
        input_output_aliases={5: 0},
        compiler_params=params(2),
        cost_estimate=cost(8 * rows * wide),
    )(starts, lens, *held_in_vmem(own, lse, got, before), weights)


NEAR = (0, 1, 2, 7, 6)
FAR = (3, 5, 4)


def products(pieces, weights, held):
    w00, w01, w10, w11 = weights
    depth = w00.shape[1]
    place = 0
    for piece in pieces:
        held[place : place + piece.shape[0], :] = piece[...]
        place += piece.shape[0]
    left = held[:, :depth]
    right = held[:, depth:]
    mine = nt(left, w00[...]) + nt(right, w10[...])
    other = nt(left, w01[...]) + nt(right, w11[...])
    swapped = lax.axis_index("yh") != lax.axis_index("yl")
    return jnp.concatenate(
        [jnp.where(swapped, other, mine), jnp.where(swapped, mine, other)], axis=1
    ).astype(bf16)


def near_kernel(*refs):
    count = len(NEAR)
    out, held = refs[-2:]
    out[...] = products(refs[:count], refs[count : count + 4], held)


def far_kernel(rows, *refs):
    near = refs[8]
    outs = refs[9:17]
    held, full = refs[17:]
    both = products(refs[:4], refs[4:8], held)
    for place, slot in enumerate(FAR):
        full[slot * rows : (slot + 1) * rows, :] = both[place * rows : (place + 1) * rows]
    for place, slot in enumerate(NEAR):
        full[slot * rows : (slot + 1) * rows, :] = near[place * rows : (place + 1) * rows, :]
    z, core, x = (lax.axis_index(name) for name in ("z", "core", "x"))
    odd = x & 1
    partners = (x, x + 1 - 2 * odd, (x - 1 + 2 * odd) & 3, (x + 2) & 3)
    for k, out in enumerate(outs):
        to_x, to_core = partners[k // 2], (core if k % 2 == 0 else 1 - core)
        slot = (z - 2 * to_x - to_core) & 7
        out[...] = full[pl.ds(pl.multiple_of(slot * rows, rows), rows), :]


def project_near(pieces, weights):
    rows, wide = pieces[0].shape
    cols = weights[0].shape[0]
    count = len(NEAR)
    return pl.pallas_call(
        near_kernel,
        out_shape=pltpu.VMEM((count * rows, 2 * cols), bf16),
        in_specs=[VMEM] * (count + 4),
        out_specs=VMEM,
        scratch_shapes=[pltpu.VMEM((count * rows, wide), bf16)],
        compiler_params=params(12),
        cost_estimate=cost(4 * count * rows * wide * cols),
    )(*held_in_vmem(*pieces, *weights))


def project_far(pieces, weights, near):
    rows, wide = pieces[0].shape
    cols = weights[0].shape[0]
    count = len(FAR)
    return pl.pallas_call(
        functools.partial(far_kernel, rows),
        out_shape=(pltpu.VMEM((rows, 2 * cols), bf16),) * 8,
        in_specs=[VMEM] * 9,
        out_specs=(VMEM,) * 8,
        scratch_shapes=[
            pltpu.VMEM((count * rows, wide), bf16),
            pltpu.VMEM((8 * rows, 2 * cols), bf16),
        ],
        compiler_params=params(12),
        cost_estimate=cost(4 * count * rows * wide * cols),
    )(*held_in_vmem(*pieces, *weights, near))


def level_kernel(*refs):
    pass


def level(arrays, earlier=()):
    count = len(arrays)
    return pl.pallas_call(
        level_kernel,
        out_shape=tuple(pltpu.VMEM(x.shape, x.dtype) for x in arrays),
        in_specs=[ANY] * (count + len(earlier)),
        out_specs=(ANY,) * count,
        input_output_aliases={i: i for i in range(count)},
        compiler_params=params(1),
    )(*held_in_vmem(*arrays, *earlier))


def swap(x, axis):
    return lax.ppermute(x, axis, [(0, 1), (1, 0)])


UP = [(i, (i + 1) % 8) for i in range(8)]
DOWN = [(i, (i - 1) % 8) for i in range(8)]


def step(a, b):
    return lax.ppermute(a, "z", UP), lax.ppermute(b, "z", DOWN)


def last(a, b):
    cut = a.shape[0] // 2
    return step(a[:cut], b[cut:])


X_PAIRS = ((1, 0, 3, 2), (3, 2, 1, 0), (2, 3, 0, 1))


def to_partner(x, pairs, flip):
    moves = [(2 * i + c, 2 * j + (c ^ flip)) for i, j in enumerate(pairs) for c in range(2)]
    return lax.ppermute(x, ("x", "core"), moves)


def pack_kernel(q_nope, q_rope, cache, stretch, latent, q_own, q_sent, sems):
    core = lax.axis_index("core")
    rows, wide = q_nope.shape[1:]
    moves = [
        (cache.at[core], latent.at[:rows, :]),
        (stretch.at[core], latent.at[rows:, :]),
        (q_nope.at[core], q_own.at[:, :wide]),
        (q_rope.at[core], q_own.at[:, wide:]),
        (q_nope.at[1 - core], q_sent.at[:, :wide]),
        (q_rope.at[1 - core], q_sent.at[:, wide:]),
    ]
    copies = [pltpu.make_async_copy(a, b, sems.at[i]) for i, (a, b) in enumerate(moves)]
    for copy in copies:
        copy.start()
    for copy in copies:
        copy.wait()


def pack(q_nope, q_rope, cache, stretch):
    rows, width = cache.shape[1:]
    wide = q_nope.shape[2] + q_rope.shape[2]
    return pl.pallas_call(
        pack_kernel,
        out_shape=(
            pltpu.VMEM((2 * rows, width), bf16),
            pltpu.VMEM((rows, wide), bf16),
            pltpu.VMEM((rows, wide), bf16),
        ),
        in_specs=[ANY] * 4,
        out_specs=(ANY,) * 3,
        scratch_shapes=[pltpu.SemaphoreType.DMA((6,))],
        compiler_params=params(1),
    )(*in_hbm(q_nope, q_rope, cache, stretch))


def sum_kernel(*refs):
    parts, (first, second) = refs[:8], refs[8:]
    core = lax.axis_index("core")
    cols = first.shape[2]
    for k in range(2):
        total = parts[4 * k][...].astype(f32)
        for part in parts[4 * k + 1 : 4 * k + 4]:
            total += part[...].astype(f32)
        total = total.astype(bf16)
        to = core if k == 0 else 1 - core
        first[to] = total[:, :cols]
        second[to] = total[:, cols:]


def sums(own_seq, other_seq):
    rows, cols = own_seq[0].shape
    out = pltpu.VMEM((2, rows, cols // 2), bf16)
    return pl.pallas_call(
        sum_kernel,
        out_shape=(out, out),
        in_specs=[VMEM] * 8,
        out_specs=(VMEM, VMEM),
        compiler_params=params(4),
    )(*held_in_vmem(*own_seq, *other_seq))


def local(q_nope, q_rope, cache_latent, stretch_latent, w_uk, w_uv, w_o, stretch_start, prompt_len):
    half = 8 * q_nope.shape[1]
    latent, q_own, q_sent = pack(q_nope, q_rope, cache_latent, stretch_latent)
    q_own_y = swap(q_own, "yl")
    q_got = swap(q_sent, "core")
    u1, d1, q_got = level((*step(latent, latent), q_got))
    u2, d2, q_got = level((*step(u1, d1), q_got))
    q_got_y = swap(q_got, "yl")
    w_uk2 = swap(w_uk, "core")
    w_uv2 = swap(w_uv, "core")
    near = [latent, u1, u2, d1]
    near_at, far_at = (0, 1, 2, 7), (6, 3, 5, 4)
    a1 = attention_first(stretch_start, q_own, q_own_y, w_uk, near, near_at, half, u1)
    u3, d3 = level(step(u2, d2), (q_got_y, w_uk2, w_uv2, a1[2]))
    b1 = attention_first(stretch_start, q_got, q_got_y, w_uk2, near, near_at, half, u3)
    far = [d2, u3, d3, *last(u3, d3)]
    a2 = attention_second(stretch_start, a1, w_uv, far, far_at, half, b1[2])
    got_a = swap(a2[2], "yl")
    b2 = attention_second(stretch_start, b1, w_uv2, far, far_at, half, a2[1])
    got_b = swap(b2[2], "yl")
    known = (stretch_start, prompt_len)
    attention = combine_first(*known, *a2[:2], got_a, half, b2[1])
    attention, w_t = combine_second(*known, *b2[:2], got_b, half, attention, w_o.T)

    u1, d1 = level(step(attention, attention))
    w_t_c = swap(w_t, "core")
    w_t_y = swap(w_t, "yl")
    u2, d2 = level(step(u1, d1), (w_t_c,))
    u3, d3, w_t_y = level((*step(u2, d2), w_t_y))
    w_t_cy = swap(w_t_y, "core")
    weights = (w_t, w_t_y, w_t_c, w_t_cy)
    near = project_near([attention, u1, u2, d1, d2], weights)
    parts = project_far([u3, d3, *last(u3, d3)], weights, near)

    other_seq = [swap(parts[1], "core")]
    other_seq += [to_partner(parts[2 * k + 3], X_PAIRS[k], 1) for k in range(3)]
    own_seq = [parts[0]] + [to_partner(parts[2 * k + 2], X_PAIRS[k], 0) for k in range(3)]
    first, second = sums(own_seq, other_seq)
    first = lax.ppermute(first, ("yl", "yh"), [(0, 0), (1, 2), (2, 1), (3, 3)])
    second = lax.ppermute(second, ("yl", "yh"), [(0, 2), (2, 3), (1, 0), (3, 1)])
    return (first.astype(f32) + second.astype(f32)).astype(bf16)


def solution(mesh):
    fine = Mesh(mesh.devices.reshape(2, 8, 2, 4, 2), ("yl", "z", "yh", "x", "core"))
    ctx = ("yl", "z")
    head = ("yh", "x", "core")
    placed = (
        P(None, ctx, head),
        P(None, ctx, head),
        P(None, ctx, None),
        P(None, ctx, None),
        P(None, head),
        P(None, head),
        P(head, ctx),
        P(),
        P(),
    )
    return jax.shard_map(
        local, mesh=fine, in_specs=placed, out_specs=P(None, head, ctx), check_vma=False
    )
```

time: 121 us -> 111 us (0.917)
  blocking collectives: 18.7 us -> 0 us
  starting transfers between devices: 37 us -> 45.1 us
  Pallas kernels: 15.9 us -> 17.5 us
    all_to_all x1 -> x0, blocking collectives: 18.7 us -> none  [local(): parts = lax.all_to_all(partial, ('x', 'core'), 0, 0, tiled=True)]
    ppermute x2 -> x8, starting transfers between devices: 3.57 us -> 11.9 us  [the longest x6 7.52 us: to_partner(): return lax.ppermute(x, ('x', 'core'), moves)]
    ppermute x2 -> x8, waiting for transfers between devices: 4.95 us -> 12.9 us  [the longest x6 7.98 us: to_partner(): return lax.ppermute(x, ('x', 'core'), moves)]
    ppermute x10 -> x11, waiting for transfers between devices: 8.69 us -> 4.2 us  [swap(): return lax.ppermute(x, axis, [(0, 1), (1, 0)])]
    ppermute x16, waiting for transfers between devices: 32.2 us -> 27.9 us  [step(): return (lax.ppermute(a, 'z', UP), lax.ppermute(b, 'z', DOWN))]
    pallas_call x5 -> x10, Pallas kernels: 15.9 us -> 17.5 us  [the longest x2 6.09 us: attention_second(): pl.pallas_call(functools.partial(second_kernel, rows, heads, half, slots)...]
    ppermute x10 -> x11, starting transfers between devices: 5.37 us -> 4.36 us  [swap(): return lax.ppermute(x, axis, [(0, 1), (1, 0)])]
  transfers between devices with their start and end apart: 28 -> 35, of which waited for: 17 -> 19; matrix products, arithmetic and copies ran while one was open for 0% -> 0% of each run, Pallas kernels for 2% -> 11%
where the time goes in v3:
time: 111 us; the launch traced here: 110 us
  starting transfers between devices  45.1 us (41%)
  waiting for transfers between devices  45 us (41%)
  Pallas kernels  17.5 us (16%)
  local copies, waits for them, and re-layouts  1.93 us (2%)
    ppermute x16, starting transfers between devices, step(): return (lax.ppermute(a, 'z', UP), lax.ppermute(b, 'z', DOWN))  28.9 us
    ppermute x16, waiting for transfers between devices, step(): return (lax.ppermute(a, 'z', UP), lax.ppermute(b, 'z', DOWN))  27.9 us
    ppermute x6, waiting for transfers between devices, to_partner(): return lax.ppermute(x, ('x', 'core'), moves)  7.98 us
    ppermute x6, starting transfers between devices, to_partner(): return lax.ppermute(x, ('x', 'core'), moves)  7.52 us
    pallas_call x2, Pallas kernels, attention_second(): pl.pallas_call(functools.partial(second_kernel, rows, heads, half, slots)...  6.09 us
    pallas_call x2, Pallas kernels, attention_first(): pl.pallas_call(functools.partial(first_kernel, rows, heads, half, slots),...  5.15 us
    ppermute x11, starting transfers between devices, swap(): return lax.ppermute(x, axis, [(0, 1), (1, 0)])  4.36 us
    ppermute x1, starting transfers between devices, local(): first = lax.ppermute(first, ('yl', 'yh'), [(0, 0), (1, 2), (2, 1), (3, 3)])  4.27 us
  transfers between devices with their start and end apart: 35, of which 19 were waited for; matrix products, arithmetic and copies ran while one was open for 0% of the time, Pallas kernels for 11%

profile of v3, /device:TPU:8, one launch (start us, length us, event | category | flops | bytes accessed | tf_op | source)
XLA Modules:
  0.0 110.5 jit_solution(203223600373535461)
XLA Ops:
  0.0 0.5 collective-permute-start.9
  0.5 1.1 %shard_map.91 = (bf16[128,576]{1,0:T(8,128)(2,1)S(1)}, bf16[64,1536]{1,0:T(8,128)(2,1)S(1)}, bf16[64,1536]{1,0:T(8,128)(2,1)S(1)}) custom-call(bf16[2,64,1024]{2,1,0:T(8,128)(2,1)} %q_nope.1, bf16[2,64,512]{2,1,0:T(8,128)(2,1)} %q_rope.1, bf16[2,64,576]{2,1,0:T(8,128)(2,1)} %cache.1, bf16[2,64,576]{2,1,0:T(8,128)(2,1)} %stretch.1), custom_call_target="tpu_custom_call" | custom-call | tf_op jit(solution)/shard_map/pallas_call | solution.py:408
  1.6 0.1 collective-permute-start.2
  1.7 2.0 %collective-permute-start = (bf16[128,576]{1,0:T(8,128)(2,1)S(1)}, bf16[128,576]{1,0:T(8,128)(2,1)S(1)}, u32[]{:S(2)}, u32[]{:S(2)}) collective-permute-start(bf16[128,576]{1,0:T(8,128)(2,1)S(1)} %get-tuple-element.47.refs_4_), channel_id=1, source_target_pairs={{0,16},{16,32},{32,48},{48,64},{64,80},{80,96},{96,112},{112,0},{1... | collective-permute-start | bytes 442376 | tf_op jit(solution)/shard_map/ppermute | solution.py:371
  3.7 4.0 %collective-permute-start.1 = (bf16[128,576]{1,0:T(8,128)(2,1)S(1)}, bf16[128,576]{1,0:T(8,128)(2,1)S(1)}, u32[]{:S(2)}, u32[]{:S(2)}) collective-permute-start(bf16[128,576]{1,0:T(8,128)(2,1)S(1)} %get-tuple-element.47.refs_4_), channel_id=1, source_target_pairs={{0,112},{16,0},{32,16},{48,32},{64,48},{80,64},{96,80},{112,96},{1... | collective-permute-start | bytes 442376 | tf_op jit(solution)/shard_map/ppermute | solution.py:371
  7.8 4.7 %collective-permute-done.refs_0_ = bf16[128,576]{1,0:T(8,128)(2,1)S(1)} collective-permute-done((bf16[128,576]{1,0:T(8,128)(2,1)S(1)}, bf16[128,576]{1,0:T(8,128)(2,1)S(1)}, u32[]{:S(2)}, u32[]{:S(2)}) %collective-permute-start) | collective-permute-done | bytes 147488 | tf_op jit(solution)/shard_map/ppermute | solution.py:371
  12.5 0.1 collective-permute-start.3
  12.6 3.2 %collective-permute-start.4 = (bf16[128,576]{1,0:T(8,128)(2,1)S(1)}, bf16[128,576]{1,0:T(8,128)(2,1)S(1)}, u32[]{:S(2)}, u32[]{:S(2)}) collective-permute-start(bf16[128,576]{1,0:T(8,128)(2,1)S(1)} %get-tuple-element.50.refs_7_), channel_id=1, source_target_pairs={{0,112},{16,0},{32,16},{48,32},{64,48},{80,64},{96,80},{112,96},{1... | collective-permute-start | bytes 442376 | tf_op jit(solution)/shard_map/ppermute | solution.py:371
  15.8 0.4 collective-permute-start.10
  16.2 3.5 %collective-permute-done.3.refs_0_ = bf16[128,576]{1,0:T(8,128)(2,1)S(1)} collective-permute-done((bf16[128,576]{1,0:T(8,128)(2,1)S(1)}, bf16[128,576]{1,0:T(8,128)(2,1)S(1)}, u32[]{:S(2)}, u32[]{:S(2)}) %collective-permute-start.3) | collective-permute-done | bytes 147488 | tf_op jit(solution)/shard_map/ppermute | solution.py:371
  19.7 0.5 collective-permute-start.5
  20.2 1.9 %collective-permute-start.7 = (bf16[128,576]{1,0:T(8,128)(2,1)S(1)}, bf16[128,576]{1,0:T(8,128)(2,1)S(1)}, u32[]{:S(2)}, u32[]{:S(2)}) collective-permute-start(bf16[128,576]{1,0:T(8,128)(2,1)S(1)} %get-tuple-element.53.refs_6_), channel_id=1, source_target_pairs={{0,16},{16,32},{32,48},{48,64},{64,80},{80,96},{96,112},{112,0},{1... | collective-permute-start | bytes 442376 | tf_op jit(solution)/shard_map/ppermute | solution.py:371
  22.0 0.4 collective-permute-done.10.refs_2_
  22.4 1.0 collective-permute-start.8
  23.4 0.7 copy-done.2
  24.1 1.2 %copy-done.4 = bf16[512,1024]{1,0:T(8,128)(2,1)S(1)} copy-done((bf16[512,1024]{1,0:T(8,128)(2,1)S(1)}, bf16[512,1024]{1,0:T(8,128)(2,1)}, u32[]{:S(2)}) %copy-start.4) | copy-done | bytes 1048600
  25.3 2.6 %shard_map.94 = (bf16[1024,640]{1,0:T(8,128)(2,1)S(1)}, f32[1024,512]{1,0:T(8,128)S(1)}, f32[1024,256]{1,0:T(8,128)S(1)}) custom-call(s32[2]{0:T(128)S(1)} %copy-done.2, bf16[64,1536]{1,0:T(8,128)(2,1)S(1)} %get-tuple-element.55.refs_1_, bf16[64,1536]{1,0:T(8,128)(2,1)S(1)} %collective-permute-done.10.refs_2_, bf16[512,1024]{1,0:T(8,128)(2,1)S(1)} %copy-done.4, ...), custom_call_target="tpu_custom_call" | custom-call | flops 1207959552 | bytes 4194304 | tf_op jit(solution)/shard_map/pallas_call | solution.py:170
  27.9 1.5 %collective-permute-start.11 = (bf16[64,576]{1,0:T(8,128)(2,1)S(1)}, bf16[64,576]{1,0:T(8,128)(2,1)S(1)}, u32[]{:S(2)}, u32[]{:S(2)}) collective-permute-start(bf16[64,576]{1,0:T(8,128)(2,1)S(1)} %slice.12), channel_id=1, source_target_pairs={{0,16},{16,32},{32,48},{48,64},{64,80},{80,96},{96,112},{112,0},{1... | collective-permute-start | bytes 221192 | tf_op jit(solution)/shard_map/ppermute | solution.py:371
  29.4 0.0 copy-start
  29.4 2.1 %collective-permute-start.12 = (bf16[64,576]{1,0:T(8,128)(2,1)S(1)}, bf16[64,576]{1,0:T(8,128)(2,1)S(1)}, u32[]{:S(2)}, u32[]{:S(2)}) collective-permute-start(bf16[64,576]{1,0:T(8,128)(2,1)S(1)} %slice.13), channel_id=1, source_target_pairs={{0,112},{16,0},{32,16},{48,32},{64,48},{80,64},{96,80},{112,96},{1... | collective-permute-start | bytes 221192 | tf_op jit(solution)/shard_map/ppermute | solution.py:371
  31.5 2.6 %shard_map.96 = (bf16[1024,640]{1,0:T(8,128)(2,1)S(1)}, f32[1024,512]{1,0:T(8,128)S(1)}, f32[1024,256]{1,0:T(8,128)S(1)}) custom-call(s32[2]{0:T(128)S(1)} %copy-done.2, bf16[64,1536]{1,0:T(8,128)(2,1)S(1)} %get-tuple-element.52.refs_1_, bf16[64,1536]{1,0:T(8,128)(2,1)S(1)} %collective-permute-done.5.refs_2_, ...), custom_call_target="tpu_custom_call" | custom-call | flops 1207959552 | bytes 4194304 | tf_op jit(solution)/shard_map/pallas_call | solution.py:170
  34.1 3.1 %shard_map.97 = (f32[64,1024]{1,0:T(8,128)S(1)}, f32[64,128]{1,0:T(8,128)S(1)}, bf16[64,1152]{1,0:T(8,128)(2,1)S(1)}) custom-call(s32[2]{0:T(128)S(1)} %copy-done.2, bf16[1024,640]{1,0:T(8,128)(2,1)S(1)} %get-tuple-element.62.refs_1_, f32[1024,512]{1,0:T(8,128)S(1)} %get-tuple-element.63.refs_2_, f32[1024,256]{1,0:T(8,128)S(1)} %get-tuple-element.56.refs_5_.refs_3_, ...), custom_call_target="tpu_custom_call" | custom-call | flops 1207959552 | bytes 4194304 | tf_op jit(solution)/shard_map/pallas_call | solution.py:194
  37.2 1.7 %collective-permute-start.14 = (bf16[64,1152]{1,0:T(8,128)(2,1)S(1)}, bf16[64,1152]{1,0:T(8,128)(2,1)S(1)}, u32[]{:S(2)}, u32[]{:S(2)}) collective-permute-start(bf16[64,1152]{1,0:T(8,128)(2,1)S(1)} %get-tuple-element.69), channel_id=1, source_target_pairs={{0,128},{128,0},{1,129},{129,1},{2,130},{130,2},{3,131},{131,3},{4... | collective-permute-start | bytes 442376 | tf_op jit(solution)/shard_map/ppermute | solution.py:363
  38.9 3.0 %shard_map.98 = (f32[64,1024]{1,0:T(8,128)S(1)}, f32[64,128]{1,0:T(8,128)S(1)}, bf16[64,1152]{1,0:T(8,128)(2,1)S(1)}) custom-call(s32[2]{0:T(128)S(1)} %copy-done.2, bf16[1024,640]{1,0:T(8,128)(2,1)S(1)} %get-tuple-element.58.refs_1_, f32[1024,512]{1,0:T(8,128)S(1)} %get-tuple-element.59.refs_2_, f32[1024,256]{1,0:T(8,128)S(1)} %get-tuple-element.60.refs_10_.refs_3_, ...), custom_call_target="tpu_custom_call" | custom-call | flops 1207959552 | bytes 4194304 | tf_op jit(solution)/shard_map/pallas_call | solution.py:194
  41.9 0.6 collective-permute-start.13
  42.5 0.5 collective-permute-done.14.got
  43.0 0.8 shard_map.99.refs_0_
  43.9 3.3 %collective-permute-done.13.got = bf16[64,1152]{1,0:T(8,128)(2,1)S(1)} collective-permute-done((bf16[64,1152]{1,0:T(8,128)(2,1)S(1)}, bf16[64,1152]{1,0:T(8,128)(2,1)S(1)}, u32[]{:S(2)}, u32[]{:S(2)}) %collective-permute-start.13) | collective-permute-done | bytes 147488 | tf_op jit(solution)/shard_map/ppermute | solution.py:363
  47.1 1.1 shard_map.100
  48.2 0.1 collective-permute-start.19
  48.3 0.6 collective-permute-start.22
  48.9 1.7 %collective-permute-start.15 = (bf16[64,2048]{1,0:T(8,128)(2,1)S(1)}, bf16[64,2048]{1,0:T(8,128)(2,1)S(1)}, u32[]{:S(2)}, u32[]{:S(2)}) collective-permute-start(bf16[64,2048]{1,0:T(8,128)(2,1)S(1)} %get-tuple-element.70.refs_0_), channel_id=1, source_target_pairs={{0,16},{16,32},{32,48},{48,64},{64,80},{80,96},{96,112},{112,0},{1... | collective-permute-start | bytes 786440 | tf_op jit(solution)/shard_map/ppermute | solution.py:371
  50.6 1.6 %collective-permute-start.16 = (bf16[64,2048]{1,0:T(8,128)(2,1)S(1)}, bf16[64,2048]{1,0:T(8,128)(2,1)S(1)}, u32[]{:S(2)}, u32[]{:S(2)}) collective-permute-start(bf16[64,2048]{1,0:T(8,128)(2,1)S(1)} %get-tuple-element.70.refs_0_), channel_id=1, source_target_pairs={{0,112},{16,0},{32,16},{48,32},{64,48},{80,64},{96,80},{112,96},{1... | collective-permute-start | bytes 786440 | tf_op jit(solution)/shard_map/ppermute | solution.py:371
  52.1 6.4 %collective-permute-done.15.refs_0_ = bf16[64,2048]{1,0:T(8,128)(2,1)S(1)} collective-permute-done((bf16[64,2048]{1,0:T(8,128)(2,1)S(1)}, bf16[64,2048]{1,0:T(8,128)(2,1)S(1)}, u32[]{:S(2)}, u32[]{:S(2)}) %collective-permute-start.15) | collective-permute-done | bytes 262176 | tf_op jit(solution)/shard_map/ppermute | solution.py:371
  58.5 0.1 collective-permute-done.16.refs_1_
  58.6 2.2 %collective-permute-start.17 = (bf16[64,2048]{1,0:T(8,128)(2,1)S(1)}, bf16[64,2048]{1,0:T(8,128)(2,1)S(1)}, u32[]{:S(2)}, u32[]{:S(2)}) collective-permute-start(bf16[64,2048]{1,0:T(8,128)(2,1)S(1)} %get-tuple-element.71.refs_1_), channel_id=1, source_target_pairs={{0,16},{16,32},{32,48},{48,64},{64,80},{80,96},{96,112},{112,0},{1... | collective-permute-start | bytes 786440 | tf_op jit(solution)/shard_map/ppermute | solution.py:371
  60.9 1.0 collective-permute-start.18
  61.9 5.5 %collective-permute-done.17.refs_0_ = bf16[64,2048]{1,0:T(8,128)(2,1)S(1)} collective-permute-done((bf16[64,2048]{1,0:T(8,128)(2,1)S(1)}, bf16[64,2048]{1,0:T(8,128)(2,1)S(1)}, u32[]{:S(2)}, u32[]{:S(2)}) %collective-permute-start.17) | collective-permute-done | bytes 262176 | tf_op jit(solution)/shard_map/ppermute | solution.py:371
  67.4 0.8 collective-permute-done.18.refs_1_
  68.1 1.4 %collective-permute-start.20 = (bf16[64,2048]{1,0:T(8,128)(2,1)S(1)}, bf16[64,2048]{1,0:T(8,128)(2,1)S(1)}, u32[]{:S(2)}, u32[]{:S(2)}) collective-permute-start(bf16[64,2048]{1,0:T(8,128)(2,1)S(1)} %get-tuple-element.74.refs_2_), channel_id=1, source_target_pairs={{0,16},{16,32},{32,48},{48,64},{64,80},{80,96},{96,112},{112,0},{1... | collective-permute-start | bytes 786440 | tf_op jit(solution)/shard_map/ppermute | solution.py:371
  69.5 1.8 %collective-permute-start.21 = (bf16[64,2048]{1,0:T(8,128)(2,1)S(1)}, bf16[64,2048]{1,0:T(8,128)(2,1)S(1)}, u32[]{:S(2)}, u32[]{:S(2)}) collective-permute-start(bf16[64,2048]{1,0:T(8,128)(2,1)S(1)} %get-tuple-element.75.refs_4_), channel_id=1, source_target_pairs={{0,112},{16,0},{32,16},{48,32},{64,48},{80,64},{96,80},{112,96},{1... | collective-permute-start | bytes 786440 | tf_op jit(solution)/shard_map/ppermute | solution.py:371
  71.4 4.3 %collective-permute-done.20.refs_0_ = bf16[64,2048]{1,0:T(8,128)(2,1)S(1)} collective-permute-done((bf16[64,2048]{1,0:T(8,128)(2,1)S(1)}, bf16[64,2048]{1,0:T(8,128)(2,1)S(1)}, u32[]{:S(2)}, u32[]{:S(2)}) %collective-permute-start.20) | collective-permute-done | bytes 262176 | tf_op jit(solution)/shard_map/ppermute | solution.py:371
  75.7 0.2 collective-permute-done.21.refs_1_
  75.9 1.7 %collective-permute-start.23 = (bf16[32,2048]{1,0:T(8,128)(2,1)S(1)}, bf16[32,2048]{1,0:T(8,128)(2,1)S(1)}, u32[]{:S(2)}, u32[]{:S(2)}) collective-permute-start(bf16[32,2048]{1,0:T(8,128)(2,1)S(1)} %slice.14), channel_id=1, source_target_pairs={{0,16},{16,32},{32,48},{48,64},{64,80},{80,96},{96,112},{112,0},{1... | collective-permute-start | bytes 393224 | tf_op jit(solution)/shard_map/ppermute | solution.py:371
  77.6 1.7 %collective-permute-start.24 = (bf16[32,2048]{1,0:T(8,128)(2,1)S(1)}, bf16[32,2048]{1,0:T(8,128)(2,1)S(1)}, u32[]{:S(2)}, u32[]{:S(2)}) collective-permute-start(bf16[32,2048]{1,0:T(8,128)(2,1)S(1)} %slice.15), channel_id=1, source_target_pairs={{0,112},{16,0},{32,16},{48,32},{64,48},{80,64},{96,80},{112,96},{1... | collective-permute-start | bytes 393224 | tf_op jit(solution)/shard_map/ppermute | solution.py:371
  79.3 1.6 %shard_map.104.refs_8_ = bf16[320,896]{1,0:T(8,128)(2,1)S(1)} custom-call(bf16[64,2048]{1,0:T(8,128)(2,1)S(1)} %get-tuple-element.70.refs_0_, bf16[64,2048]{1,0:T(8,128)(2,1)S(1)} %get-tuple-element.71.refs_1_, bf16[64,2048]{1,0:T(8,128)(2,1)S(1)} %get-tuple-element.74.refs_2_, bf16[64,2048]{1,0:T(8,128)(2,1)S(1)} %get-tuple-element.72.refs_3_, ...), custom_call_target="tpu_custom_call" | custom-call | flops 1174405120 | bytes 4194304 | tf_op jit(solution)/shard_map/pallas_call | solution.py:317
  81.0 2.2 %collective-permute-done.23.refs_2_ = bf16[32,2048]{1,0:T(8,128)(2,1)S(1)} collective-permute-done((bf16[32,2048]{1,0:T(8,128)(2,1)S(1)}, bf16[32,2048]{1,0:T(8,128)(2,1)S(1)}, u32[]{:S(2)}, u32[]{:S(2)}) %collective-permute-start.23) | collective-permute-done | bytes 131104 | tf_op jit(solution)/shard_map/ppermute | solution.py:371
  83.2 0.2 collective-permute-done.24.refs_3_
  83.4 1.4 %shard_map.105 = (bf16[64,896]{1,0:T(8,128)(2,1)S(1)}, bf16[64,896]{1,0:T(8,128)(2,1)S(1)}, bf16[64,896]{1,0:T(8,128)(2,1)S(1)}, bf16[64,896]{1,0:T(8,128)(2,1)S...) custom-call(bf16[64,2048]{1,0:T(8,128)(2,1)S(1)} %get-tuple-element., ...), custom_call_target="tpu_custom_call" | custom-call | flops 704643072 | bytes 4194304 | tf_op jit(solution)/shard_map/pallas_call | solution.py:332
  84.8 1.6 %collective-permute-start.26 = (bf16[64,896]{1,0:T(8,128)(2,1)S(1)}, bf16[64,896]{1,0:T(8,128)(2,1)S(1)}, u32[]{:S(2)}, u32[]{:S(2)}) collective-permute-start(bf16[64,896]{1,0:T(8,128)(2,1)S(1)} %get-tuple-element.80), channel_id=1, source_target_pairs={{0,2},{1,3},{2,0},{3,1},{4,6},{5,7},{6,4},{7,5},{8,10},{9,11},{10,... | collective-permute-start | bytes 344072 | tf_op jit(solution)/shard_map/ppermute | solution.py:384
  86.3 2.1 %collective-permute-start.27 = (bf16[64,896]{1,0:T(8,128)(2,1)S(1)}, bf16[64,896]{1,0:T(8,128)(2,1)S(1)}, u32[]{:S(2)}, u32[]{:S(2)}) collective-permute-start(bf16[64,896]{1,0:T(8,128)(2,1)S(1)} %get-tuple-element.81), channel_id=1, source_target_pairs={{0,6},{1,7},{2,4},{3,5},{4,2},{5,3},{6,0},{7,1},{8,14},{9,15},{10,... | collective-permute-start | bytes 344072 | tf_op jit(solution)/shard_map/ppermute | solution.py:384
  88.5 0.6 collective-permute-start.28
  89.1 1.5 %collective-permute-start.30 = (bf16[64,896]{1,0:T(8,128)(2,1)S(1)}, bf16[64,896]{1,0:T(8,128)(2,1)S(1)}, u32[]{:S(2)}, u32[]{:S(2)}) collective-permute-start(bf16[64,896]{1,0:T(8,128)(2,1)S(1)} %get-tuple-element.84), channel_id=1, source_target_pairs={{0,3},{1,2},{2,1},{3,0},{4,7},{5,6},{6,5},{7,4},{8,11},{9,10},{10,... | collective-permute-start | bytes 344072 | tf_op jit(solution)/shard_map/ppermute | solution.py:384
  90.6 1.7 %collective-permute-start.31 = (bf16[64,896]{1,0:T(8,128)(2,1)S(1)}, bf16[64,896]{1,0:T(8,128)(2,1)S(1)}, u32[]{:S(2)}, u32[]{:S(2)}) collective-permute-start(bf16[64,896]{1,0:T(8,128)(2,1)S(1)} %get-tuple-element.85), channel_id=1, source_target_pairs={{0,7},{1,6},{2,5},{3,4},{4,3},{5,2},{6,1},{7,0},{8,15},{9,14},{10,... | collective-permute-start | bytes 344072 | tf_op jit(solution)/shard_map/ppermute | solution.py:384
  92.3 1.6 %collective-permute-done.27.refs_2_ = bf16[64,896]{1,0:T(8,128)(2,1)S(1)} collective-permute-done((bf16[64,896]{1,0:T(8,128)(2,1)S(1)}, bf16[64,896]{1,0:T(8,128)(2,1)S(1)}, u32[]{:S(2)}, u32[]{:S(2)}) %collective-permute-start.27) | collective-permute-done | bytes 114720 | tf_op jit(solution)/shard_map/ppermute | solution.py:384
  93.9 1.5 %collective-permute-done.28.refs_3_ = bf16[64,896]{1,0:T(8,128)(2,1)S(1)} collective-permute-done((bf16[64,896]{1,0:T(8,128)(2,1)S(1)}, bf16[64,896]{1,0:T(8,128)(2,1)S(1)}, u32[]{:S(2)}, u32[]{:S(2)}) %collective-permute-start.28) | collective-permute-done | bytes 114720 | tf_op jit(solution)/shard_map/ppermute | solution.py:384
  95.5 2.0 %collective-permute-done.31.refs_6_ = bf16[64,896]{1,0:T(8,128)(2,1)S(1)} collective-permute-done((bf16[64,896]{1,0:T(8,128)(2,1)S(1)}, bf16[64,896]{1,0:T(8,128)(2,1)S(1)}, u32[]{:S(2)}, u32[]{:S(2)}) %collective-permute-start.31) | collective-permute-done | bytes 114720 | tf_op jit(solution)/shard_map/ppermute | solution.py:384
  97.5 2.8 %collective-permute-done.32.refs_7_ = bf16[64,896]{1,0:T(8,128)(2,1)S(1)} collective-permute-done((bf16[64,896]{1,0:T(8,128)(2,1)S(1)}, bf16[64,896]{1,0:T(8,128)(2,1)S(1)}, u32[]{:S(2)}, u32[]{:S(2)}) %collective-permute-start.32) | collective-permute-done | bytes 114720 | tf_op jit(solution)/shard_map/ppermute | solution.py:384
  100.3 0.2 shard_map.106
  100.5 4.3 %collective-permute-start.33 = (bf16[2,64,448]{2,1,0:T(8,128)(2,1)S(1)}, bf16[2,64,448]{2,1,0:T(8,128)(2,1)S(1)}, u32[]{:S(2)}, u32[]{:S(2)}) collective-permute-start(bf16[2,64,448]{2,1,0:T(8,128)(2,1)S(1)} %get-tuple-element.87), channel_id=1, source_target_pairs={{0,0},{8,128},{128,8},{136,136},{1,1},{9,129},{129,9},{137,137},{2... | collective-permute-start | bytes 344072 | tf_op jit(solution)/shard_map/ppermute | solution.py:486
  104.7 0.1 collective-permute-start.34
  104.8 2.8 %collective-permute-done.33 = bf16[2,64,448]{2,1,0:T(8,128)(2,1)S(1)} collective-permute-done((bf16[2,64,448]{2,1,0:T(8,128)(2,1)S(1)}, bf16[2,64,448]{2,1,0:T(8,128)(2,1)S(1)}, u32[]{:S(2)}, u32[]{:S(2)}) %collective-permute-start.33) | collective-permute-done | bytes 114720 | tf_op jit(solution)/shard_map/ppermute | solution.py:486
  107.7 2.1 %collective-permute-done.34 = bf16[2,64,448]{2,1,0:T(8,128)(2,1)S(1)} collective-permute-done((bf16[2,64,448]{2,1,0:T(8,128)(2,1)S(1)}, bf16[2,64,448]{2,1,0:T(8,128)(2,1)S(1)}, u32[]{:S(2)}, u32[]{:S(2)}) %collective-permute-start.34) | collective-permute-done | bytes 114720 | tf_op jit(solution)/shard_map/ppermute | solution.py:487
  109.8 0.7 add_convert_fusion
  (37 shorter events, 0.1 us)
Async XLA Ops:
  0.0 27.9 %collective-permute-start.6 = (bf16[512,1024]{1,0:T(8,128)(2,1)}, bf16[512,1024]{1,0:T(8,128)(2,1)S(1)}, u32[]{:S(2)}, u32[]{:S(2)}) collective-permute-start(bf16[512,1024]{1,0:T(8,128)(2,1)} %refs_3_.1), channel_id=1, source_target_pairs={{0,1},{1,0},{2,3},{3,2},{4,5},{5,4},{6,7},{7,6},{8,9},{9,8},{10,11... | collective-permute-start | bytes 3145736 | tf_op jit(solution)/shard_map/ppermute | solution.py:363
  0.0 27.9 %collective-permute-start.9 = (bf16[512,1024]{1,0:T(8,128)(2,1)}, bf16[512,1024]{1,0:T(8,128)(2,1)S(1)}, u32[]{:S(2)}, u32[]{:S(2)}) collective-permute-start(bf16[512,1024]{1,0:T(8,128)(2,1)} %refs_4_.1), channel_id=1, source_target_pairs={{0,1},{1,0},{2,3},{3,2},{4,5},{5,4},{6,7},{7,6},{8,9},{9,8},{10,11... | collective-permute-start | bytes 3145736 | tf_op jit(solution)/shard_map/ppermute | solution.py:363
  1.6 10.8 %collective-permute-start.2 = (bf16[64,1536]{1,0:T(8,128)(2,1)S(1)}, bf16[64,1536]{1,0:T(8,128)(2,1)S(1)}, u32[]{:S(2)}, u32[]{:S(2)}) collective-permute-start(bf16[64,1536]{1,0:T(8,128)(2,1)S(1)} %get-tuple-element.48), channel_id=1, source_target_pairs={{0,1},{1,0},{2,3},{3,2},{4,5},{5,4},{6,7},{7,6},{8,9},{9,8},{10,11... | collective-permute-start | bytes 589832 | tf_op jit(solution)/shard_map/ppermute | solution.py:363
  1.7 10.7 %collective-permute-start = (bf16[128,576]{1,0:T(8,128)(2,1)S(1)}, bf16[128,576]{1,0:T(8,128)(2,1)S(1)}, u32[]{:S(2)}, u32[]{:S(2)}) collective-permute-start(bf16[128,576]{1,0:T(8,128)(2,1)S(1)} %get-tuple-element.47.refs_4_), channel_id=1, source_target_pairs={{0,16},{16,32},{32,48},{48,64},{64,80},{80,96},{96,112},{112,0},{1... | collective-permute-start | bytes 442376 | tf_op jit(solution)/shard_map/ppermute | solution.py:371
  3.7 8.7 %collective-permute-start.1 = (bf16[128,576]{1,0:T(8,128)(2,1)S(1)}, bf16[128,576]{1,0:T(8,128)(2,1)S(1)}, u32[]{:S(2)}, u32[]{:S(2)}) collective-permute-start(bf16[128,576]{1,0:T(8,128)(2,1)S(1)} %get-tuple-element.47.refs_4_), channel_id=1, source_target_pairs={{0,112},{16,0},{32,16},{48,32},{64,48},{80,64},{96,80},{112,96},{1... | collective-permute-start | bytes 442376 | tf_op jit(solution)/shard_map/ppermute | solution.py:371
  12.5 7.2 %collective-permute-start.3 = (bf16[128,576]{1,0:T(8,128)(2,1)S(1)}, bf16[128,576]{1,0:T(8,128)(2,1)S(1)}, u32[]{:S(2)}, u32[]{:S(2)}) collective-permute-start(bf16[128,576]{1,0:T(8,128)(2,1)S(1)} %get-tuple-element.49.refs_5_.refs_8_), channel_id=1, source_target_pairs={{0,16},{16,32},{32,48},{48,64},{64,80},{80,96},{96,112},{112,0},{1... | collective-permute-start | bytes 442376 | tf_op jit(solution)/shard_map/ppermute | solution.py:371
  12.6 7.1 %collective-permute-start.4 = (bf16[128,576]{1,0:T(8,128)(2,1)S(1)}, bf16[128,576]{1,0:T(8,128)(2,1)S(1)}, u32[]{:S(2)}, u32[]{:S(2)}) collective-permute-start(bf16[128,576]{1,0:T(8,128)(2,1)S(1)} %get-tuple-element.50.refs_7_), channel_id=1, source_target_pairs={{0,112},{16,0},{32,16},{48,32},{64,48},{80,64},{96,80},{112,96},{1... | collective-permute-start | bytes 442376 | tf_op jit(solution)/shard_map/ppermute | solution.py:371
  15.8 6.6 %collective-permute-start.10 = (bf16[64,1536]{1,0:T(8,128)(2,1)S(1)}, bf16[64,1536]{1,0:T(8,128)(2,1)S(1)}, u32[]{:S(2)}, u32[]{:S(2)}) collective-permute-start(bf16[64,1536]{1,0:T(8,128)(2,1)S(1)} %get-tuple-element.55.refs_1_), channel_id=1, source_target_pairs={{0,128},{128,0},{1,129},{129,1},{2,130},{130,2},{3,131},{131,3},{4... | collective-permute-start | bytes 589832 | tf_op jit(solution)/shard_map/ppermute | solution.py:363
  19.7 8.2 %collective-permute-start.5 = (bf16[64,1536]{1,0:T(8,128)(2,1)S(1)}, bf16[64,1536]{1,0:T(8,128)(2,1)S(1)}, u32[]{:S(2)}, u32[]{:S(2)}) collective-permute-start(bf16[64,1536]{1,0:T(8,128)(2,1)S(1)} %get-tuple-element.52.refs_1_), channel_id=1, source_target_pairs={{0,128},{128,0},{1,129},{129,1},{2,130},{130,2},{3,131},{131,3},{4... | collective-permute-start | bytes 589832 | tf_op jit(solution)/shard_map/ppermute | solution.py:363
  20.2 7.7 %collective-permute-start.7 = (bf16[128,576]{1,0:T(8,128)(2,1)S(1)}, bf16[128,576]{1,0:T(8,128)(2,1)S(1)}, u32[]{:S(2)}, u32[]{:S(2)}) collective-permute-start(bf16[128,576]{1,0:T(8,128)(2,1)S(1)} %get-tuple-element.53.refs_6_), channel_id=1, source_target_pairs={{0,16},{16,32},{32,48},{48,64},{64,80},{80,96},{96,112},{112,0},{1... | collective-permute-start | bytes 442376 | tf_op jit(solution)/shard_map/ppermute | solution.py:371
  22.4 5.5 %collective-permute-start.8 = (bf16[128,576]{1,0:T(8,128)(2,1)S(1)}, bf16[128,576]{1,0:T(8,128)(2,1)S(1)}, u32[]{:S(2)}, u32[]{:S(2)}) collective-permute-start(bf16[128,576]{1,0:T(8,128)(2,1)S(1)} %get-tuple-element.54.refs_5_), channel_id=1, source_target_pairs={{0,112},{16,0},{32,16},{48,32},{64,48},{80,64},{96,80},{112,96},{1... | collective-permute-start | bytes 442376 | tf_op jit(solution)/shard_map/ppermute | solution.py:371
  23.4 0.7 copy-start.2
  24.1 1.2 %copy-start.4 = (bf16[512,1024]{1,0:T(8,128)(2,1)S(1)}, bf16[512,1024]{1,0:T(8,128)(2,1)}, u32[]{:S(2)}) copy-start(bf16[512,1024]{1,0:T(8,128)(2,1)} %refs_3_.1) | copy-start | bytes 3145732
  27.9 6.2 %collective-permute-start.11 = (bf16[64,576]{1,0:T(8,128)(2,1)S(1)}, bf16[64,576]{1,0:T(8,128)(2,1)S(1)}, u32[]{:S(2)}, u32[]{:S(2)}) collective-permute-start(bf16[64,576]{1,0:T(8,128)(2,1)S(1)} %slice.12), channel_id=1, source_target_pairs={{0,16},{16,32},{32,48},{48,64},{64,80},{80,96},{96,112},{112,0},{1... | collective-permute-start | bytes 221192 | tf_op jit(solution)/shard_map/ppermute | solution.py:371
  29.4 4.7 %copy-start = (bf16[512,1024]{1,0:T(8,128)(2,1)S(1)}, bf16[512,1024]{1,0:T(8,128)(2,1)}, u32[]{:S(2)}) copy-start(bf16[512,1024]{1,0:T(8,128)(2,1)} %refs_4_.1) | copy-start | bytes 3145732
  29.4 4.7 %collective-permute-start.12 = (bf16[64,576]{1,0:T(8,128)(2,1)S(1)}, bf16[64,576]{1,0:T(8,128)(2,1)S(1)}, u32[]{:S(2)}, u32[]{:S(2)}) collective-permute-start(bf16[64,576]{1,0:T(8,128)(2,1)S(1)} %slice.13), channel_id=1, source_target_pairs={{0,112},{16,0},{32,16},{48,32},{64,48},{80,64},{96,80},{112,96},{1... | collective-permute-start | bytes 221192 | tf_op jit(solution)/shard_map/ppermute | solution.py:371
  37.2 5.8 %collective-permute-start.14 = (bf16[64,1152]{1,0:T(8,128)(2,1)S(1)}, bf16[64,1152]{1,0:T(8,128)(2,1)S(1)}, u32[]{:S(2)}, u32[]{:S(2)}) collective-permute-start(bf16[64,1152]{1,0:T(8,128)(2,1)S(1)} %get-tuple-element.69), channel_id=1, source_target_pairs={{0,128},{128,0},{1,129},{129,1},{2,130},{130,2},{3,131},{131,3},{4... | collective-permute-start | bytes 442376 | tf_op jit(solution)/shard_map/ppermute | solution.py:363
  38.9 4.2 %copy-start.3 = (s32[2]{0:T(128)S(1)}, s32[2]{0:T(128)}, u32[]{:S(2)}) copy-start(s32[2]{0:T(128)} %lens.3) | copy-start | bytes 28
  38.9 8.3 %copy-start.1 = (bf16[1024,448]{0,1:T(8,128)(2,1)S(1)}, bf16[1024,448]{0,1:T(8,128)(2,1)}, u32[]{:S(2)}) copy-start(bf16[1024,448]{0,1:T(8,128)(2,1)} %param.15) | copy-start | bytes 2752516
  41.9 5.2 %collective-permute-start.13 = (bf16[64,1152]{1,0:T(8,128)(2,1)S(1)}, bf16[64,1152]{1,0:T(8,128)(2,1)S(1)}, u32[]{:S(2)}, u32[]{:S(2)}) collective-permute-start(bf16[64,1152]{1,0:T(8,128)(2,1)S(1)} %get-tuple-element.67), channel_id=1, source_target_pairs={{0,128},{128,0},{1,129},{129,1},{2,130},{130,2},{3,131},{131,3},{4... | collective-permute-start | bytes 442376 | tf_op jit(solution)/shard_map/ppermute | solution.py:363
  48.2 19.9 %collective-permute-start.19 = (bf16[448,1024]{1,0:T(8,128)(2,1)S(1)}, bf16[448,1024]{1,0:T(8,128)(2,1)S(1)}, u32[]{:S(2)}, u32[]{:S(2)}) collective-permute-start(bf16[448,1024]{1,0:T(8,128)(2,1)S(1)} %get-tuple-element.73.refs_5_.refs_4_), channel_id=1, source_target_pairs={{0,1},{1,0},{2,3},{3,2},{4,5},{5,4},{6,7},{7,6},{8,9},{9,8},{10,11... | collective-permute-start | bytes 2752520 | tf_op jit(solution)/shard_map/ppermute | solution.py:363
  48.3 23.0 %collective-permute-start.22 = (bf16[448,1024]{1,0:T(8,128)(2,1)S(1)}, bf16[448,1024]{1,0:T(8,128)(2,1)S(1)}, u32[]{:S(2)}, u32[]{:S(2)}) collective-permute-start(bf16[448,1024]{1,0:T(8,128)(2,1)S(1)} %get-tuple-element.73.refs_5_.refs_4_), channel_id=1, source_target_pairs={{0,128},{128,0},{1,129},{129,1},{2,130},{130,2},{3,131},{131,3},{4... | collective-permute-start | bytes 2752520 | tf_op jit(solution)/shard_map/ppermute | solution.py:363
  48.9 9.6 %collective-permute-start.15 = (bf16[64,2048]{1,0:T(8,128)(2,1)S(1)}, bf16[64,2048]{1,0:T(8,128)(2,1)S(1)}, u32[]{:S(2)}, u32[]{:S(2)}) collective-permute-start(bf16[64,2048]{1,0:T(8,128)(2,1)S(1)} %get-tuple-element.70.refs_0_), channel_id=1, source_target_pairs={{0,16},{16,32},{32,48},{48,64},{64,80},{80,96},{96,112},{112,0},{1... | collective-permute-start | bytes 786440 | tf_op jit(solution)/shard_map/ppermute | solution.py:371
  50.6 8.1 %collective-permute-start.16 = (bf16[64,2048]{1,0:T(8,128)(2,1)S(1)}, bf16[64,2048]{1,0:T(8,128)(2,1)S(1)}, u32[]{:S(2)}, u32[]{:S(2)}) collective-permute-start(bf16[64,2048]{1,0:T(8,128)(2,1)S(1)} %get-tuple-element.70.refs_0_), channel_id=1, source_target_pairs={{0,112},{16,0},{32,16},{48,32},{64,48},{80,64},{96,80},{112,96},{1... | collective-permute-start | bytes 786440 | tf_op jit(solution)/shard_map/ppermute | solution.py:371
  58.6 8.7 %collective-permute-start.17 = (bf16[64,2048]{1,0:T(8,128)(2,1)S(1)}, bf16[64,2048]{1,0:T(8,128)(2,1)S(1)}, u32[]{:S(2)}, u32[]{:S(2)}) collective-permute-start(bf16[64,2048]{1,0:T(8,128)(2,1)S(1)} %get-tuple-element.71.refs_1_), channel_id=1, source_target_pairs={{0,16},{16,32},{32,48},{48,64},{64,80},{80,96},{96,112},{112,0},{1... | collective-permute-start | bytes 786440 | tf_op jit(solution)/shard_map/ppermute | solution.py:371
  60.9 7.3 %collective-permute-start.18 = (bf16[64,2048]{1,0:T(8,128)(2,1)S(1)}, bf16[64,2048]{1,0:T(8,128)(2,1)S(1)}, u32[]{:S(2)}, u32[]{:S(2)}) collective-permute-start(bf16[64,2048]{1,0:T(8,128)(2,1)S(1)} %get-tuple-element.72.refs_3_), channel_id=1, source_target_pairs={{0,112},{16,0},{32,16},{48,32},{64,48},{80,64},{96,80},{112,96},{1... | collective-permute-start | bytes 786440 | tf_op jit(solution)/shard_map/ppermute | solution.py:371
  68.1 7.6 %collective-permute-start.20 = (bf16[64,2048]{1,0:T(8,128)(2,1)S(1)}, bf16[64,2048]{1,0:T(8,128)(2,1)S(1)}, u32[]{:S(2)}, u32[]{:S(2)}) collective-permute-start(bf16[64,2048]{1,0:T(8,128)(2,1)S(1)} %get-tuple-element.74.refs_2_), channel_id=1, source_target_pairs={{0,16},{16,32},{32,48},{48,64},{64,80},{80,96},{96,112},{112,0},{1... | collective-permute-start | bytes 786440 | tf_op jit(solution)/shard_map/ppermute | solution.py:371
  69.5 6.4 %collective-permute-start.21 = (bf16[64,2048]{1,0:T(8,128)(2,1)S(1)}, bf16[64,2048]{1,0:T(8,128)(2,1)S(1)}, u32[]{:S(2)}, u32[]{:S(2)}) collective-permute-start(bf16[64,2048]{1,0:T(8,128)(2,1)S(1)} %get-tuple-element.75.refs_4_), channel_id=1, source_target_pairs={{0,112},{16,0},{32,16},{48,32},{64,48},{80,64},{96,80},{112,96},{1... | collective-permute-start | bytes 786440 | tf_op jit(solution)/shard_map/ppermute | solution.py:371
  75.9 3.4 %collective-permute-start.25 = (bf16[448,1024]{1,0:T(8,128)(2,1)S(1)}, bf16[448,1024]{1,0:T(8,128)(2,1)S(1)}, u32[]{:S(2)}, u32[]{:S(2)}) collective-permute-start(bf16[448,1024]{1,0:T(8,128)(2,1)S(1)} %get-tuple-element.78.refs_6_.refs_5_), channel_id=1, source_target_pairs={{0,1},{1,0},{2,3},{3,2},{4,5},{5,4},{6,7},{7,6},{8,9},{9,8},{10,11... | collective-permute-start | bytes 2752520 | tf_op jit(solution)/shard_map/ppermute | solution.py:363
  75.9 7.3 %collective-permute-start.23 = (bf16[32,2048]{1,0:T(8,128)(2,1)S(1)}, bf16[32,2048]{1,0:T(8,128)(2,1)S(1)}, u32[]{:S(2)}, u32[]{:S(2)}) collective-permute-start(bf16[32,2048]{1,0:T(8,128)(2,1)S(1)} %slice.14), channel_id=1, source_target_pairs={{0,16},{16,32},{32,48},{48,64},{64,80},{80,96},{96,112},{112,0},{1... | collective-permute-start | bytes 393224 | tf_op jit(solution)/shard_map/ppermute | solution.py:371
  77.6 5.8 %collective-permute-start.24 = (bf16[32,2048]{1,0:T(8,128)(2,1)S(1)}, bf16[32,2048]{1,0:T(8,128)(2,1)S(1)}, u32[]{:S(2)}, u32[]{:S(2)}) collective-permute-start(bf16[32,2048]{1,0:T(8,128)(2,1)S(1)} %slice.15), channel_id=1, source_target_pairs={{0,112},{16,0},{32,16},{48,32},{64,48},{80,64},{96,80},{112,96},{1... | collective-permute-start | bytes 393224 | tf_op jit(solution)/shard_map/ppermute | solution.py:371
  84.8 5.8 %collective-permute-start.26 = (bf16[64,896]{1,0:T(8,128)(2,1)S(1)}, bf16[64,896]{1,0:T(8,128)(2,1)S(1)}, u32[]{:S(2)}, u32[]{:S(2)}) collective-permute-start(bf16[64,896]{1,0:T(8,128)(2,1)S(1)} %get-tuple-element.80), channel_id=1, source_target_pairs={{0,2},{1,3},{2,0},{3,1},{4,6},{5,7},{6,4},{7,5},{8,10},{9,11},{10,... | collective-permute-start | bytes 344072 | tf_op jit(solution)/shard_map/ppermute | solution.py:384
  86.3 7.6 %collective-permute-start.27 = (bf16[64,896]{1,0:T(8,128)(2,1)S(1)}, bf16[64,896]{1,0:T(8,128)(2,1)S(1)}, u32[]{:S(2)}, u32[]{:S(2)}) collective-permute-start(bf16[64,896]{1,0:T(8,128)(2,1)S(1)} %get-tuple-element.81), channel_id=1, source_target_pairs={{0,6},{1,7},{2,4},{3,5},{4,2},{5,3},{6,0},{7,1},{8,14},{9,15},{10,... | collective-permute-start | bytes 344072 | tf_op jit(solution)/shard_map/ppermute | solution.py:384
  88.5 7.0 %collective-permute-start.28 = (bf16[64,896]{1,0:T(8,128)(2,1)S(1)}, bf16[64,896]{1,0:T(8,128)(2,1)S(1)}, u32[]{:S(2)}, u32[]{:S(2)}) collective-permute-start(bf16[64,896]{1,0:T(8,128)(2,1)S(1)} %get-tuple-element.82), channel_id=1, source_target_pairs={{0,4},{1,5},{2,6},{3,7},{4,0},{5,1},{6,2},{7,3},{8,12},{9,13},{10,... | collective-permute-start | bytes 344072 | tf_op jit(solution)/shard_map/ppermute | solution.py:384
  89.1 6.4 %collective-permute-start.29 = (bf16[64,896]{1,0:T(8,128)(2,1)S(1)}, bf16[64,896]{1,0:T(8,128)(2,1)S(1)}, u32[]{:S(2)}, u32[]{:S(2)}) collective-permute-start(bf16[64,896]{1,0:T(8,128)(2,1)S(1)} %get-tuple-element.83), channel_id=1, source_target_pairs={{0,1},{1,0},{2,3},{3,2},{4,5},{5,4},{6,7},{7,6},{8,9},{9,8},{10,11... | collective-permute-start | bytes 344072 | tf_op jit(solution)/shard_map/ppermute | solution.py:363
  89.1 6.4 %collective-permute-start.30 = (bf16[64,896]{1,0:T(8,128)(2,1)S(1)}, bf16[64,896]{1,0:T(8,128)(2,1)S(1)}, u32[]{:S(2)}, u32[]{:S(2)}) collective-permute-start(bf16[64,896]{1,0:T(8,128)(2,1)S(1)} %get-tuple-element.84), channel_id=1, source_target_pairs={{0,3},{1,2},{2,1},{3,0},{4,7},{5,6},{6,5},{7,4},{8,11},{9,10},{10,... | collective-permute-start | bytes 344072 | tf_op jit(solution)/shard_map/ppermute | solution.py:384
  90.6 6.9 %collective-permute-start.31 = (bf16[64,896]{1,0:T(8,128)(2,1)S(1)}, bf16[64,896]{1,0:T(8,128)(2,1)S(1)}, u32[]{:S(2)}, u32[]{:S(2)}) collective-permute-start(bf16[64,896]{1,0:T(8,128)(2,1)S(1)} %get-tuple-element.85), channel_id=1, source_target_pairs={{0,7},{1,6},{2,5},{3,4},{4,3},{5,2},{6,1},{7,0},{8,15},{9,14},{10,... | collective-permute-start | bytes 344072 | tf_op jit(solution)/shard_map/ppermute | solution.py:384
  93.9 6.3 %collective-permute-start.32 = (bf16[64,896]{1,0:T(8,128)(2,1)S(1)}, bf16[64,896]{1,0:T(8,128)(2,1)S(1)}, u32[]{:S(2)}, u32[]{:S(2)}) collective-permute-start(bf16[64,896]{1,0:T(8,128)(2,1)S(1)} %get-tuple-element.86), channel_id=1, source_target_pairs={{0,5},{1,4},{2,7},{3,6},{4,1},{5,0},{6,3},{7,2},{8,13},{9,12},{10,... | collective-permute-start | bytes 344072 | tf_op jit(solution)/shard_map/ppermute | solution.py:384
  100.5 7.2 %collective-permute-start.33 = (bf16[2,64,448]{2,1,0:T(8,128)(2,1)S(1)}, bf16[2,64,448]{2,1,0:T(8,128)(2,1)S(1)}, u32[]{:S(2)}, u32[]{:S(2)}) collective-permute-start(bf16[2,64,448]{2,1,0:T(8,128)(2,1)S(1)} %get-tuple-element.87), channel_id=1, source_target_pairs={{0,0},{8,128},{128,8},{136,136},{1,1},{9,129},{129,9},{137,137},{2... | collective-permute-start | bytes 344072 | tf_op jit(solution)/shard_map/ppermute | solution.py:486
  104.7 5.0 %collective-permute-start.34 = (bf16[2,64,448]{2,1,0:T(8,128)(2,1)S(1)}, bf16[2,64,448]{2,1,0:T(8,128)(2,1)S(1)}, u32[]{:S(2)}, u32[]{:S(2)}) collective-permute-start(bf16[2,64,448]{2,1,0:T(8,128)(2,1)S(1)} %get-tuple-element.88), channel_id=1, source_target_pairs={{0,128},{128,136},{8,0},{136,8},{1,129},{129,137},{9,1},{137,9},{2... | collective-permute-start | bytes 344072 | tf_op jit(solution)/shard_map/ppermute | solution.py:487

commit v4 on v3

--- a/solution.py
+++ b/solution.py
@@ -72,7 +72,13 @@
     c = (NOPE + ROPE) ** -0.5 * LOG2E
     starts, q0, q1, wuk = refs[:4]
     pieces = refs[4 : 4 + len(slots)]
-    qaug, acc, stats, keys, bias = refs[5 + len(slots) :]
+    rest = refs[5 + len(slots) :]
+    moving = None
+    if len(rest) > 5:
+        moving = pltpu.make_async_copy(rest[0], rest[4], rest[-1])
+        moving.start()
+        rest = (*rest[1:4], *rest[5:7])
+    qaug, acc, stats, keys, bias = rest
     load_keys(rows, slots, pieces, keys)
     bias[...] = hidden_keys(rows, slots, half, starts)
     wide = heads * NOPE
@@ -96,14 +102,15 @@
         acc[here] = nn(p.astype(bf16), keys[:, :LATENT])
         stats[here, :128] = m
         stats[here, 128:] = jnp.broadcast_to(jnp.sum(p, axis=-1, keepdims=True), (block, 128))
+    if moving is not None:
+        moving.wait()
 
 
 def second_kernel(rows, heads, half, slots, *refs):
     c = (NOPE + ROPE) ** -0.5 * LOG2E
     starts, qaug, acc, stats, wuv = refs[:5]
-    count = len(refs) - 11
-    pieces = refs[5 : 5 + count]
-    own, own_lse, message, keys, bias = refs[6 + count :]
+    pieces = refs[5 : 6 + len(slots)]
+    own, own_lse, message, keys, bias = refs[-5:]
     load_keys(rows, slots, pieces, keys)
     bias[...] = hidden_keys(rows, slots, half, starts)
     wide = heads * NOPE
@@ -162,19 +169,46 @@
     return pl.CostEstimate(flops=flops, transcendentals=exps, bytes_accessed=4 * MIB)
 
 
-def attention_first(starts, q0, q1, wuk, pieces, slots, half, earlier):
+def attention_first(starts, q0, q1, wuk, pieces, slots, half, earlier, weights=None):
     rows = q0.shape[0]
     heads = wuk.shape[1] // NOPE
     height = heads * 2 * rows
     count = 2 * rows * len(slots)
+    carried = () if weights is None else in_hbm(weights)
     return pl.pallas_call(
         functools.partial(first_kernel, rows, heads, half, slots),
         out_shape=(
             pltpu.VMEM((height, LATENT + 2 * ROPE), bf16),
             pltpu.VMEM((height, LATENT), f32),
             pltpu.VMEM((height, 256), f32),
+            *(pltpu.VMEM(x.shape, bf16) for x in carried),
         ),
-        in_specs=[SMEM] + [VMEM] * (3 + len(pieces)) + [ANY],
+        in_specs=[SMEM] + [VMEM] * (3 + len(pieces)) + [ANY] * (1 + len(carried)),
+        out_specs=(VMEM,) * 3 + (ANY,) * len(carried),
+        scratch_shapes=[
+            pltpu.VMEM((count, LATENT + 2 * ROPE), bf16),
+            pltpu.VMEM((2 * rows, count), f32),
+        ]
+        + [pltpu.SemaphoreType.DMA(())] * len(carried),
+        compiler_params=params(16),
+        cost_estimate=cost(2 * height * count * (2 * LATENT + 2 * ROPE), height * count),
+    )(starts, *held_in_vmem(q0, q1, wuk, *pieces, earlier), *carried)
+
+
+def attention_second(starts, state, wuv, pieces, slots, half, *earlier):
+    heads = wuv.shape[1] // NOPE
+    height = state[0].shape[0]
+    rows = height // heads // 2
+    count = 2 * rows * len(slots)
+    wide = heads * NOPE
+    return pl.pallas_call(
+        functools.partial(second_kernel, rows, heads, half, slots),
+        out_shape=(
+            pltpu.VMEM((rows, wide), f32),
+            pltpu.VMEM((rows, 128), f32),
+            pltpu.VMEM((rows, wide + 128), bf16),
+        ),
+        in_specs=[SMEM] + [VMEM] * (4 + len(pieces)) + [ANY] * len(earlier),
         out_specs=(VMEM, VMEM, VMEM),
         scratch_shapes=[
             pltpu.VMEM((count, LATENT + 2 * ROPE), bf16),
@@ -182,31 +216,7 @@
         ],
         compiler_params=params(16),
         cost_estimate=cost(2 * height * count * (2 * LATENT + 2 * ROPE), height * count),
-    )(starts, *held_in_vmem(q0, q1, wuk, *pieces, earlier))
-
-
-def attention_second(starts, state, wuv, pieces, slots, half, earlier):
-    heads = wuv.shape[1] // NOPE
-    height = state[0].shape[0]
-    rows = height // heads // 2
-    count = 2 * rows * len(slots)
-    wide = heads * NOPE
-    return pl.pallas_call(
-        functools.partial(second_kernel, rows, heads, half, slots),
-        out_shape=(
-            pltpu.VMEM((rows, wide), f32),
-            pltpu.VMEM((rows, 128), f32),
-            pltpu.VMEM((rows, wide + 128), bf16),
-        ),
-        in_specs=[SMEM] + [VMEM] * (4 + len(pieces)) + [ANY],
-        out_specs=(VMEM, VMEM, VMEM),
-        scratch_shapes=[
-            pltpu.VMEM((count, LATENT + 2 * ROPE), bf16),
-            pltpu.VMEM((2 * rows, count), f32),
-        ],
-        compiler_params=params(16),
-        cost_estimate=cost(2 * height * count * (2 * LATENT + 2 * ROPE), height * count),
-    )(starts, *held_in_vmem(*state, wuv, *pieces, earlier))
+    )(starts, *held_in_vmem(*state, wuv, *pieces, *earlier))
 
 
 def combine_kernel(rows, heads, half, part, starts, lens, own, lse, got, *refs):
@@ -457,22 +467,24 @@
     w_uv2 = swap(w_uv, "core")
     near = [latent, u1, u2, d1]
     near_at, far_at = (0, 1, 2, 7), (6, 3, 5, 4)
-    a1 = attention_first(stretch_start, q_own, q_own_y, w_uk, near, near_at, half, u1)
-    u3, d3 = level(step(u2, d2), (q_got_y, w_uk2, w_uv2, a1[2]))
+    *a1, w_t = attention_first(
+        stretch_start, q_own, q_own_y, w_uk, near, near_at, half, u1, w_o.T
+    )
+    u3, d3, w_t = level((*step(u2, d2), w_t), (q_got_y, w_uk2, w_uv2, a1[2]))
+    w_t_c = swap(w_t, "core")
     b1 = attention_first(stretch_start, q_got, q_got_y, w_uk2, near, near_at, half, u3)
     far = [d2, u3, d3, *last(u3, d3)]
     a2 = attention_second(stretch_start, a1, w_uv, far, far_at, half, b1[2])
     got_a = swap(a2[2], "yl")
-    b2 = attention_second(stretch_start, b1, w_uv2, far, far_at, half, a2[1])
+    b2 = attention_second(stretch_start, b1, w_uv2, far, far_at, half, a2[1], w_t_c)
     got_b = swap(b2[2], "yl")
     known = (stretch_start, prompt_len)
     attention = combine_first(*known, *a2[:2], got_a, half, b2[1])
     attention, w_t = combine_second(*known, *b2[:2], got_b, half, attention, w_o.T)
 
     u1, d1 = level(step(attention, attention))
-    w_t_c = swap(w_t, "core")
     w_t_y = swap(w_t, "yl")
-    u2, d2 = level(step(u1, d1), (w_t_c,))
+    u2, d2 = level(step(u1, d1))
     u3, d3, w_t_y = level((*step(u2, d2), w_t_y))
     w_t_cy = swap(w_t_y, "core")
     weights = (w_t, w_t_y, w_t_c, w_t_cy)

time: 111 us -> 108 us (0.973)
  waiting for transfers between devices: 45 us -> 42.9 us
    ppermute x16, waiting for transfers between devices: 27.9 us -> 25.5 us  [step(): return (lax.ppermute(a, 'z', UP), lax.ppermute(b, 'z', DOWN))]
  transfers between devices with their start and end apart: 35 -> 35, of which waited for: 19 -> 19; matrix products, arithmetic and copies ran while one was open for 0% -> 0% of each run, Pallas kernels for 11% -> 14%
where the time goes in v4:
time: 108 us
  starting transfers between devices  45.1 us (42%)
  waiting for transfers between devices  42.9 us (40%)
  Pallas kernels  17.5 us (16%)
  local copies, waits for them, and re-layouts  1.93 us (2%)
    ppermute x16, starting transfers between devices, step(): return (lax.ppermute(a, 'z', UP), lax.ppermute(b, 'z', DOWN))  28.9 us
    ppermute x16, waiting for transfers between devices, step(): return (lax.ppermute(a, 'z', UP), lax.ppermute(b, 'z', DOWN))  25.5 us
    ppermute x6, waiting for transfers between devices, to_partner(): return lax.ppermute(x, ('x', 'core'), moves)  8.04 us
    ppermute x6, starting transfers between devices, to_partner(): return lax.ppermute(x, ('x', 'core'), moves)  7.51 us
    pallas_call x2, Pallas kernels, attention_second(): pl.pallas_call(functools.partial(second_kernel, rows, heads, half, slots)...  6.09 us
    pallas_call x2, Pallas kernels, attention_first(): pl.pallas_call(functools.partial(first_kernel, rows, heads, half, slots),...  5.16 us
    ppermute x11, waiting for transfers between devices, swap(): return lax.ppermute(x, axis, [(0, 1), (1, 0)])  4.4 us
    ppermute x11, starting transfers between devices, swap(): return lax.ppermute(x, axis, [(0, 1), (1, 0)])  4.34 us
  transfers between devices with their start and end apart: 35, of which 19 were waited for; matrix products, arithmetic and copies ran while one was open for 0% of the time, Pallas kernels for 14%

profile of v4, /device:TPU:8, one launch (start us, length us, event | category | flops | bytes accessed | tf_op | source)
XLA Modules:
  0.0 108.3 jit_solution(12815154314956283666)
XLA Ops:
  0.0 0.5 collective-permute-start.6
  0.5 1.1 %shard_map.91 = (bf16[128,576]{1,0:T(8,128)(2,1)S(1)}, bf16[64,1536]{1,0:T(8,128)(2,1)S(1)}, bf16[64,1536]{1,0:T(8,128)(2,1)S(1)}) custom-call(bf16[2,64,1024]{2,1,0:T(8,128)(2,1)} %q_nope.1, bf16[2,64,512]{2,1,0:T(8,128)(2,1)} %q_rope.1, bf16[2,64,576]{2,1,0:T(8,128)(2,1)} %cache.1, bf16[2,64,576]{2,1,0:T(8,128)(2,1)} %stretch.1), custom_call_target="tpu_custom_call" | custom-call | tf_op jit(solution)/shard_map/pallas_call | solution.py:418
  1.6 0.1 collective-permute-start.2
  1.7 2.0 %collective-permute-start = (bf16[128,576]{1,0:T(8,128)(2,1)S(1)}, bf16[128,576]{1,0:T(8,128)(2,1)S(1)}, u32[]{:S(2)}, u32[]{:S(2)}) collective-permute-start(bf16[128,576]{1,0:T(8,128)(2,1)S(1)} %get-tuple-element.49.refs_4_), channel_id=1, source_target_pairs={{0,16},{16,32},{32,48},{48,64},{64,80},{80,96},{96,112},{112,0},{1... | collective-permute-start | bytes 442376 | tf_op jit(solution)/shard_map/ppermute | solution.py:381
  3.7 4.0 %collective-permute-start.1 = (bf16[128,576]{1,0:T(8,128)(2,1)S(1)}, bf16[128,576]{1,0:T(8,128)(2,1)S(1)}, u32[]{:S(2)}, u32[]{:S(2)}) collective-permute-start(bf16[128,576]{1,0:T(8,128)(2,1)S(1)} %get-tuple-element.49.refs_4_), channel_id=1, source_target_pairs={{0,112},{16,0},{32,16},{48,32},{64,48},{80,64},{96,80},{112,96},{1... | collective-permute-start | bytes 442376 | tf_op jit(solution)/shard_map/ppermute | solution.py:381
  7.8 4.7 %collective-permute-done.refs_0_ = bf16[128,576]{1,0:T(8,128)(2,1)S(1)} collective-permute-done((bf16[128,576]{1,0:T(8,128)(2,1)S(1)}, bf16[128,576]{1,0:T(8,128)(2,1)S(1)}, u32[]{:S(2)}, u32[]{:S(2)}) %collective-permute-start) | collective-permute-done | bytes 147488 | tf_op jit(solution)/shard_map/ppermute | solution.py:381
  12.5 0.1 collective-permute-start.3
  12.6 3.2 %collective-permute-start.4 = (bf16[128,576]{1,0:T(8,128)(2,1)S(1)}, bf16[128,576]{1,0:T(8,128)(2,1)S(1)}, u32[]{:S(2)}, u32[]{:S(2)}) collective-permute-start(bf16[128,576]{1,0:T(8,128)(2,1)S(1)} %get-tuple-element.52.refs_7_), channel_id=1, source_target_pairs={{0,112},{16,0},{32,16},{48,32},{64,48},{80,64},{96,80},{112,96},{1... | collective-permute-start | bytes 442376 | tf_op jit(solution)/shard_map/ppermute | solution.py:381
  15.8 0.4 collective-permute-start.9
  16.2 3.5 %collective-permute-done.3.refs_0_ = bf16[128,576]{1,0:T(8,128)(2,1)S(1)} collective-permute-done((bf16[128,576]{1,0:T(8,128)(2,1)S(1)}, bf16[128,576]{1,0:T(8,128)(2,1)S(1)}, u32[]{:S(2)}, u32[]{:S(2)}) %collective-permute-start.3) | collective-permute-done | bytes 147488 | tf_op jit(solution)/shard_map/ppermute | solution.py:381
  19.7 0.5 collective-permute-start.5
  20.2 1.9 %collective-permute-start.7 = (bf16[128,576]{1,0:T(8,128)(2,1)S(1)}, bf16[128,576]{1,0:T(8,128)(2,1)S(1)}, u32[]{:S(2)}, u32[]{:S(2)}) collective-permute-start(bf16[128,576]{1,0:T(8,128)(2,1)S(1)} %get-tuple-element.55.refs_6_), channel_id=1, source_target_pairs={{0,16},{16,32},{32,48},{48,64},{64,80},{80,96},{96,112},{112,0},{1... | collective-permute-start | bytes 442376 | tf_op jit(solution)/shard_map/ppermute | solution.py:381
  22.0 0.4 collective-permute-done.9.refs_2_
  22.4 1.0 collective-permute-start.8
  23.4 0.7 copy-done.2
  24.1 1.2 %copy-done.4 = bf16[512,1024]{1,0:T(8,128)(2,1)S(1)} copy-done((bf16[512,1024]{1,0:T(8,128)(2,1)S(1)}, bf16[512,1024]{1,0:T(8,128)(2,1)}, u32[]{:S(2)}) %copy-start.4) | copy-done | bytes 1048600
  25.3 2.6 %shard_map.94 = (bf16[1024,640]{1,0:T(8,128)(2,1)S(1)}, f32[1024,512]{1,0:T(8,128)S(1)}, f32[1024,256]{1,0:T(8,128)S(1)}, bf16[448,1024]{1,0:T(8,128)(2,1)S(1)}) custom-call(s32[2]{0:T(128)S(1)} %copy-done.2, bf16[64,1536]{1,0:T(8,128)(2,1)S(1)} %get-tuple-element.57.refs_1_, bf16[64,1536]{1,0:T(8,128)(2,1)S(1)} %collective-permute-done.9.refs_2_, ...), custom_call_target="tpu_custom_call" | custom-call | flops 1207959552 | bytes 4194304 | tf_op jit(solution)/shard_map/pallas_call | solution.py:178
  27.9 0.1 collective-permute-start.13
  28.1 1.4 %collective-permute-start.11 = (bf16[64,576]{1,0:T(8,128)(2,1)S(1)}, bf16[64,576]{1,0:T(8,128)(2,1)S(1)}, u32[]{:S(2)}, u32[]{:S(2)}) collective-permute-start(bf16[64,576]{1,0:T(8,128)(2,1)S(1)} %slice.12), channel_id=1, source_target_pairs={{0,16},{16,32},{32,48},{48,64},{64,80},{80,96},{96,112},{112,0},{1... | collective-permute-start | bytes 221192 | tf_op jit(solution)/shard_map/ppermute | solution.py:381
  29.5 2.1 %collective-permute-start.12 = (bf16[64,576]{1,0:T(8,128)(2,1)S(1)}, bf16[64,576]{1,0:T(8,128)(2,1)S(1)}, u32[]{:S(2)}, u32[]{:S(2)}) collective-permute-start(bf16[64,576]{1,0:T(8,128)(2,1)S(1)} %slice.13), channel_id=1, source_target_pairs={{0,112},{16,0},{32,16},{48,32},{64,48},{80,64},{96,80},{112,96},{1... | collective-permute-start | bytes 221192 | tf_op jit(solution)/shard_map/ppermute | solution.py:381
  31.7 2.6 %shard_map.96 = (bf16[1024,640]{1,0:T(8,128)(2,1)S(1)}, f32[1024,512]{1,0:T(8,128)S(1)}, f32[1024,256]{1,0:T(8,128)S(1)}) custom-call(s32[2]{0:T(128)S(1)} %copy-done.2, bf16[64,1536]{1,0:T(8,128)(2,1)S(1)} %get-tuple-element.54.refs_1_, bf16[64,1536]{1,0:T(8,128)(2,1)S(1)} %collective-permute-done.5.refs_3_.refs_2_, ...), custom_call_target="tpu_custom_call" | custom-call | flops 1207959552 | bytes 4194304 | tf_op jit(solution)/shard_map/pallas_call | solution.py:178
  34.2 0.1 collective-permute-done.12.refs_9_
  34.3 3.0 %shard_map.97 = (f32[64,1024]{1,0:T(8,128)S(1)}, f32[64,128]{1,0:T(8,128)S(1)}, bf16[64,1152]{1,0:T(8,128)(2,1)S(1)}) custom-call(s32[2]{0:T(128)S(1)} %copy-done.2, bf16[1024,640]{1,0:T(8,128)(2,1)S(1)} %get-tuple-element.65.refs_1_, f32[1024,512]{1,0:T(8,128)S(1)} %get-tuple-element.66.refs_2_, f32[1024,256]{1,0:T(8,128)S(1)} %get-tuple-element.59.refs_6_.refs_3_, ...), custom_call_target="tpu_custom_call" | custom-call | flops 1207959552 | bytes 4194304 | tf_op jit(solution)/shard_map/pallas_call | solution.py:204
  37.4 1.7 %collective-permute-start.15 = (bf16[64,1152]{1,0:T(8,128)(2,1)S(1)}, bf16[64,1152]{1,0:T(8,128)(2,1)S(1)}, u32[]{:S(2)}, u32[]{:S(2)}) collective-permute-start(bf16[64,1152]{1,0:T(8,128)(2,1)S(1)} %get-tuple-element.73), channel_id=1, source_target_pairs={{0,128},{128,0},{1,129},{129,1},{2,130},{130,2},{3,131},{131,3},{4... | collective-permute-start | bytes 442376 | tf_op jit(solution)/shard_map/ppermute | solution.py:373
  39.1 3.0 %shard_map.98 = (f32[64,1024]{1,0:T(8,128)S(1)}, f32[64,128]{1,0:T(8,128)S(1)}, bf16[64,1152]{1,0:T(8,128)(2,1)S(1)}) custom-call(s32[2]{0:T(128)S(1)} %copy-done.2, bf16[1024,640]{1,0:T(8,128)(2,1)S(1)} %get-tuple-element.61.refs_1_, f32[1024,512]{1,0:T(8,128)S(1)} %get-tuple-element.62.refs_2_, f32[1024,256]{1,0:T(8,128)S(1)} %get-tuple-element.63.refs_10_.refs_3_, ...), custom_call_target="tpu_custom_call" | custom-call | flops 1207959552 | bytes 4194304 | tf_op jit(solution)/shard_map/pallas_call | solution.py:204
  42.1 0.5 collective-permute-start.14
  42.7 0.4 collective-permute-done.15.got
  43.1 0.8 shard_map.99.refs_0_
  43.9 3.6 %collective-permute-done.14.got = bf16[64,1152]{1,0:T(8,128)(2,1)S(1)} collective-permute-done((bf16[64,1152]{1,0:T(8,128)(2,1)S(1)}, bf16[64,1152]{1,0:T(8,128)(2,1)S(1)}, u32[]{:S(2)}, u32[]{:S(2)}) %collective-permute-start.14) | collective-permute-done | bytes 147488 | tf_op jit(solution)/shard_map/ppermute | solution.py:373
  47.5 1.1 %shard_map.100 = (bf16[64,2048]{1,0:T(8,128)(2,1)S(1)}, bf16[448,1024]{1,0:T(8,128)(2,1)S(1)}) custom-call(s32[2]{0:T(128)S(1)} %copy-done.2, s32[2]{0:T(128)S(1)} %copy-done.3, f32[64,1024]{1,0:T(8,128)S(1)} %get-tuple-element.69.own, f32[64,128]{1,0:T(8,128)S(1)} %get-tuple-element.70.refs_0_.lse, ...), custom_call_target="tpu_custom_call", output_to_operand_aliasing={{0}: (5, {})} | custom-call | flops 524288 | bytes 4194304 | tf_op jit(solution)/shard_map/pallas_call | solution.py:263
  48.6 0.5 collective-permute-start.22
  49.2 1.5 %collective-permute-start.16 = (bf16[64,2048]{1,0:T(8,128)(2,1)S(1)}, bf16[64,2048]{1,0:T(8,128)(2,1)S(1)}, u32[]{:S(2)}, u32[]{:S(2)}) collective-permute-start(bf16[64,2048]{1,0:T(8,128)(2,1)S(1)} %get-tuple-element.74.refs_0_), channel_id=1, source_target_pairs={{0,16},{16,32},{32,48},{48,64},{64,80},{80,96},{96,112},{112,0},{1... | collective-permute-start | bytes 786440 | tf_op jit(solution)/shard_map/ppermute | solution.py:381
  50.7 1.7 %collective-permute-start.17 = (bf16[64,2048]{1,0:T(8,128)(2,1)S(1)}, bf16[64,2048]{1,0:T(8,128)(2,1)S(1)}, u32[]{:S(2)}, u32[]{:S(2)}) collective-permute-start(bf16[64,2048]{1,0:T(8,128)(2,1)S(1)} %get-tuple-element.74.refs_0_), channel_id=1, source_target_pairs={{0,112},{16,0},{32,16},{48,32},{64,48},{80,64},{96,80},{112,96},{1... | collective-permute-start | bytes 786440 | tf_op jit(solution)/shard_map/ppermute | solution.py:381
  52.4 4.6 %collective-permute-done.16.refs_0_ = bf16[64,2048]{1,0:T(8,128)(2,1)S(1)} collective-permute-done((bf16[64,2048]{1,0:T(8,128)(2,1)S(1)}, bf16[64,2048]{1,0:T(8,128)(2,1)S(1)}, u32[]{:S(2)}, u32[]{:S(2)}) %collective-permute-start.16) | collective-permute-done | bytes 262176 | tf_op jit(solution)/shard_map/ppermute | solution.py:381
  57.0 0.1 collective-permute-done.17.refs_1_
  57.1 1.9 %collective-permute-start.18 = (bf16[64,2048]{1,0:T(8,128)(2,1)S(1)}, bf16[64,2048]{1,0:T(8,128)(2,1)S(1)}, u32[]{:S(2)}, u32[]{:S(2)}) collective-permute-start(bf16[64,2048]{1,0:T(8,128)(2,1)S(1)} %get-tuple-element.75.refs_1_), channel_id=1, source_target_pairs={{0,16},{16,32},{32,48},{48,64},{64,80},{80,96},{96,112},{112,0},{1... | collective-permute-start | bytes 786440 | tf_op jit(solution)/shard_map/ppermute | solution.py:381
  59.0 1.3 %collective-permute-start.19 = (bf16[64,2048]{1,0:T(8,128)(2,1)S(1)}, bf16[64,2048]{1,0:T(8,128)(2,1)S(1)}, u32[]{:S(2)}, u32[]{:S(2)}) collective-permute-start(bf16[64,2048]{1,0:T(8,128)(2,1)S(1)} %get-tuple-element.76.refs_3_), channel_id=1, source_target_pairs={{0,112},{16,0},{32,16},{48,32},{64,48},{80,64},{96,80},{112,96},{1... | collective-permute-start | bytes 786440 | tf_op jit(solution)/shard_map/ppermute | solution.py:381
  60.3 4.3 %collective-permute-done.18.refs_0_ = bf16[64,2048]{1,0:T(8,128)(2,1)S(1)} collective-permute-done((bf16[64,2048]{1,0:T(8,128)(2,1)S(1)}, bf16[64,2048]{1,0:T(8,128)(2,1)S(1)}, u32[]{:S(2)}, u32[]{:S(2)}) %collective-permute-start.18) | collective-permute-done | bytes 262176 | tf_op jit(solution)/shard_map/ppermute | solution.py:381
  64.7 0.7 collective-permute-done.19.refs_1_
  65.4 2.2 %collective-permute-start.20 = (bf16[64,2048]{1,0:T(8,128)(2,1)S(1)}, bf16[64,2048]{1,0:T(8,128)(2,1)S(1)}, u32[]{:S(2)}, u32[]{:S(2)}) collective-permute-start(bf16[64,2048]{1,0:T(8,128)(2,1)S(1)} %get-tuple-element.77.refs_2_), channel_id=1, source_target_pairs={{0,16},{16,32},{32,48},{48,64},{64,80},{80,96},{96,112},{112,0},{1... | collective-permute-start | bytes 786440 | tf_op jit(solution)/shard_map/ppermute | solution.py:381
  67.6 1.0 collective-permute-start.21
  68.6 4.3 %collective-permute-done.20.refs_0_ = bf16[64,2048]{1,0:T(8,128)(2,1)S(1)} collective-permute-done((bf16[64,2048]{1,0:T(8,128)(2,1)S(1)}, bf16[64,2048]{1,0:T(8,128)(2,1)S(1)}, u32[]{:S(2)}, u32[]{:S(2)}) %collective-permute-start.20) | collective-permute-done | bytes 262176 | tf_op jit(solution)/shard_map/ppermute | solution.py:381
  73.0 1.0 collective-permute-done.21.refs_1_
  74.0 1.5 %collective-permute-start.23 = (bf16[32,2048]{1,0:T(8,128)(2,1)S(1)}, bf16[32,2048]{1,0:T(8,128)(2,1)S(1)}, u32[]{:S(2)}, u32[]{:S(2)}) collective-permute-start(bf16[32,2048]{1,0:T(8,128)(2,1)S(1)} %slice.14), channel_id=1, source_target_pairs={{0,16},{16,32},{32,48},{48,64},{64,80},{80,96},{96,112},{112,0},{1... | collective-permute-start | bytes 393224 | tf_op jit(solution)/shard_map/ppermute | solution.py:381
  75.5 1.9 %collective-permute-start.24 = (bf16[32,2048]{1,0:T(8,128)(2,1)S(1)}, bf16[32,2048]{1,0:T(8,128)(2,1)S(1)}, u32[]{:S(2)}, u32[]{:S(2)}) collective-permute-start(bf16[32,2048]{1,0:T(8,128)(2,1)S(1)} %slice.15), channel_id=1, source_target_pairs={{0,112},{16,0},{32,16},{48,32},{64,48},{80,64},{96,80},{112,96},{1... | collective-permute-start | bytes 393224 | tf_op jit(solution)/shard_map/ppermute | solution.py:381
  77.4 1.6 %shard_map.104.refs_8_ = bf16[320,896]{1,0:T(8,128)(2,1)S(1)} custom-call(bf16[64,2048]{1,0:T(8,128)(2,1)S(1)} %get-tuple-element.74.refs_0_, bf16[64,2048]{1,0:T(8,128)(2,1)S(1)} %get-tuple-element.75.refs_1_, bf16[64,2048]{1,0:T(8,128)(2,1)S(1)} %get-tuple-element.77.refs_2_, bf16[64,2048]{1,0:T(8,128)(2,1)S(1)} %get-tuple-element.76.refs_3_, ...), custom_call_target="tpu_custom_call" | custom-call | flops 1174405120 | bytes 4194304 | tf_op jit(solution)/shard_map/pallas_call | solution.py:327
  79.0 2.2 %collective-permute-done.23.refs_2_ = bf16[32,2048]{1,0:T(8,128)(2,1)S(1)} collective-permute-done((bf16[32,2048]{1,0:T(8,128)(2,1)S(1)}, bf16[32,2048]{1,0:T(8,128)(2,1)S(1)}, u32[]{:S(2)}, u32[]{:S(2)}) %collective-permute-start.23) | collective-permute-done | bytes 131104 | tf_op jit(solution)/shard_map/ppermute | solution.py:381
  81.2 0.0 collective-permute-done.24.refs_3_
  81.2 1.4 %shard_map.105 = (bf16[64,896]{1,0:T(8,128)(2,1)S(1)}, bf16[64,896]{1,0:T(8,128)(2,1)S(1)}, bf16[64,896]{1,0:T(8,128)(2,1)S(1)}, bf16[64,896]{1,0:T(8,128)(2,1)S...) custom-call(bf16[64,2048]{1,0:T(8,128)(2,1)S(1)} %get-tuple-element., ...), custom_call_target="tpu_custom_call" | custom-call | flops 704643072 | bytes 4194304 | tf_op jit(solution)/shard_map/pallas_call | solution.py:342
  82.6 1.6 %collective-permute-start.26 = (bf16[64,896]{1,0:T(8,128)(2,1)S(1)}, bf16[64,896]{1,0:T(8,128)(2,1)S(1)}, u32[]{:S(2)}, u32[]{:S(2)}) collective-permute-start(bf16[64,896]{1,0:T(8,128)(2,1)S(1)} %get-tuple-element.84), channel_id=1, source_target_pairs={{0,2},{1,3},{2,0},{3,1},{4,6},{5,7},{6,4},{7,5},{8,10},{9,11},{10,... | collective-permute-start | bytes 344072 | tf_op jit(solution)/shard_map/ppermute | solution.py:394
  84.1 2.1 %collective-permute-start.27 = (bf16[64,896]{1,0:T(8,128)(2,1)S(1)}, bf16[64,896]{1,0:T(8,128)(2,1)S(1)}, u32[]{:S(2)}, u32[]{:S(2)}) collective-permute-start(bf16[64,896]{1,0:T(8,128)(2,1)S(1)} %get-tuple-element.85), channel_id=1, source_target_pairs={{0,6},{1,7},{2,4},{3,5},{4,2},{5,3},{6,0},{7,1},{8,14},{9,15},{10,... | collective-permute-start | bytes 344072 | tf_op jit(solution)/shard_map/ppermute | solution.py:394
  86.2 0.6 collective-permute-start.28
  86.9 1.5 %collective-permute-start.30 = (bf16[64,896]{1,0:T(8,128)(2,1)S(1)}, bf16[64,896]{1,0:T(8,128)(2,1)S(1)}, u32[]{:S(2)}, u32[]{:S(2)}) collective-permute-start(bf16[64,896]{1,0:T(8,128)(2,1)S(1)} %get-tuple-element.88), channel_id=1, source_target_pairs={{0,3},{1,2},{2,1},{3,0},{4,7},{5,6},{6,5},{7,4},{8,11},{9,10},{10,... | collective-permute-start | bytes 344072 | tf_op jit(solution)/shard_map/ppermute | solution.py:394
  88.3 1.7 %collective-permute-start.31 = (bf16[64,896]{1,0:T(8,128)(2,1)S(1)}, bf16[64,896]{1,0:T(8,128)(2,1)S(1)}, u32[]{:S(2)}, u32[]{:S(2)}) collective-permute-start(bf16[64,896]{1,0:T(8,128)(2,1)S(1)} %get-tuple-element.89), channel_id=1, source_target_pairs={{0,7},{1,6},{2,5},{3,4},{4,3},{5,2},{6,1},{7,0},{8,15},{9,14},{10,... | collective-permute-start | bytes 344072 | tf_op jit(solution)/shard_map/ppermute | solution.py:394
  90.1 1.9 %collective-permute-done.27.refs_2_ = bf16[64,896]{1,0:T(8,128)(2,1)S(1)} collective-permute-done((bf16[64,896]{1,0:T(8,128)(2,1)S(1)}, bf16[64,896]{1,0:T(8,128)(2,1)S(1)}, u32[]{:S(2)}, u32[]{:S(2)}) %collective-permute-start.27) | collective-permute-done | bytes 114720 | tf_op jit(solution)/shard_map/ppermute | solution.py:394
  92.0 1.2 %collective-permute-done.28.refs_3_ = bf16[64,896]{1,0:T(8,128)(2,1)S(1)} collective-permute-done((bf16[64,896]{1,0:T(8,128)(2,1)S(1)}, bf16[64,896]{1,0:T(8,128)(2,1)S(1)}, u32[]{:S(2)}, u32[]{:S(2)}) %collective-permute-start.28) | collective-permute-done | bytes 114720 | tf_op jit(solution)/shard_map/ppermute | solution.py:394
  93.2 2.0 %collective-permute-done.31.refs_6_ = bf16[64,896]{1,0:T(8,128)(2,1)S(1)} collective-permute-done((bf16[64,896]{1,0:T(8,128)(2,1)S(1)}, bf16[64,896]{1,0:T(8,128)(2,1)S(1)}, u32[]{:S(2)}, u32[]{:S(2)}) %collective-permute-start.31) | collective-permute-done | bytes 114720 | tf_op jit(solution)/shard_map/ppermute | solution.py:394
  95.2 2.9 %collective-permute-done.32.refs_7_ = bf16[64,896]{1,0:T(8,128)(2,1)S(1)} collective-permute-done((bf16[64,896]{1,0:T(8,128)(2,1)S(1)}, bf16[64,896]{1,0:T(8,128)(2,1)S(1)}, u32[]{:S(2)}, u32[]{:S(2)}) %collective-permute-start.32) | collective-permute-done | bytes 114720 | tf_op jit(solution)/shard_map/ppermute | solution.py:394
  98.1 0.2 shard_map.106
  98.3 4.3 %collective-permute-start.33 = (bf16[2,64,448]{2,1,0:T(8,128)(2,1)S(1)}, bf16[2,64,448]{2,1,0:T(8,128)(2,1)S(1)}, u32[]{:S(2)}, u32[]{:S(2)}) collective-permute-start(bf16[2,64,448]{2,1,0:T(8,128)(2,1)S(1)} %get-tuple-element.91), channel_id=1, source_target_pairs={{0,0},{8,128},{128,8},{136,136},{1,1},{9,129},{129,9},{137,137},{2... | collective-permute-start | bytes 344072 | tf_op jit(solution)/shard_map/ppermute | solution.py:498
  102.6 0.1 collective-permute-start.34
  102.7 2.9 %collective-permute-done.33 = bf16[2,64,448]{2,1,0:T(8,128)(2,1)S(1)} collective-permute-done((bf16[2,64,448]{2,1,0:T(8,128)(2,1)S(1)}, bf16[2,64,448]{2,1,0:T(8,128)(2,1)S(1)}, u32[]{:S(2)}, u32[]{:S(2)}) %collective-permute-start.33) | collective-permute-done | bytes 114720 | tf_op jit(solution)/shard_map/ppermute | solution.py:498
  105.5 2.1 %collective-permute-done.34 = bf16[2,64,448]{2,1,0:T(8,128)(2,1)S(1)} collective-permute-done((bf16[2,64,448]{2,1,0:T(8,128)(2,1)S(1)}, bf16[2,64,448]{2,1,0:T(8,128)(2,1)S(1)}, u32[]{:S(2)}, u32[]{:S(2)}) %collective-permute-start.34) | collective-permute-done | bytes 114720 | tf_op jit(solution)/shard_map/ppermute | solution.py:499
  107.6 0.7 add_convert_fusion
  (37 shorter events, 0.1 us)
Async XLA Ops:
  0.0 27.9 %collective-permute-start.10 = (bf16[512,1024]{1,0:T(8,128)(2,1)}, bf16[512,1024]{1,0:T(8,128)(2,1)S(1)}, u32[]{:S(2)}, u32[]{:S(2)}) collective-permute-start(bf16[512,1024]{1,0:T(8,128)(2,1)} %refs_4_.1), channel_id=1, source_target_pairs={{0,1},{1,0},{2,3},{3,2},{4,5},{5,4},{6,7},{7,6},{8,9},{9,8},{10,11... | collective-permute-start | bytes 3145736 | tf_op jit(solution)/shard_map/ppermute | solution.py:373
  0.0 27.9 %collective-permute-start.6 = (bf16[512,1024]{1,0:T(8,128)(2,1)}, bf16[512,1024]{1,0:T(8,128)(2,1)S(1)}, u32[]{:S(2)}, u32[]{:S(2)}) collective-permute-start(bf16[512,1024]{1,0:T(8,128)(2,1)} %refs_3_.1), channel_id=1, source_target_pairs={{0,1},{1,0},{2,3},{3,2},{4,5},{5,4},{6,7},{7,6},{8,9},{9,8},{10,11... | collective-permute-start | bytes 3145736 | tf_op jit(solution)/shard_map/ppermute | solution.py:373
  1.6 10.8 %collective-permute-start.2 = (bf16[64,1536]{1,0:T(8,128)(2,1)S(1)}, bf16[64,1536]{1,0:T(8,128)(2,1)S(1)}, u32[]{:S(2)}, u32[]{:S(2)}) collective-permute-start(bf16[64,1536]{1,0:T(8,128)(2,1)S(1)} %get-tuple-element.50), channel_id=1, source_target_pairs={{0,1},{1,0},{2,3},{3,2},{4,5},{5,4},{6,7},{7,6},{8,9},{9,8},{10,11... | collective-permute-start | bytes 589832 | tf_op jit(solution)/shard_map/ppermute | solution.py:373
  1.7 10.7 %collective-permute-start = (bf16[128,576]{1,0:T(8,128)(2,1)S(1)}, bf16[128,576]{1,0:T(8,128)(2,1)S(1)}, u32[]{:S(2)}, u32[]{:S(2)}) collective-permute-start(bf16[128,576]{1,0:T(8,128)(2,1)S(1)} %get-tuple-element.49.refs_4_), channel_id=1, source_target_pairs={{0,16},{16,32},{32,48},{48,64},{64,80},{80,96},{96,112},{112,0},{1... | collective-permute-start | bytes 442376 | tf_op jit(solution)/shard_map/ppermute | solution.py:381
  3.7 8.7 %collective-permute-start.1 = (bf16[128,576]{1,0:T(8,128)(2,1)S(1)}, bf16[128,576]{1,0:T(8,128)(2,1)S(1)}, u32[]{:S(2)}, u32[]{:S(2)}) collective-permute-start(bf16[128,576]{1,0:T(8,128)(2,1)S(1)} %get-tuple-element.49.refs_4_), channel_id=1, source_target_pairs={{0,112},{16,0},{32,16},{48,32},{64,48},{80,64},{96,80},{112,96},{1... | collective-permute-start | bytes 442376 | tf_op jit(solution)/shard_map/ppermute | solution.py:381
  12.5 7.2 %collective-permute-start.3 = (bf16[128,576]{1,0:T(8,128)(2,1)S(1)}, bf16[128,576]{1,0:T(8,128)(2,1)S(1)}, u32[]{:S(2)}, u32[]{:S(2)}) collective-permute-start(bf16[128,576]{1,0:T(8,128)(2,1)S(1)} %get-tuple-element.51.refs_5_.refs_8_), channel_id=1, source_target_pairs={{0,16},{16,32},{32,48},{48,64},{64,80},{80,96},{96,112},{112,0},{1... | collective-permute-start | bytes 442376 | tf_op jit(solution)/shard_map/ppermute | solution.py:381
  12.6 7.1 %collective-permute-start.4 = (bf16[128,576]{1,0:T(8,128)(2,1)S(1)}, bf16[128,576]{1,0:T(8,128)(2,1)S(1)}, u32[]{:S(2)}, u32[]{:S(2)}) collective-permute-start(bf16[128,576]{1,0:T(8,128)(2,1)S(1)} %get-tuple-element.52.refs_7_), channel_id=1, source_target_pairs={{0,112},{16,0},{32,16},{48,32},{64,48},{80,64},{96,80},{112,96},{1... | collective-permute-start | bytes 442376 | tf_op jit(solution)/shard_map/ppermute | solution.py:381
  15.8 6.6 %collective-permute-start.9 = (bf16[64,1536]{1,0:T(8,128)(2,1)S(1)}, bf16[64,1536]{1,0:T(8,128)(2,1)S(1)}, u32[]{:S(2)}, u32[]{:S(2)}) collective-permute-start(bf16[64,1536]{1,0:T(8,128)(2,1)S(1)} %get-tuple-element.57.refs_1_), channel_id=1, source_target_pairs={{0,128},{128,0},{1,129},{129,1},{2,130},{130,2},{3,131},{131,3},{4... | collective-permute-start | bytes 589832 | tf_op jit(solution)/shard_map/ppermute | solution.py:373
  19.7 8.2 %collective-permute-start.5 = (bf16[64,1536]{1,0:T(8,128)(2,1)S(1)}, bf16[64,1536]{1,0:T(8,128)(2,1)S(1)}, u32[]{:S(2)}, u32[]{:S(2)}) collective-permute-start(bf16[64,1536]{1,0:T(8,128)(2,1)S(1)} %get-tuple-element.54.refs_1_), channel_id=1, source_target_pairs={{0,128},{128,0},{1,129},{129,1},{2,130},{130,2},{3,131},{131,3},{4... | collective-permute-start | bytes 589832 | tf_op jit(solution)/shard_map/ppermute | solution.py:373
  20.2 7.7 %collective-permute-start.7 = (bf16[128,576]{1,0:T(8,128)(2,1)S(1)}, bf16[128,576]{1,0:T(8,128)(2,1)S(1)}, u32[]{:S(2)}, u32[]{:S(2)}) collective-permute-start(bf16[128,576]{1,0:T(8,128)(2,1)S(1)} %get-tuple-element.55.refs_6_), channel_id=1, source_target_pairs={{0,16},{16,32},{32,48},{48,64},{64,80},{80,96},{96,112},{112,0},{1... | collective-permute-start | bytes 442376 | tf_op jit(solution)/shard_map/ppermute | solution.py:381
  22.4 5.5 %collective-permute-start.8 = (bf16[128,576]{1,0:T(8,128)(2,1)S(1)}, bf16[128,576]{1,0:T(8,128)(2,1)S(1)}, u32[]{:S(2)}, u32[]{:S(2)}) collective-permute-start(bf16[128,576]{1,0:T(8,128)(2,1)S(1)} %get-tuple-element.56.refs_5_), channel_id=1, source_target_pairs={{0,112},{16,0},{32,16},{48,32},{64,48},{80,64},{96,80},{112,96},{1... | collective-permute-start | bytes 442376 | tf_op jit(solution)/shard_map/ppermute | solution.py:381
  23.4 0.7 copy-start.2
  24.1 1.2 %copy-start.4 = (bf16[512,1024]{1,0:T(8,128)(2,1)S(1)}, bf16[512,1024]{1,0:T(8,128)(2,1)}, u32[]{:S(2)}) copy-start(bf16[512,1024]{1,0:T(8,128)(2,1)} %refs_3_.1) | copy-start | bytes 3145732
  27.9 11.1 %collective-permute-start.13 = (bf16[448,1024]{1,0:T(8,128)(2,1)S(1)}, bf16[448,1024]{1,0:T(8,128)(2,1)S(1)}, u32[]{:S(2)}, u32[]{:S(2)}) collective-permute-start(bf16[448,1024]{1,0:T(8,128)(2,1)S(1)} %get-tuple-element.68), channel_id=1, source_target_pairs={{0,1},{1,0},{2,3},{3,2},{4,5},{5,4},{6,7},{7,6},{8,9},{9,8},{10,11... | collective-permute-start | bytes 2752520 | tf_op jit(solution)/shard_map/ppermute | solution.py:373
  28.1 6.2 %collective-permute-start.11 = (bf16[64,576]{1,0:T(8,128)(2,1)S(1)}, bf16[64,576]{1,0:T(8,128)(2,1)S(1)}, u32[]{:S(2)}, u32[]{:S(2)}) collective-permute-start(bf16[64,576]{1,0:T(8,128)(2,1)S(1)} %slice.12), channel_id=1, source_target_pairs={{0,16},{16,32},{32,48},{48,64},{64,80},{80,96},{96,112},{112,0},{1... | collective-permute-start | bytes 221192 | tf_op jit(solution)/shard_map/ppermute | solution.py:381
  29.5 4.8 %copy-start = (bf16[512,1024]{1,0:T(8,128)(2,1)S(1)}, bf16[512,1024]{1,0:T(8,128)(2,1)}, u32[]{:S(2)}) copy-start(bf16[512,1024]{1,0:T(8,128)(2,1)} %refs_4_.1) | copy-start | bytes 3145732
  29.5 4.8 %collective-permute-start.12 = (bf16[64,576]{1,0:T(8,128)(2,1)S(1)}, bf16[64,576]{1,0:T(8,128)(2,1)S(1)}, u32[]{:S(2)}, u32[]{:S(2)}) collective-permute-start(bf16[64,576]{1,0:T(8,128)(2,1)S(1)} %slice.13), channel_id=1, source_target_pairs={{0,112},{16,0},{32,16},{48,32},{64,48},{80,64},{96,80},{112,96},{1... | collective-permute-start | bytes 221192 | tf_op jit(solution)/shard_map/ppermute | solution.py:381
  37.4 5.7 %collective-permute-start.15 = (bf16[64,1152]{1,0:T(8,128)(2,1)S(1)}, bf16[64,1152]{1,0:T(8,128)(2,1)S(1)}, u32[]{:S(2)}, u32[]{:S(2)}) collective-permute-start(bf16[64,1152]{1,0:T(8,128)(2,1)S(1)} %get-tuple-element.73), channel_id=1, source_target_pairs={{0,128},{128,0},{1,129},{129,1},{2,130},{130,2},{3,131},{131,3},{4... | collective-permute-start | bytes 442376 | tf_op jit(solution)/shard_map/ppermute | solution.py:373
  39.1 4.0 %copy-start.3 = (s32[2]{0:T(128)S(1)}, s32[2]{0:T(128)}, u32[]{:S(2)}) copy-start(s32[2]{0:T(128)} %lens.3) | copy-start | bytes 28
  39.1 8.5 %copy-start.1 = (bf16[1024,448]{0,1:T(8,128)(2,1)S(1)}, bf16[1024,448]{0,1:T(8,128)(2,1)}, u32[]{:S(2)}) copy-start(bf16[1024,448]{0,1:T(8,128)(2,1)} %param.15) | copy-start | bytes 2752516
  42.1 5.4 %collective-permute-start.14 = (bf16[64,1152]{1,0:T(8,128)(2,1)S(1)}, bf16[64,1152]{1,0:T(8,128)(2,1)S(1)}, u32[]{:S(2)}, u32[]{:S(2)}) collective-permute-start(bf16[64,1152]{1,0:T(8,128)(2,1)S(1)} %get-tuple-element.71), channel_id=1, source_target_pairs={{0,128},{128,0},{1,129},{129,1},{2,130},{130,2},{3,131},{131,3},{4... | collective-permute-start | bytes 442376 | tf_op jit(solution)/shard_map/ppermute | solution.py:373
  48.6 25.3 %collective-permute-start.22 = (bf16[448,1024]{1,0:T(8,128)(2,1)S(1)}, bf16[448,1024]{1,0:T(8,128)(2,1)S(1)}, u32[]{:S(2)}, u32[]{:S(2)}) collective-permute-start(bf16[448,1024]{1,0:T(8,128)(2,1)S(1)} %get-tuple-element.79.refs_5_.refs_4_), channel_id=1, source_target_pairs={{0,128},{128,0},{1,129},{129,1},{2,130},{130,2},{3,131},{131,3},{4... | collective-permute-start | bytes 2752520 | tf_op jit(solution)/shard_map/ppermute | solution.py:373
  49.2 7.8 %collective-permute-start.16 = (bf16[64,2048]{1,0:T(8,128)(2,1)S(1)}, bf16[64,2048]{1,0:T(8,128)(2,1)S(1)}, u32[]{:S(2)}, u32[]{:S(2)}) collective-permute-start(bf16[64,2048]{1,0:T(8,128)(2,1)S(1)} %get-tuple-element.74.refs_0_), channel_id=1, source_target_pairs={{0,16},{16,32},{32,48},{48,64},{64,80},{80,96},{96,112},{112,0},{1... | collective-permute-start | bytes 786440 | tf_op jit(solution)/shard_map/ppermute | solution.py:381
  50.7 6.4 %collective-permute-start.17 = (bf16[64,2048]{1,0:T(8,128)(2,1)S(1)}, bf16[64,2048]{1,0:T(8,128)(2,1)S(1)}, u32[]{:S(2)}, u32[]{:S(2)}) collective-permute-start(bf16[64,2048]{1,0:T(8,128)(2,1)S(1)} %get-tuple-element.74.refs_0_), channel_id=1, source_target_pairs={{0,112},{16,0},{32,16},{48,32},{64,48},{80,64},{96,80},{112,96},{1... | collective-permute-start | bytes 786440 | tf_op jit(solution)/shard_map/ppermute | solution.py:381
  57.1 7.6 %collective-permute-start.18 = (bf16[64,2048]{1,0:T(8,128)(2,1)S(1)}, bf16[64,2048]{1,0:T(8,128)(2,1)S(1)}, u32[]{:S(2)}, u32[]{:S(2)}) collective-permute-start(bf16[64,2048]{1,0:T(8,128)(2,1)S(1)} %get-tuple-element.75.refs_1_), channel_id=1, source_target_pairs={{0,16},{16,32},{32,48},{48,64},{64,80},{80,96},{96,112},{112,0},{1... | collective-permute-start | bytes 786440 | tf_op jit(solution)/shard_map/ppermute | solution.py:381
  59.0 6.4 %collective-permute-start.19 = (bf16[64,2048]{1,0:T(8,128)(2,1)S(1)}, bf16[64,2048]{1,0:T(8,128)(2,1)S(1)}, u32[]{:S(2)}, u32[]{:S(2)}) collective-permute-start(bf16[64,2048]{1,0:T(8,128)(2,1)S(1)} %get-tuple-element.76.refs_3_), channel_id=1, source_target_pairs={{0,112},{16,0},{32,16},{48,32},{64,48},{80,64},{96,80},{112,96},{1... | collective-permute-start | bytes 786440 | tf_op jit(solution)/shard_map/ppermute | solution.py:381
  65.4 7.6 %collective-permute-start.20 = (bf16[64,2048]{1,0:T(8,128)(2,1)S(1)}, bf16[64,2048]{1,0:T(8,128)(2,1)S(1)}, u32[]{:S(2)}, u32[]{:S(2)}) collective-permute-start(bf16[64,2048]{1,0:T(8,128)(2,1)S(1)} %get-tuple-element.77.refs_2_), channel_id=1, source_target_pairs={{0,16},{16,32},{32,48},{48,64},{64,80},{80,96},{96,112},{112,0},{1... | collective-permute-start | bytes 786440 | tf_op jit(solution)/shard_map/ppermute | solution.py:381
  67.6 6.4 %collective-permute-start.21 = (bf16[64,2048]{1,0:T(8,128)(2,1)S(1)}, bf16[64,2048]{1,0:T(8,128)(2,1)S(1)}, u32[]{:S(2)}, u32[]{:S(2)}) collective-permute-start(bf16[64,2048]{1,0:T(8,128)(2,1)S(1)} %get-tuple-element.78.refs_4_), channel_id=1, source_target_pairs={{0,112},{16,0},{32,16},{48,32},{64,48},{80,64},{96,80},{112,96},{1... | collective-permute-start | bytes 786440 | tf_op jit(solution)/shard_map/ppermute | solution.py:381
  73.9 3.4 %collective-permute-start.25 = (bf16[448,1024]{1,0:T(8,128)(2,1)S(1)}, bf16[448,1024]{1,0:T(8,128)(2,1)S(1)}, u32[]{:S(2)}, u32[]{:S(2)}) collective-permute-start(bf16[448,1024]{1,0:T(8,128)(2,1)S(1)} %get-tuple-element.82.refs_6_.refs_5_), channel_id=1, source_target_pairs={{0,1},{1,0},{2,3},{3,2},{4,5},{5,4},{6,7},{7,6},{8,9},{9,8},{10,11... | collective-permute-start | bytes 2752520 | tf_op jit(solution)/shard_map/ppermute | solution.py:373
  74.0 7.2 %collective-permute-start.23 = (bf16[32,2048]{1,0:T(8,128)(2,1)S(1)}, bf16[32,2048]{1,0:T(8,128)(2,1)S(1)}, u32[]{:S(2)}, u32[]{:S(2)}) collective-permute-start(bf16[32,2048]{1,0:T(8,128)(2,1)S(1)} %slice.14), channel_id=1, source_target_pairs={{0,16},{16,32},{32,48},{48,64},{64,80},{80,96},{96,112},{112,0},{1... | collective-permute-start | bytes 393224 | tf_op jit(solution)/shard_map/ppermute | solution.py:381
  75.5 5.7 %collective-permute-start.24 = (bf16[32,2048]{1,0:T(8,128)(2,1)S(1)}, bf16[32,2048]{1,0:T(8,128)(2,1)S(1)}, u32[]{:S(2)}, u32[]{:S(2)}) collective-permute-start(bf16[32,2048]{1,0:T(8,128)(2,1)S(1)} %slice.15), channel_id=1, source_target_pairs={{0,112},{16,0},{32,16},{48,32},{64,48},{80,64},{96,80},{112,96},{1... | collective-permute-start | bytes 393224 | tf_op jit(solution)/shard_map/ppermute | solution.py:381
  82.6 5.8 %collective-permute-start.26 = (bf16[64,896]{1,0:T(8,128)(2,1)S(1)}, bf16[64,896]{1,0:T(8,128)(2,1)S(1)}, u32[]{:S(2)}, u32[]{:S(2)}) collective-permute-start(bf16[64,896]{1,0:T(8,128)(2,1)S(1)} %get-tuple-element.84), channel_id=1, source_target_pairs={{0,2},{1,3},{2,0},{3,1},{4,6},{5,7},{6,4},{7,5},{8,10},{9,11},{10,... | collective-permute-start | bytes 344072 | tf_op jit(solution)/shard_map/ppermute | solution.py:394
  84.1 7.8 %collective-permute-start.27 = (bf16[64,896]{1,0:T(8,128)(2,1)S(1)}, bf16[64,896]{1,0:T(8,128)(2,1)S(1)}, u32[]{:S(2)}, u32[]{:S(2)}) collective-permute-start(bf16[64,896]{1,0:T(8,128)(2,1)S(1)} %get-tuple-element.85), channel_id=1, source_target_pairs={{0,6},{1,7},{2,4},{3,5},{4,2},{5,3},{6,0},{7,1},{8,14},{9,15},{10,... | collective-permute-start | bytes 344072 | tf_op jit(solution)/shard_map/ppermute | solution.py:394
  86.2 7.0 %collective-permute-start.28 = (bf16[64,896]{1,0:T(8,128)(2,1)S(1)}, bf16[64,896]{1,0:T(8,128)(2,1)S(1)}, u32[]{:S(2)}, u32[]{:S(2)}) collective-permute-start(bf16[64,896]{1,0:T(8,128)(2,1)S(1)} %get-tuple-element.86), channel_id=1, source_target_pairs={{0,4},{1,5},{2,6},{3,7},{4,0},{5,1},{6,2},{7,3},{8,12},{9,13},{10,... | collective-permute-start | bytes 344072 | tf_op jit(solution)/shard_map/ppermute | solution.py:394
  86.9 6.3 %collective-permute-start.29 = (bf16[64,896]{1,0:T(8,128)(2,1)S(1)}, bf16[64,896]{1,0:T(8,128)(2,1)S(1)}, u32[]{:S(2)}, u32[]{:S(2)}) collective-permute-start(bf16[64,896]{1,0:T(8,128)(2,1)S(1)} %get-tuple-element.87), channel_id=1, source_target_pairs={{0,1},{1,0},{2,3},{3,2},{4,5},{5,4},{6,7},{7,6},{8,9},{9,8},{10,11... | collective-permute-start | bytes 344072 | tf_op jit(solution)/shard_map/ppermute | solution.py:373
  86.9 6.3 %collective-permute-start.30 = (bf16[64,896]{1,0:T(8,128)(2,1)S(1)}, bf16[64,896]{1,0:T(8,128)(2,1)S(1)}, u32[]{:S(2)}, u32[]{:S(2)}) collective-permute-start(bf16[64,896]{1,0:T(8,128)(2,1)S(1)} %get-tuple-element.88), channel_id=1, source_target_pairs={{0,3},{1,2},{2,1},{3,0},{4,7},{5,6},{6,5},{7,4},{8,11},{9,10},{10,... | collective-permute-start | bytes 344072 | tf_op jit(solution)/shard_map/ppermute | solution.py:394
  88.3 6.9 %collective-permute-start.31 = (bf16[64,896]{1,0:T(8,128)(2,1)S(1)}, bf16[64,896]{1,0:T(8,128)(2,1)S(1)}, u32[]{:S(2)}, u32[]{:S(2)}) collective-permute-start(bf16[64,896]{1,0:T(8,128)(2,1)S(1)} %get-tuple-element.89), channel_id=1, source_target_pairs={{0,7},{1,6},{2,5},{3,4},{4,3},{5,2},{6,1},{7,0},{8,15},{9,14},{10,... | collective-permute-start | bytes 344072 | tf_op jit(solution)/shard_map/ppermute | solution.py:394
  92.0 6.1 %collective-permute-start.32 = (bf16[64,896]{1,0:T(8,128)(2,1)S(1)}, bf16[64,896]{1,0:T(8,128)(2,1)S(1)}, u32[]{:S(2)}, u32[]{:S(2)}) collective-permute-start(bf16[64,896]{1,0:T(8,128)(2,1)S(1)} %get-tuple-element.90), channel_id=1, source_target_pairs={{0,5},{1,4},{2,7},{3,6},{4,1},{5,0},{6,3},{7,2},{8,13},{9,12},{10,... | collective-permute-start | bytes 344072 | tf_op jit(solution)/shard_map/ppermute | solution.py:394
  98.3 7.2 %collective-permute-start.33 = (bf16[2,64,448]{2,1,0:T(8,128)(2,1)S(1)}, bf16[2,64,448]{2,1,0:T(8,128)(2,1)S(1)}, u32[]{:S(2)}, u32[]{:S(2)}) collective-permute-start(bf16[2,64,448]{2,1,0:T(8,128)(2,1)S(1)} %get-tuple-element.91), channel_id=1, source_target_pairs={{0,0},{8,128},{128,8},{136,136},{1,1},{9,129},{129,9},{137,137},{2... | collective-permute-start | bytes 344072 | tf_op jit(solution)/shard_map/ppermute | solution.py:498
  102.6 5.0 %collective-permute-start.34 = (bf16[2,64,448]{2,1,0:T(8,128)(2,1)S(1)}, bf16[2,64,448]{2,1,0:T(8,128)(2,1)S(1)}, u32[]{:S(2)}, u32[]{:S(2)}) collective-permute-start(bf16[2,64,448]{2,1,0:T(8,128)(2,1)S(1)} %get-tuple-element.92), channel_id=1, source_target_pairs={{0,128},{128,136},{8,0},{136,8},{1,129},{129,137},{9,1},{137,9},{2... | collective-permute-start | bytes 344072 | tf_op jit(solution)/shard_map/ppermute | solution.py:499

commit v5 on v4

--- a/solution.py
+++ b/solution.py
@@ -275,8 +275,7 @@
     )(starts, lens, *held_in_vmem(own, lse, got, before), weights)
 
 
-NEAR = (0, 1, 2, 7, 6)
-FAR = (3, 5, 4)
+NEAR = (0, 1, 2, 3, 5, 6, 7)
 
 
 def products(pieces, weights, held):
@@ -296,21 +295,18 @@
     ).astype(bf16)
 
 
-def near_kernel(*refs):
+def near_kernel(rows, *refs):
     count = len(NEAR)
     out, held = refs[-2:]
-    out[...] = products(refs[:count], refs[count : count + 4], held)
+    both = products(refs[:count], refs[count : count + 4], held)
+    out[: 4 * rows, :] = both[: 4 * rows]
+    out[5 * rows :, :] = both[4 * rows :]
 
 
 def far_kernel(rows, *refs):
-    near = refs[8]
-    outs = refs[9:17]
-    held, full = refs[17:]
-    both = products(refs[:4], refs[4:8], held)
-    for place, slot in enumerate(FAR):
-        full[slot * rows : (slot + 1) * rows, :] = both[place * rows : (place + 1) * rows]
-    for place, slot in enumerate(NEAR):
-        full[slot * rows : (slot + 1) * rows, :] = near[place * rows : (place + 1) * rows, :]
+    outs = refs[7:15]
+    full, held = refs[15:]
+    full[4 * rows : 5 * rows, :] = products(refs[:2], refs[2:6], held)
     z, core, x = (lax.axis_index(name) for name in ("z", "core", "x"))
     odd = x & 1
     partners = (x, x + 1 - 2 * odd, (x - 1 + 2 * odd) & 3, (x + 2) & 3)
@@ -325,8 +321,8 @@
     cols = weights[0].shape[0]
     count = len(NEAR)
     return pl.pallas_call(
-        near_kernel,
-        out_shape=pltpu.VMEM((count * rows, 2 * cols), bf16),
+        functools.partial(near_kernel, rows),
+        out_shape=pltpu.VMEM((8 * rows, 2 * cols), bf16),
         in_specs=[VMEM] * (count + 4),
         out_specs=VMEM,
         scratch_shapes=[pltpu.VMEM((count * rows, wide), bf16)],
@@ -336,20 +332,19 @@
 
 
 def project_far(pieces, weights, near):
-    rows, wide = pieces[0].shape
+    wide = pieces[0].shape[1]
     cols = weights[0].shape[0]
-    count = len(FAR)
+    rows = near.shape[0] // 8
+    block = pltpu.VMEM((rows, 2 * cols), bf16)
     return pl.pallas_call(
         functools.partial(far_kernel, rows),
-        out_shape=(pltpu.VMEM((rows, 2 * cols), bf16),) * 8,
-        in_specs=[VMEM] * 9,
-        out_specs=(VMEM,) * 8,
-        scratch_shapes=[
-            pltpu.VMEM((count * rows, wide), bf16),
-            pltpu.VMEM((8 * rows, 2 * cols), bf16),
-        ],
+        out_shape=(block,) * 8 + (pltpu.VMEM(near.shape, bf16),),
+        in_specs=[VMEM] * 7,
+        out_specs=(VMEM,) * 9,
+        scratch_shapes=[pltpu.VMEM((rows, wide), bf16)],
+        input_output_aliases={6: 8},
         compiler_params=params(12),
-        cost_estimate=cost(4 * count * rows * wide * cols),
+        cost_estimate=cost(4 * rows * wide * cols),
     )(*held_in_vmem(*pieces, *weights, near))
 
 
@@ -394,7 +389,7 @@
     return lax.ppermute(x, ("x", "core"), moves)
 
 
-def pack_kernel(q_nope, q_rope, cache, stretch, latent, q_own, q_sent, sems):
+def pack_kernel(q_nope, q_rope, cache, stretch, w, latent, q_own, q_sent, w_near, sems):
     core = lax.axis_index("core")
     rows, wide = q_nope.shape[1:]
     moves = [
@@ -404,6 +399,7 @@
         (q_rope.at[core], q_own.at[:, wide:]),
         (q_nope.at[1 - core], q_sent.at[:, :wide]),
         (q_rope.at[1 - core], q_sent.at[:, wide:]),
+        (w, w_near),
     ]
     copies = [pltpu.make_async_copy(a, b, sems.at[i]) for i, (a, b) in enumerate(moves)]
     for copy in copies:
@@ -412,7 +408,7 @@
         copy.wait()
 
 
-def pack(q_nope, q_rope, cache, stretch):
+def pack(q_nope, q_rope, cache, stretch, w):
     rows, width = cache.shape[1:]
     wide = q_nope.shape[2] + q_rope.shape[2]
     return pl.pallas_call(
@@ -421,12 +417,13 @@
             pltpu.VMEM((2 * rows, width), bf16),
             pltpu.VMEM((rows, wide), bf16),
             pltpu.VMEM((rows, wide), bf16),
+            pltpu.VMEM(w.shape, bf16),
         ),
-        in_specs=[ANY] * 4,
-        out_specs=(ANY,) * 3,
-        scratch_shapes=[pltpu.SemaphoreType.DMA((6,))],
+        in_specs=[ANY] * 5,
+        out_specs=(ANY,) * 4,
+        scratch_shapes=[pltpu.SemaphoreType.DMA((7,))],
         compiler_params=params(1),
-    )(*in_hbm(q_nope, q_rope, cache, stretch))
+    )(*in_hbm(q_nope, q_rope, cache, stretch, w))
 
 
 def sum_kernel(*refs):
@@ -457,18 +454,20 @@
 
 def local(q_nope, q_rope, cache_latent, stretch_latent, w_uk, w_uv, w_o, stretch_start, prompt_len):
     half = 8 * q_nope.shape[1]
-    latent, q_own, q_sent = pack(q_nope, q_rope, cache_latent, stretch_latent)
+    latent, q_own, q_sent, w_uk_near = pack(
+        q_nope, q_rope, cache_latent, stretch_latent, w_uk
+    )
     q_own_y = swap(q_own, "yl")
     q_got = swap(q_sent, "core")
     u1, d1, q_got = level((*step(latent, latent), q_got))
-    u2, d2, q_got = level((*step(u1, d1), q_got))
+    u2, d2 = level(step(u1, d1))
     q_got_y = swap(q_got, "yl")
     w_uk2 = swap(w_uk, "core")
     w_uv2 = swap(w_uv, "core")
     near = [latent, u1, u2, d1]
     near_at, far_at = (0, 1, 2, 7), (6, 3, 5, 4)
     *a1, w_t = attention_first(
-        stretch_start, q_own, q_own_y, w_uk, near, near_at, half, u1, w_o.T
+        stretch_start, q_own, q_own_y, w_uk_near, near, near_at, half, u1, w_o.T
     )
     u3, d3, w_t = level((*step(u2, d2), w_t), (q_got_y, w_uk2, w_uv2, a1[2]))
     w_t_c = swap(w_t, "core")
@@ -488,8 +487,8 @@
     u3, d3, w_t_y = level((*step(u2, d2), w_t_y))
     w_t_cy = swap(w_t_y, "core")
     weights = (w_t, w_t_y, w_t_c, w_t_cy)
-    near = project_near([attention, u1, u2, d1, d2], weights)
-    parts = project_far([u3, d3, *last(u3, d3)], weights, near)
+    near = project_near([attention, u1, u2, u3, d3, d2, d1], weights)
+    parts = project_far(last(u3, d3), weights, near)
 
     other_seq = [swap(parts[1], "core")]
     other_seq += [to_partner(parts[2 * k + 3], X_PAIRS[k], 1) for k in range(3)]

time: 108 us -> 108 us (level)
  local copies, waits for them, and re-layouts: 1.93 us -> 0.05 us
    unnamed x10 -> x8, local copies, waits for them, and re-layouts: 1.89 us -> 0.02 us
  transfers between devices with their start and end apart: 35 -> 35, of which waited for: 19 -> 18; matrix products, arithmetic and copies ran while one was open for 0% -> 0% of each run, Pallas kernels for 14% -> 15%
where the time goes in v5:
time: 108 us
  starting transfers between devices  45.5 us (42%)
  waiting for transfers between devices  42.9 us (40%)
  Pallas kernels  18.4 us (17%)
    ppermute x16, starting transfers between devices, step(): return (lax.ppermute(a, 'z', UP), lax.ppermute(b, 'z', DOWN))  29.4 us
    ppermute x16, waiting for transfers between devices, step(): return (lax.ppermute(a, 'z', UP), lax.ppermute(b, 'z', DOWN))  26.1 us
    ppermute x6, waiting for transfers between devices, to_partner(): return lax.ppermute(x, ('x', 'core'), moves)  8.06 us
    ppermute x6, starting transfers between devices, to_partner(): return lax.ppermute(x, ('x', 'core'), moves)  7.49 us
    pallas_call x2, Pallas kernels, attention_second(): pl.pallas_call(functools.partial(second_kernel, rows, heads, half, slots)...  6.09 us
    pallas_call x2, Pallas kernels, attention_first(): pl.pallas_call(functools.partial(first_kernel, rows, heads, half, slots),...  5.17 us
    ppermute x11, starting transfers between devices, swap(): return lax.ppermute(x, axis, [(0, 1), (1, 0)])  4.7 us
    ppermute x1, starting transfers between devices, local(): first = lax.ppermute(first, ('yl', 'yh'), [(0, 0), (1, 2), (2, 1), (3, 3)])  3.84 us
  transfers between devices with their start and end apart: 35, of which 18 were waited for; matrix products, arithmetic and copies ran while one was open for 0% of the time, Pallas kernels for 15%

profile of v5, /device:TPU:8, one launch (start us, length us, event | category | flops | bytes accessed | tf_op | source)
XLA Modules:
  0.0 107.7 jit_solution(4731834783342217129)
XLA Ops:
  0.0 0.5 collective-permute-start.4
  0.5 1.6 %shard_map.91 = (bf16[128,576]{1,0:T(8,128)(2,1)S(1)}, bf16[64,1536]{1,0:T(8,128)(2,1)S(1)}, bf16[64,1536]{1,0:T(8,128)(2,1)S(1)}, bf16[512,1024]{1,0:T(8,128)(2,1)S(1)}) custom-call(bf16[2,64,1024]{2,1,0:T(8,128)(2,1)} %q_nope.1, bf16[2,64,512]{2,1,0:T(8,128)(2,1)} %q_rope.1, bf16[2,64,576]{2,1,0:T(8,128)(2,1)} %cache.1, bf16[2,64,576]{2,1,0:T(8,128)(2,1)} %stretch.1, ...), custom_call_target="tpu_custom_call" | custom-call | tf_op jit(solution)/shard_map/pallas_call | solution.py:414
  2.1 0.2 collective-permute-start.2
  2.3 1.9 %collective-permute-start = (bf16[128,576]{1,0:T(8,128)(2,1)S(1)}, bf16[128,576]{1,0:T(8,128)(2,1)S(1)}, u32[]{:S(2)}, u32[]{:S(2)}) collective-permute-start(bf16[128,576]{1,0:T(8,128)(2,1)S(1)} %get-tuple-element.49.refs_4_), channel_id=1, source_target_pairs={{0,16},{16,32},{32,48},{48,64},{64,80},{80,96},{96,112},{112,0},{1... | collective-permute-start | bytes 442376 | tf_op jit(solution)/shard_map/ppermute | solution.py:376
  4.2 4.0 %collective-permute-start.1 = (bf16[128,576]{1,0:T(8,128)(2,1)S(1)}, bf16[128,576]{1,0:T(8,128)(2,1)S(1)}, u32[]{:S(2)}, u32[]{:S(2)}) collective-permute-start(bf16[128,576]{1,0:T(8,128)(2,1)S(1)} %get-tuple-element.49.refs_4_), channel_id=1, source_target_pairs={{0,112},{16,0},{32,16},{48,32},{64,48},{80,64},{96,80},{112,96},{1... | collective-permute-start | bytes 442376 | tf_op jit(solution)/shard_map/ppermute | solution.py:376
  8.2 4.7 %collective-permute-done.refs_0_ = bf16[128,576]{1,0:T(8,128)(2,1)S(1)} collective-permute-done((bf16[128,576]{1,0:T(8,128)(2,1)S(1)}, bf16[128,576]{1,0:T(8,128)(2,1)S(1)}, u32[]{:S(2)}, u32[]{:S(2)}) %collective-permute-start) | collective-permute-done | bytes 147488 | tf_op jit(solution)/shard_map/ppermute | solution.py:376
  12.9 0.0 collective-permute-done.1.refs_1_
  12.9 0.0 collective-permute-done.2.refs_2_
  12.9 0.1 collective-permute-start.5
  13.0 0.5 collective-permute-start.9
  13.5 3.1 %collective-permute-start.6 = (bf16[128,576]{1,0:T(8,128)(2,1)S(1)}, bf16[128,576]{1,0:T(8,128)(2,1)S(1)}, u32[]{:S(2)}, u32[]{:S(2)}) collective-permute-start(bf16[128,576]{1,0:T(8,128)(2,1)S(1)} %get-tuple-element.53.refs_7_), channel_id=1, source_target_pairs={{0,112},{16,0},{32,16},{48,32},{64,48},{80,64},{96,80},{112,96},{1... | collective-permute-start | bytes 442376 | tf_op jit(solution)/shard_map/ppermute | solution.py:376
  16.7 3.5 %collective-permute-done.5.refs_0_ = bf16[128,576]{1,0:T(8,128)(2,1)S(1)} collective-permute-done((bf16[128,576]{1,0:T(8,128)(2,1)S(1)}, bf16[128,576]{1,0:T(8,128)(2,1)S(1)}, u32[]{:S(2)}, u32[]{:S(2)}) %collective-permute-start.5) | collective-permute-done | bytes 147488 | tf_op jit(solution)/shard_map/ppermute | solution.py:376
  20.1 0.4 collective-permute-start.3
  20.6 1.8 %collective-permute-start.7 = (bf16[128,576]{1,0:T(8,128)(2,1)S(1)}, bf16[128,576]{1,0:T(8,128)(2,1)S(1)}, u32[]{:S(2)}, u32[]{:S(2)}) collective-permute-start(bf16[128,576]{1,0:T(8,128)(2,1)S(1)} %get-tuple-element.54.refs_6_), channel_id=1, source_target_pairs={{0,16},{16,32},{32,48},{48,64},{64,80},{80,96},{96,112},{112,0},{1... | collective-permute-start | bytes 442376 | tf_op jit(solution)/shard_map/ppermute | solution.py:376
  22.4 1.5 %collective-permute-start.8 = (bf16[128,576]{1,0:T(8,128)(2,1)S(1)}, bf16[128,576]{1,0:T(8,128)(2,1)S(1)}, u32[]{:S(2)}, u32[]{:S(2)}) collective-permute-start(bf16[128,576]{1,0:T(8,128)(2,1)S(1)} %get-tuple-element.55.refs_5_), channel_id=1, source_target_pairs={{0,112},{16,0},{32,16},{48,32},{64,48},{80,64},{96,80},{112,96},{1... | collective-permute-start | bytes 442376 | tf_op jit(solution)/shard_map/ppermute | solution.py:376
  23.8 2.6 %shard_map.94 = (bf16[1024,640]{1,0:T(8,128)(2,1)S(1)}, f32[1024,512]{1,0:T(8,128)S(1)}, f32[1024,256]{1,0:T(8,128)S(1)}, bf16[448,1024]{1,0:T(8,128)(2,1)S(1)}) custom-call(s32[2]{0:T(128)S(1)} %copy-done.2, bf16[64,1536]{1,0:T(8,128)(2,1)S(1)} %get-tuple-element.56.refs_1_, bf16[64,1536]{1,0:T(8,128)(2,1)S(1)} %collective-permute-done.9.refs_2_, ...), custom_call_target="tpu_custom_call" | custom-call | flops 1207959552 | bytes 4194304 | tf_op jit(solution)/shard_map/pallas_call | solution.py:178
  26.5 0.7 collective-permute-done.7.refs_0_
  27.1 0.6 collective-permute-done.8.refs_1_
  27.7 0.1 collective-permute-start.13
  27.8 2.1 %collective-permute-start.11 = (bf16[64,576]{1,0:T(8,128)(2,1)S(1)}, bf16[64,576]{1,0:T(8,128)(2,1)S(1)}, u32[]{:S(2)}, u32[]{:S(2)}) collective-permute-start(bf16[64,576]{1,0:T(8,128)(2,1)S(1)} %slice.12), channel_id=1, source_target_pairs={{0,16},{16,32},{32,48},{48,64},{64,80},{80,96},{96,112},{112,0},{1... | collective-permute-start | bytes 221192 | tf_op jit(solution)/shard_map/ppermute | solution.py:376
  29.9 0.0 copy-start
  29.9 1.5 %collective-permute-start.12 = (bf16[64,576]{1,0:T(8,128)(2,1)S(1)}, bf16[64,576]{1,0:T(8,128)(2,1)S(1)}, u32[]{:S(2)}, u32[]{:S(2)}) collective-permute-start(bf16[64,576]{1,0:T(8,128)(2,1)S(1)} %slice.13), channel_id=1, source_target_pairs={{0,112},{16,0},{32,16},{48,32},{64,48},{80,64},{96,80},{112,96},{1... | collective-permute-start | bytes 221192 | tf_op jit(solution)/shard_map/ppermute | solution.py:376
  31.4 2.6 %shard_map.96 = (bf16[1024,640]{1,0:T(8,128)(2,1)S(1)}, f32[1024,512]{1,0:T(8,128)S(1)}, f32[1024,256]{1,0:T(8,128)S(1)}) custom-call(s32[2]{0:T(128)S(1)} %copy-done.2, bf16[64,1536]{1,0:T(8,128)(2,1)S(1)} %get-tuple-element.51.refs_1_, bf16[64,1536]{1,0:T(8,128)(2,1)S(1)} %collective-permute-done.3.refs_3_.refs_2_, ...), custom_call_target="tpu_custom_call" | custom-call | flops 1207959552 | bytes 4194304 | tf_op jit(solution)/shard_map/pallas_call | solution.py:178
  34.0 0.9 collective-permute-done.12.refs_9_
  34.9 3.0 %shard_map.97 = (f32[64,1024]{1,0:T(8,128)S(1)}, f32[64,128]{1,0:T(8,128)S(1)}, bf16[64,1152]{1,0:T(8,128)(2,1)S(1)}) custom-call(s32[2]{0:T(128)S(1)} %copy-done.2, bf16[1024,640]{1,0:T(8,128)(2,1)S(1)} %get-tuple-element.65.refs_1_, f32[1024,512]{1,0:T(8,128)S(1)} %get-tuple-element.66.refs_2_, f32[1024,256]{1,0:T(8,128)S(1)} %get-tuple-element.59.refs_6_.refs_3_, ...), custom_call_target="tpu_custom_call" | custom-call | flops 1207959552 | bytes 4194304 | tf_op jit(solution)/shard_map/pallas_call | solution.py:204
  37.9 1.5 %collective-permute-start.15 = (bf16[64,1152]{1,0:T(8,128)(2,1)S(1)}, bf16[64,1152]{1,0:T(8,128)(2,1)S(1)}, u32[]{:S(2)}, u32[]{:S(2)}) collective-permute-start(bf16[64,1152]{1,0:T(8,128)(2,1)S(1)} %get-tuple-element.73), channel_id=1, source_target_pairs={{0,128},{128,0},{1,129},{129,1},{2,130},{130,2},{3,131},{131,3},{4... | collective-permute-start | bytes 442376 | tf_op jit(solution)/shard_map/ppermute | solution.py:368
  39.5 3.0 %shard_map.98 = (f32[64,1024]{1,0:T(8,128)S(1)}, f32[64,128]{1,0:T(8,128)S(1)}, bf16[64,1152]{1,0:T(8,128)(2,1)S(1)}) custom-call(s32[2]{0:T(128)S(1)} %copy-done.2, bf16[1024,640]{1,0:T(8,128)(2,1)S(1)} %get-tuple-element.61.refs_1_, f32[1024,512]{1,0:T(8,128)S(1)} %get-tuple-element.62.refs_2_, f32[1024,256]{1,0:T(8,128)S(1)} %get-tuple-element.63.refs_10_.refs_3_, ...), custom_call_target="tpu_custom_call" | custom-call | flops 1207959552 | bytes 4194304 | tf_op jit(solution)/shard_map/pallas_call | solution.py:204
  42.5 0.7 collective-permute-start.14
  43.2 0.1 collective-permute-done.15.got
  43.3 0.8 shard_map.99.refs_0_
  44.1 3.6 %collective-permute-done.14.got = bf16[64,1152]{1,0:T(8,128)(2,1)S(1)} collective-permute-done((bf16[64,1152]{1,0:T(8,128)(2,1)S(1)}, bf16[64,1152]{1,0:T(8,128)(2,1)S(1)}, u32[]{:S(2)}, u32[]{:S(2)}) %collective-permute-start.14) | collective-permute-done | bytes 147488 | tf_op jit(solution)/shard_map/ppermute | solution.py:368
  47.8 1.1 %shard_map.100 = (bf16[64,2048]{1,0:T(8,128)(2,1)S(1)}, bf16[448,1024]{1,0:T(8,128)(2,1)S(1)}) custom-call(s32[2]{0:T(128)S(1)} %copy-done.2, s32[2]{0:T(128)S(1)} %copy-done.3, f32[64,1024]{1,0:T(8,128)S(1)} %get-tuple-element.69.own, f32[64,128]{1,0:T(8,128)S(1)} %get-tuple-element.70.refs_0_.lse, ...), custom_call_target="tpu_custom_call", output_to_operand_aliasing={{0}: (5, {})} | custom-call | flops 524288 | bytes 4194304 | tf_op jit(solution)/shard_map/pallas_call | solution.py:263
  48.9 0.7 collective-permute-start.22
  49.5 1.7 %collective-permute-start.16 = (bf16[64,2048]{1,0:T(8,128)(2,1)S(1)}, bf16[64,2048]{1,0:T(8,128)(2,1)S(1)}, u32[]{:S(2)}, u32[]{:S(2)}) collective-permute-start(bf16[64,2048]{1,0:T(8,128)(2,1)S(1)} %get-tuple-element.74.refs_0_), channel_id=1, source_target_pairs={{0,16},{16,32},{32,48},{48,64},{64,80},{80,96},{96,112},{112,0},{1... | collective-permute-start | bytes 786440 | tf_op jit(solution)/shard_map/ppermute | solution.py:376
  51.3 1.5 %collective-permute-start.17 = (bf16[64,2048]{1,0:T(8,128)(2,1)S(1)}, bf16[64,2048]{1,0:T(8,128)(2,1)S(1)}, u32[]{:S(2)}, u32[]{:S(2)}) collective-permute-start(bf16[64,2048]{1,0:T(8,128)(2,1)S(1)} %get-tuple-element.74.refs_0_), channel_id=1, source_target_pairs={{0,112},{16,0},{32,16},{48,32},{64,48},{80,64},{96,80},{112,96},{1... | collective-permute-start | bytes 786440 | tf_op jit(solution)/shard_map/ppermute | solution.py:376
  52.8 4.3 %collective-permute-done.16.refs_0_ = bf16[64,2048]{1,0:T(8,128)(2,1)S(1)} collective-permute-done((bf16[64,2048]{1,0:T(8,128)(2,1)S(1)}, bf16[64,2048]{1,0:T(8,128)(2,1)S(1)}, u32[]{:S(2)}, u32[]{:S(2)}) %collective-permute-start.16) | collective-permute-done | bytes 262176 | tf_op jit(solution)/shard_map/ppermute | solution.py:376
  57.1 0.5 collective-permute-done.17.refs_1_
  57.6 1.4 %collective-permute-start.18 = (bf16[64,2048]{1,0:T(8,128)(2,1)S(1)}, bf16[64,2048]{1,0:T(8,128)(2,1)S(1)}, u32[]{:S(2)}, u32[]{:S(2)}) collective-permute-start(bf16[64,2048]{1,0:T(8,128)(2,1)S(1)} %get-tuple-element.75.refs_1_), channel_id=1, source_target_pairs={{0,16},{16,32},{32,48},{48,64},{64,80},{80,96},{96,112},{112,0},{1... | collective-permute-start | bytes 786440 | tf_op jit(solution)/shard_map/ppermute | solution.py:376
  59.0 1.9 %collective-permute-start.19 = (bf16[64,2048]{1,0:T(8,128)(2,1)S(1)}, bf16[64,2048]{1,0:T(8,128)(2,1)S(1)}, u32[]{:S(2)}, u32[]{:S(2)}) collective-permute-start(bf16[64,2048]{1,0:T(8,128)(2,1)S(1)} %get-tuple-element.76.refs_6_), channel_id=1, source_target_pairs={{0,112},{16,0},{32,16},{48,32},{64,48},{80,64},{96,80},{112,96},{1... | collective-permute-start | bytes 786440 | tf_op jit(solution)/shard_map/ppermute | solution.py:376
  60.9 4.8 %collective-permute-done.18.refs_0_ = bf16[64,2048]{1,0:T(8,128)(2,1)S(1)} collective-permute-done((bf16[64,2048]{1,0:T(8,128)(2,1)S(1)}, bf16[64,2048]{1,0:T(8,128)(2,1)S(1)}, u32[]{:S(2)}, u32[]{:S(2)}) %collective-permute-start.18) | collective-permute-done | bytes 262176 | tf_op jit(solution)/shard_map/ppermute | solution.py:376
  65.7 1.2 %collective-permute-start.20 = (bf16[64,2048]{1,0:T(8,128)(2,1)S(1)}, bf16[64,2048]{1,0:T(8,128)(2,1)S(1)}, u32[]{:S(2)}, u32[]{:S(2)}) collective-permute-start(bf16[64,2048]{1,0:T(8,128)(2,1)S(1)} %get-tuple-element.77.refs_2_), channel_id=1, source_target_pairs={{0,16},{16,32},{32,48},{48,64},{64,80},{80,96},{96,112},{112,0},{1... | collective-permute-start | bytes 786440 | tf_op jit(solution)/shard_map/ppermute | solution.py:376
  66.9 2.3 %collective-permute-start.21 = (bf16[64,2048]{1,0:T(8,128)(2,1)S(1)}, bf16[64,2048]{1,0:T(8,128)(2,1)S(1)}, u32[]{:S(2)}, u32[]{:S(2)}) collective-permute-start(bf16[64,2048]{1,0:T(8,128)(2,1)S(1)} %get-tuple-element.78.refs_5_), channel_id=1, source_target_pairs={{0,112},{16,0},{32,16},{48,32},{64,48},{80,64},{96,80},{112,96},{1... | collective-permute-start | bytes 786440 | tf_op jit(solution)/shard_map/ppermute | solution.py:376
  69.2 4.3 %collective-permute-done.20.refs_0_ = bf16[64,2048]{1,0:T(8,128)(2,1)S(1)} collective-permute-done((bf16[64,2048]{1,0:T(8,128)(2,1)S(1)}, bf16[64,2048]{1,0:T(8,128)(2,1)S(1)}, u32[]{:S(2)}, u32[]{:S(2)}) %collective-permute-start.20) | collective-permute-done | bytes 262176 | tf_op jit(solution)/shard_map/ppermute | solution.py:376
  73.6 0.1 collective-permute-start.25
  73.7 1.3 %collective-permute-start.23 = (bf16[32,2048]{1,0:T(8,128)(2,1)S(1)}, bf16[32,2048]{1,0:T(8,128)(2,1)S(1)}, u32[]{:S(2)}, u32[]{:S(2)}) collective-permute-start(bf16[32,2048]{1,0:T(8,128)(2,1)S(1)} %slice.14), channel_id=1, source_target_pairs={{0,16},{16,32},{32,48},{48,64},{64,80},{80,96},{96,112},{112,0},{1... | collective-permute-start | bytes 393224 | tf_op jit(solution)/shard_map/ppermute | solution.py:376
  75.0 2.0 %collective-permute-start.24 = (bf16[32,2048]{1,0:T(8,128)(2,1)S(1)}, bf16[32,2048]{1,0:T(8,128)(2,1)S(1)}, u32[]{:S(2)}, u32[]{:S(2)}) collective-permute-start(bf16[32,2048]{1,0:T(8,128)(2,1)S(1)} %slice.15), channel_id=1, source_target_pairs={{0,112},{16,0},{32,16},{48,32},{64,48},{80,64},{96,80},{112,96},{1... | collective-permute-start | bytes 393224 | tf_op jit(solution)/shard_map/ppermute | solution.py:376
  77.1 2.2 %shard_map.104.refs_6_ = bf16[512,896]{1,0:T(8,128)(2,1)S(1)} custom-call(bf16[64,2048]{1,0:T(8,128)(2,1)S(1)} %get-tuple-element.74.refs_0_, bf16[64,2048]{1,0:T(8,128)(2,1)S(1)} %get-tuple-element.75.refs_1_, bf16[64,2048]{1,0:T(8,128)(2,1)S(1)} %get-tuple-element.77.refs_2_, bf16[64,2048]{1,0:T(8,128)(2,1)S(1)} %get-tuple-element.80.refs_3_, ...), custom_call_target="tpu_custom_call" | custom-call | flops 1644167168 | bytes 4194304 | tf_op jit(solution)/shard_map/pallas_call | solution.py:323
  79.3 1.8 %collective-permute-done.23.refs_0_ = bf16[32,2048]{1,0:T(8,128)(2,1)S(1)} collective-permute-done((bf16[32,2048]{1,0:T(8,128)(2,1)S(1)}, bf16[32,2048]{1,0:T(8,128)(2,1)S(1)}, u32[]{:S(2)}, u32[]{:S(2)}) %collective-permute-start.23) | collective-permute-done | bytes 131104 | tf_op jit(solution)/shard_map/ppermute | solution.py:376
  81.1 1.3 %shard_map.105 = (bf16[64,896]{1,0:T(8,128)(2,1)S(1)}, bf16[64,896]{1,0:T(8,128)(2,1)S(1)}, bf16[64,896]{1,0:T(8,128)(2,1)S(1)}, bf16[64,896]{1,0:T(8,128)(2,1)S...) custom-call(bf16[32,2048]{1,0:T(8,128)(2,1)S(1)} %collective-permute, ...), custom_call_target="tpu_custom_call", output_to_operand_aliasing={{8}: (6, {})} | custom-call | flops 234881024 | bytes 4194304 | tf_op jit(solution)/shard_map/pallas_call | solution.py:339
  82.4 1.6 %collective-permute-start.26 = (bf16[64,896]{1,0:T(8,128)(2,1)S(1)}, bf16[64,896]{1,0:T(8,128)(2,1)S(1)}, u32[]{:S(2)}, u32[]{:S(2)}) collective-permute-start(bf16[64,896]{1,0:T(8,128)(2,1)S(1)} %get-tuple-element.84), channel_id=1, source_target_pairs={{0,2},{1,3},{2,0},{3,1},{4,6},{5,7},{6,4},{7,5},{8,10},{9,11},{10,... | collective-permute-start | bytes 344072 | tf_op jit(solution)/shard_map/ppermute | solution.py:389
  84.0 2.1 %collective-permute-start.27 = (bf16[64,896]{1,0:T(8,128)(2,1)S(1)}, bf16[64,896]{1,0:T(8,128)(2,1)S(1)}, u32[]{:S(2)}, u32[]{:S(2)}) collective-permute-start(bf16[64,896]{1,0:T(8,128)(2,1)S(1)} %get-tuple-element.85), channel_id=1, source_target_pairs={{0,6},{1,7},{2,4},{3,5},{4,2},{5,3},{6,0},{7,1},{8,14},{9,15},{10,... | collective-permute-start | bytes 344072 | tf_op jit(solution)/shard_map/ppermute | solution.py:389
  86.1 0.6 collective-permute-start.28
  86.7 1.5 %collective-permute-start.30 = (bf16[64,896]{1,0:T(8,128)(2,1)S(1)}, bf16[64,896]{1,0:T(8,128)(2,1)S(1)}, u32[]{:S(2)}, u32[]{:S(2)}) collective-permute-start(bf16[64,896]{1,0:T(8,128)(2,1)S(1)} %get-tuple-element.88), channel_id=1, source_target_pairs={{0,3},{1,2},{2,1},{3,0},{4,7},{5,6},{6,5},{7,4},{8,11},{9,10},{10,... | collective-permute-start | bytes 344072 | tf_op jit(solution)/shard_map/ppermute | solution.py:389
  88.2 1.7 %collective-permute-start.31 = (bf16[64,896]{1,0:T(8,128)(2,1)S(1)}, bf16[64,896]{1,0:T(8,128)(2,1)S(1)}, u32[]{:S(2)}, u32[]{:S(2)}) collective-permute-start(bf16[64,896]{1,0:T(8,128)(2,1)S(1)} %get-tuple-element.89), channel_id=1, source_target_pairs={{0,7},{1,6},{2,5},{3,4},{4,3},{5,2},{6,1},{7,0},{8,15},{9,14},{10,... | collective-permute-start | bytes 344072 | tf_op jit(solution)/shard_map/ppermute | solution.py:389
  89.9 2.0 %collective-permute-done.27.refs_2_ = bf16[64,896]{1,0:T(8,128)(2,1)S(1)} collective-permute-done((bf16[64,896]{1,0:T(8,128)(2,1)S(1)}, bf16[64,896]{1,0:T(8,128)(2,1)S(1)}, u32[]{:S(2)}, u32[]{:S(2)}) %collective-permute-start.27) | collective-permute-done | bytes 114720 | tf_op jit(solution)/shard_map/ppermute | solution.py:389
  91.8 1.2 %collective-permute-done.28.refs_3_ = bf16[64,896]{1,0:T(8,128)(2,1)S(1)} collective-permute-done((bf16[64,896]{1,0:T(8,128)(2,1)S(1)}, bf16[64,896]{1,0:T(8,128)(2,1)S(1)}, u32[]{:S(2)}, u32[]{:S(2)}) %collective-permute-start.28) | collective-permute-done | bytes 114720 | tf_op jit(solution)/shard_map/ppermute | solution.py:389
  93.0 2.0 %collective-permute-done.31.refs_6_ = bf16[64,896]{1,0:T(8,128)(2,1)S(1)} collective-permute-done((bf16[64,896]{1,0:T(8,128)(2,1)S(1)}, bf16[64,896]{1,0:T(8,128)(2,1)S(1)}, u32[]{:S(2)}, u32[]{:S(2)}) %collective-permute-start.31) | collective-permute-done | bytes 114720 | tf_op jit(solution)/shard_map/ppermute | solution.py:389
  95.1 2.9 %collective-permute-done.32.refs_7_ = bf16[64,896]{1,0:T(8,128)(2,1)S(1)} collective-permute-done((bf16[64,896]{1,0:T(8,128)(2,1)S(1)}, bf16[64,896]{1,0:T(8,128)(2,1)S(1)}, u32[]{:S(2)}, u32[]{:S(2)}) %collective-permute-start.32) | collective-permute-done | bytes 114720 | tf_op jit(solution)/shard_map/ppermute | solution.py:389
  97.9 0.2 shard_map.106
  98.1 3.8 %collective-permute-start.33 = (bf16[2,64,448]{2,1,0:T(8,128)(2,1)S(1)}, bf16[2,64,448]{2,1,0:T(8,128)(2,1)S(1)}, u32[]{:S(2)}, u32[]{:S(2)}) collective-permute-start(bf16[2,64,448]{2,1,0:T(8,128)(2,1)S(1)} %get-tuple-element.91), channel_id=1, source_target_pairs={{0,0},{8,128},{128,8},{136,136},{1,1},{9,129},{129,9},{137,137},{2... | collective-permute-start | bytes 344072 | tf_op jit(solution)/shard_map/ppermute | solution.py:497
  102.0 0.1 collective-permute-start.34
  102.1 2.9 %collective-permute-done.33 = bf16[2,64,448]{2,1,0:T(8,128)(2,1)S(1)} collective-permute-done((bf16[2,64,448]{2,1,0:T(8,128)(2,1)S(1)}, bf16[2,64,448]{2,1,0:T(8,128)(2,1)S(1)}, u32[]{:S(2)}, u32[]{:S(2)}) %collective-permute-start.33) | collective-permute-done | bytes 114720 | tf_op jit(solution)/shard_map/ppermute | solution.py:497
  105.0 2.0 %collective-permute-done.34 = bf16[2,64,448]{2,1,0:T(8,128)(2,1)S(1)} collective-permute-done((bf16[2,64,448]{2,1,0:T(8,128)(2,1)S(1)}, bf16[2,64,448]{2,1,0:T(8,128)(2,1)S(1)}, u32[]{:S(2)}, u32[]{:S(2)}) %collective-permute-start.34) | collective-permute-done | bytes 114720 | tf_op jit(solution)/shard_map/ppermute | solution.py:498
  107.0 0.7 add_convert_fusion
  (35 shorter events, 0.1 us)
Async XLA Ops:
  0.0 23.8 %copy-start.2 = (s32[2]{0:T(128)S(1)}, s32[2]{0:T(128)}, u32[]{:S(2)}) copy-start(s32[2]{0:T(128)} %starts.3) | copy-start | bytes 28
  0.0 27.7 %collective-permute-start.10 = (bf16[512,1024]{1,0:T(8,128)(2,1)}, bf16[512,1024]{1,0:T(8,128)(2,1)S(1)}, u32[]{:S(2)}, u32[]{:S(2)}) collective-permute-start(bf16[512,1024]{1,0:T(8,128)(2,1)} %refs_4_.1), channel_id=1, source_target_pairs={{0,1},{1,0},{2,3},{3,2},{4,5},{5,4},{6,7},{7,6},{8,9},{9,8},{10,11... | collective-permute-start | bytes 3145736 | tf_op jit(solution)/shard_map/ppermute | solution.py:368
  0.0 27.7 %collective-permute-start.4 = (bf16[512,1024]{1,0:T(8,128)(2,1)}, bf16[512,1024]{1,0:T(8,128)(2,1)S(1)}, u32[]{:S(2)}, u32[]{:S(2)}) collective-permute-start(bf16[512,1024]{1,0:T(8,128)(2,1)} %w.1), channel_id=1, source_target_pairs={{0,1},{1,0},{2,3},{3,2},{4,5},{5,4},{6,7},{7,6},{8,9},{9,8},{10,11... | collective-permute-start | bytes 3145736 | tf_op jit(solution)/shard_map/ppermute | solution.py:368
  2.1 10.8 %collective-permute-start.2 = (bf16[64,1536]{1,0:T(8,128)(2,1)S(1)}, bf16[64,1536]{1,0:T(8,128)(2,1)S(1)}, u32[]{:S(2)}, u32[]{:S(2)}) collective-permute-start(bf16[64,1536]{1,0:T(8,128)(2,1)S(1)} %get-tuple-element.50), channel_id=1, source_target_pairs={{0,1},{1,0},{2,3},{3,2},{4,5},{5,4},{6,7},{7,6},{8,9},{9,8},{10,11... | collective-permute-start | bytes 589832 | tf_op jit(solution)/shard_map/ppermute | solution.py:368
  2.3 10.6 %collective-permute-start = (bf16[128,576]{1,0:T(8,128)(2,1)S(1)}, bf16[128,576]{1,0:T(8,128)(2,1)S(1)}, u32[]{:S(2)}, u32[]{:S(2)}) collective-permute-start(bf16[128,576]{1,0:T(8,128)(2,1)S(1)} %get-tuple-element.49.refs_4_), channel_id=1, source_target_pairs={{0,16},{16,32},{32,48},{48,64},{64,80},{80,96},{96,112},{112,0},{1... | collective-permute-start | bytes 442376 | tf_op jit(solution)/shard_map/ppermute | solution.py:376
  4.2 8.7 %collective-permute-start.1 = (bf16[128,576]{1,0:T(8,128)(2,1)S(1)}, bf16[128,576]{1,0:T(8,128)(2,1)S(1)}, u32[]{:S(2)}, u32[]{:S(2)}) collective-permute-start(bf16[128,576]{1,0:T(8,128)(2,1)S(1)} %get-tuple-element.49.refs_4_), channel_id=1, source_target_pairs={{0,112},{16,0},{32,16},{48,32},{64,48},{80,64},{96,80},{112,96},{1... | collective-permute-start | bytes 442376 | tf_op jit(solution)/shard_map/ppermute | solution.py:376
  12.9 7.2 %collective-permute-start.5 = (bf16[128,576]{1,0:T(8,128)(2,1)S(1)}, bf16[128,576]{1,0:T(8,128)(2,1)S(1)}, u32[]{:S(2)}, u32[]{:S(2)}) collective-permute-start(bf16[128,576]{1,0:T(8,128)(2,1)S(1)} %get-tuple-element.52.refs_5_.refs_8_), channel_id=1, source_target_pairs={{0,16},{16,32},{32,48},{48,64},{64,80},{80,96},{96,112},{112,0},{1... | collective-permute-start | bytes 442376 | tf_op jit(solution)/shard_map/ppermute | solution.py:376
  13.0 9.4 %collective-permute-start.9 = (bf16[64,1536]{1,0:T(8,128)(2,1)S(1)}, bf16[64,1536]{1,0:T(8,128)(2,1)S(1)}, u32[]{:S(2)}, u32[]{:S(2)}) collective-permute-start(bf16[64,1536]{1,0:T(8,128)(2,1)S(1)} %get-tuple-element.56.refs_1_), channel_id=1, source_target_pairs={{0,128},{128,0},{1,129},{129,1},{2,130},{130,2},{3,131},{131,3},{4... | collective-permute-start | bytes 589832 | tf_op jit(solution)/shard_map/ppermute | solution.py:368
  13.5 7.1 %collective-permute-start.6 = (bf16[128,576]{1,0:T(8,128)(2,1)S(1)}, bf16[128,576]{1,0:T(8,128)(2,1)S(1)}, u32[]{:S(2)}, u32[]{:S(2)}) collective-permute-start(bf16[128,576]{1,0:T(8,128)(2,1)S(1)} %get-tuple-element.53.refs_7_), channel_id=1, source_target_pairs={{0,112},{16,0},{32,16},{48,32},{64,48},{80,64},{96,80},{112,96},{1... | collective-permute-start | bytes 442376 | tf_op jit(solution)/shard_map/ppermute | solution.py:376
  20.1 6.3 %collective-permute-start.3 = (bf16[64,1536]{1,0:T(8,128)(2,1)S(1)}, bf16[64,1536]{1,0:T(8,128)(2,1)S(1)}, u32[]{:S(2)}, u32[]{:S(2)}) collective-permute-start(bf16[64,1536]{1,0:T(8,128)(2,1)S(1)} %get-tuple-element.51.refs_1_), channel_id=1, source_target_pairs={{0,128},{128,0},{1,129},{129,1},{2,130},{130,2},{3,131},{131,3},{4... | collective-permute-start | bytes 589832 | tf_op jit(solution)/shard_map/ppermute | solution.py:368
  20.6 6.5 %collective-permute-start.7 = (bf16[128,576]{1,0:T(8,128)(2,1)S(1)}, bf16[128,576]{1,0:T(8,128)(2,1)S(1)}, u32[]{:S(2)}, u32[]{:S(2)}) collective-permute-start(bf16[128,576]{1,0:T(8,128)(2,1)S(1)} %get-tuple-element.54.refs_6_), channel_id=1, source_target_pairs={{0,16},{16,32},{32,48},{48,64},{64,80},{80,96},{96,112},{112,0},{1... | collective-permute-start | bytes 442376 | tf_op jit(solution)/shard_map/ppermute | solution.py:376
  22.4 5.3 %collective-permute-start.8 = (bf16[128,576]{1,0:T(8,128)(2,1)S(1)}, bf16[128,576]{1,0:T(8,128)(2,1)S(1)}, u32[]{:S(2)}, u32[]{:S(2)}) collective-permute-start(bf16[128,576]{1,0:T(8,128)(2,1)S(1)} %get-tuple-element.55.refs_5_), channel_id=1, source_target_pairs={{0,112},{16,0},{32,16},{48,32},{64,48},{80,64},{96,80},{112,96},{1... | collective-permute-start | bytes 442376 | tf_op jit(solution)/shard_map/ppermute | solution.py:376
  27.7 11.8 %collective-permute-start.13 = (bf16[448,1024]{1,0:T(8,128)(2,1)S(1)}, bf16[448,1024]{1,0:T(8,128)(2,1)S(1)}, u32[]{:S(2)}, u32[]{:S(2)}) collective-permute-start(bf16[448,1024]{1,0:T(8,128)(2,1)S(1)} %get-tuple-element.68), channel_id=1, source_target_pairs={{0,1},{1,0},{2,3},{3,2},{4,5},{5,4},{6,7},{7,6},{8,9},{9,8},{10,11... | collective-permute-start | bytes 2752520 | tf_op jit(solution)/shard_map/ppermute | solution.py:368
  27.8 6.2 %collective-permute-start.11 = (bf16[64,576]{1,0:T(8,128)(2,1)S(1)}, bf16[64,576]{1,0:T(8,128)(2,1)S(1)}, u32[]{:S(2)}, u32[]{:S(2)}) collective-permute-start(bf16[64,576]{1,0:T(8,128)(2,1)S(1)} %slice.12), channel_id=1, source_target_pairs={{0,16},{16,32},{32,48},{48,64},{64,80},{80,96},{96,112},{112,0},{1... | collective-permute-start | bytes 221192 | tf_op jit(solution)/shard_map/ppermute | solution.py:376
  29.9 4.9 %copy-start = (bf16[512,1024]{1,0:T(8,128)(2,1)S(1)}, bf16[512,1024]{1,0:T(8,128)(2,1)}, u32[]{:S(2)}) copy-start(bf16[512,1024]{1,0:T(8,128)(2,1)} %refs_4_.1) | copy-start | bytes 3145732
  29.9 4.9 %collective-permute-start.12 = (bf16[64,576]{1,0:T(8,128)(2,1)S(1)}, bf16[64,576]{1,0:T(8,128)(2,1)S(1)}, u32[]{:S(2)}, u32[]{:S(2)}) collective-permute-start(bf16[64,576]{1,0:T(8,128)(2,1)S(1)} %slice.13), channel_id=1, source_target_pairs={{0,112},{16,0},{32,16},{48,32},{64,48},{80,64},{96,80},{112,96},{1... | collective-permute-start | bytes 221192 | tf_op jit(solution)/shard_map/ppermute | solution.py:376
  37.9 5.4 %collective-permute-start.15 = (bf16[64,1152]{1,0:T(8,128)(2,1)S(1)}, bf16[64,1152]{1,0:T(8,128)(2,1)S(1)}, u32[]{:S(2)}, u32[]{:S(2)}) collective-permute-start(bf16[64,1152]{1,0:T(8,128)(2,1)S(1)} %get-tuple-element.73), channel_id=1, source_target_pairs={{0,128},{128,0},{1,129},{129,1},{2,130},{130,2},{3,131},{131,3},{4... | collective-permute-start | bytes 442376 | tf_op jit(solution)/shard_map/ppermute | solution.py:368
  39.5 3.8 %copy-start.3 = (s32[2]{0:T(128)S(1)}, s32[2]{0:T(128)}, u32[]{:S(2)}) copy-start(s32[2]{0:T(128)} %lens.3) | copy-start | bytes 28
  39.5 8.3 %copy-start.1 = (bf16[1024,448]{0,1:T(8,128)(2,1)S(1)}, bf16[1024,448]{0,1:T(8,128)(2,1)}, u32[]{:S(2)}) copy-start(bf16[1024,448]{0,1:T(8,128)(2,1)} %param.15) | copy-start | bytes 2752516
  42.5 5.2 %collective-permute-start.14 = (bf16[64,1152]{1,0:T(8,128)(2,1)S(1)}, bf16[64,1152]{1,0:T(8,128)(2,1)S(1)}, u32[]{:S(2)}, u32[]{:S(2)}) collective-permute-start(bf16[64,1152]{1,0:T(8,128)(2,1)S(1)} %get-tuple-element.71), channel_id=1, source_target_pairs={{0,128},{128,0},{1,129},{129,1},{2,130},{130,2},{3,131},{131,3},{4... | collective-permute-start | bytes 442376 | tf_op jit(solution)/shard_map/ppermute | solution.py:368
  48.9 24.7 %collective-permute-start.22 = (bf16[448,1024]{1,0:T(8,128)(2,1)S(1)}, bf16[448,1024]{1,0:T(8,128)(2,1)S(1)}, u32[]{:S(2)}, u32[]{:S(2)}) collective-permute-start(bf16[448,1024]{1,0:T(8,128)(2,1)S(1)} %get-tuple-element.79.refs_7_.refs_2_), channel_id=1, source_target_pairs={{0,128},{128,0},{1,129},{129,1},{2,130},{130,2},{3,131},{131,3},{4... | collective-permute-start | bytes 2752520 | tf_op jit(solution)/shard_map/ppermute | solution.py:368
  49.5 7.6 %collective-permute-start.16 = (bf16[64,2048]{1,0:T(8,128)(2,1)S(1)}, bf16[64,2048]{1,0:T(8,128)(2,1)S(1)}, u32[]{:S(2)}, u32[]{:S(2)}) collective-permute-start(bf16[64,2048]{1,0:T(8,128)(2,1)S(1)} %get-tuple-element.74.refs_0_), channel_id=1, source_target_pairs={{0,16},{16,32},{32,48},{48,64},{64,80},{80,96},{96,112},{112,0},{1... | collective-permute-start | bytes 786440 | tf_op jit(solution)/shard_map/ppermute | solution.py:376
  51.3 6.4 %collective-permute-start.17 = (bf16[64,2048]{1,0:T(8,128)(2,1)S(1)}, bf16[64,2048]{1,0:T(8,128)(2,1)S(1)}, u32[]{:S(2)}, u32[]{:S(2)}) collective-permute-start(bf16[64,2048]{1,0:T(8,128)(2,1)S(1)} %get-tuple-element.74.refs_0_), channel_id=1, source_target_pairs={{0,112},{16,0},{32,16},{48,32},{64,48},{80,64},{96,80},{112,96},{1... | collective-permute-start | bytes 786440 | tf_op jit(solution)/shard_map/ppermute | solution.py:376
  57.6 8.1 %collective-permute-start.18 = (bf16[64,2048]{1,0:T(8,128)(2,1)S(1)}, bf16[64,2048]{1,0:T(8,128)(2,1)S(1)}, u32[]{:S(2)}, u32[]{:S(2)}) collective-permute-start(bf16[64,2048]{1,0:T(8,128)(2,1)S(1)} %get-tuple-element.75.refs_1_), channel_id=1, source_target_pairs={{0,16},{16,32},{32,48},{48,64},{64,80},{80,96},{96,112},{112,0},{1... | collective-permute-start | bytes 786440 | tf_op jit(solution)/shard_map/ppermute | solution.py:376
  59.0 6.7 %collective-permute-start.19 = (bf16[64,2048]{1,0:T(8,128)(2,1)S(1)}, bf16[64,2048]{1,0:T(8,128)(2,1)S(1)}, u32[]{:S(2)}, u32[]{:S(2)}) collective-permute-start(bf16[64,2048]{1,0:T(8,128)(2,1)S(1)} %get-tuple-element.76.refs_6_), channel_id=1, source_target_pairs={{0,112},{16,0},{32,16},{48,32},{64,48},{80,64},{96,80},{112,96},{1... | collective-permute-start | bytes 786440 | tf_op jit(solution)/shard_map/ppermute | solution.py:376
  65.7 7.9 %collective-permute-start.20 = (bf16[64,2048]{1,0:T(8,128)(2,1)S(1)}, bf16[64,2048]{1,0:T(8,128)(2,1)S(1)}, u32[]{:S(2)}, u32[]{:S(2)}) collective-permute-start(bf16[64,2048]{1,0:T(8,128)(2,1)S(1)} %get-tuple-element.77.refs_2_), channel_id=1, source_target_pairs={{0,16},{16,32},{32,48},{48,64},{64,80},{80,96},{96,112},{112,0},{1... | collective-permute-start | bytes 786440 | tf_op jit(solution)/shard_map/ppermute | solution.py:376
  66.9 6.7 %collective-permute-start.21 = (bf16[64,2048]{1,0:T(8,128)(2,1)S(1)}, bf16[64,2048]{1,0:T(8,128)(2,1)S(1)}, u32[]{:S(2)}, u32[]{:S(2)}) collective-permute-start(bf16[64,2048]{1,0:T(8,128)(2,1)S(1)} %get-tuple-element.78.refs_5_), channel_id=1, source_target_pairs={{0,112},{16,0},{32,16},{48,32},{64,48},{80,64},{96,80},{112,96},{1... | collective-permute-start | bytes 786440 | tf_op jit(solution)/shard_map/ppermute | solution.py:376
  73.6 3.5 %collective-permute-start.25 = (bf16[448,1024]{1,0:T(8,128)(2,1)S(1)}, bf16[448,1024]{1,0:T(8,128)(2,1)S(1)}, u32[]{:S(2)}, u32[]{:S(2)}) collective-permute-start(bf16[448,1024]{1,0:T(8,128)(2,1)S(1)} %get-tuple-element.82.refs_8_.refs_3_), channel_id=1, source_target_pairs={{0,1},{1,0},{2,3},{3,2},{4,5},{5,4},{6,7},{7,6},{8,9},{9,8},{10,11... | collective-permute-start | bytes 2752520 | tf_op jit(solution)/shard_map/ppermute | solution.py:368
  73.7 7.4 %collective-permute-start.23 = (bf16[32,2048]{1,0:T(8,128)(2,1)S(1)}, bf16[32,2048]{1,0:T(8,128)(2,1)S(1)}, u32[]{:S(2)}, u32[]{:S(2)}) collective-permute-start(bf16[32,2048]{1,0:T(8,128)(2,1)S(1)} %slice.14), channel_id=1, source_target_pairs={{0,16},{16,32},{32,48},{48,64},{64,80},{80,96},{96,112},{112,0},{1... | collective-permute-start | bytes 393224 | tf_op jit(solution)/shard_map/ppermute | solution.py:376
  75.0 6.0 %collective-permute-start.24 = (bf16[32,2048]{1,0:T(8,128)(2,1)S(1)}, bf16[32,2048]{1,0:T(8,128)(2,1)S(1)}, u32[]{:S(2)}, u32[]{:S(2)}) collective-permute-start(bf16[32,2048]{1,0:T(8,128)(2,1)S(1)} %slice.15), channel_id=1, source_target_pairs={{0,112},{16,0},{32,16},{48,32},{64,48},{80,64},{96,80},{112,96},{1... | collective-permute-start | bytes 393224 | tf_op jit(solution)/shard_map/ppermute | solution.py:376
  82.4 5.8 %collective-permute-start.26 = (bf16[64,896]{1,0:T(8,128)(2,1)S(1)}, bf16[64,896]{1,0:T(8,128)(2,1)S(1)}, u32[]{:S(2)}, u32[]{:S(2)}) collective-permute-start(bf16[64,896]{1,0:T(8,128)(2,1)S(1)} %get-tuple-element.84), channel_id=1, source_target_pairs={{0,2},{1,3},{2,0},{3,1},{4,6},{5,7},{6,4},{7,5},{8,10},{9,11},{10,... | collective-permute-start | bytes 344072 | tf_op jit(solution)/shard_map/ppermute | solution.py:389
  84.0 7.9 %collective-permute-start.27 = (bf16[64,896]{1,0:T(8,128)(2,1)S(1)}, bf16[64,896]{1,0:T(8,128)(2,1)S(1)}, u32[]{:S(2)}, u32[]{:S(2)}) collective-permute-start(bf16[64,896]{1,0:T(8,128)(2,1)S(1)} %get-tuple-element.85), channel_id=1, source_target_pairs={{0,6},{1,7},{2,4},{3,5},{4,2},{5,3},{6,0},{7,1},{8,14},{9,15},{10,... | collective-permute-start | bytes 344072 | tf_op jit(solution)/shard_map/ppermute | solution.py:389
  86.1 6.9 %collective-permute-start.28 = (bf16[64,896]{1,0:T(8,128)(2,1)S(1)}, bf16[64,896]{1,0:T(8,128)(2,1)S(1)}, u32[]{:S(2)}, u32[]{:S(2)}) collective-permute-start(bf16[64,896]{1,0:T(8,128)(2,1)S(1)} %get-tuple-element.86), channel_id=1, source_target_pairs={{0,4},{1,5},{2,6},{3,7},{4,0},{5,1},{6,2},{7,3},{8,12},{9,13},{10,... | collective-permute-start | bytes 344072 | tf_op jit(solution)/shard_map/ppermute | solution.py:389
  86.7 6.3 %collective-permute-start.29 = (bf16[64,896]{1,0:T(8,128)(2,1)S(1)}, bf16[64,896]{1,0:T(8,128)(2,1)S(1)}, u32[]{:S(2)}, u32[]{:S(2)}) collective-permute-start(bf16[64,896]{1,0:T(8,128)(2,1)S(1)} %get-tuple-element.87), channel_id=1, source_target_pairs={{0,1},{1,0},{2,3},{3,2},{4,5},{5,4},{6,7},{7,6},{8,9},{9,8},{10,11... | collective-permute-start | bytes 344072 | tf_op jit(solution)/shard_map/ppermute | solution.py:368
  86.7 6.3 %collective-permute-start.30 = (bf16[64,896]{1,0:T(8,128)(2,1)S(1)}, bf16[64,896]{1,0:T(8,128)(2,1)S(1)}, u32[]{:S(2)}, u32[]{:S(2)}) collective-permute-start(bf16[64,896]{1,0:T(8,128)(2,1)S(1)} %get-tuple-element.88), channel_id=1, source_target_pairs={{0,3},{1,2},{2,1},{3,0},{4,7},{5,6},{6,5},{7,4},{8,11},{9,10},{10,... | collective-permute-start | bytes 344072 | tf_op jit(solution)/shard_map/ppermute | solution.py:389
  88.2 6.9 %collective-permute-start.31 = (bf16[64,896]{1,0:T(8,128)(2,1)S(1)}, bf16[64,896]{1,0:T(8,128)(2,1)S(1)}, u32[]{:S(2)}, u32[]{:S(2)}) collective-permute-start(bf16[64,896]{1,0:T(8,128)(2,1)S(1)} %get-tuple-element.89), channel_id=1, source_target_pairs={{0,7},{1,6},{2,5},{3,4},{4,3},{5,2},{6,1},{7,0},{8,15},{9,14},{10,... | collective-permute-start | bytes 344072 | tf_op jit(solution)/shard_map/ppermute | solution.py:389
  91.8 6.1 %collective-permute-start.32 = (bf16[64,896]{1,0:T(8,128)(2,1)S(1)}, bf16[64,896]{1,0:T(8,128)(2,1)S(1)}, u32[]{:S(2)}, u32[]{:S(2)}) collective-permute-start(bf16[64,896]{1,0:T(8,128)(2,1)S(1)} %get-tuple-element.90), channel_id=1, source_target_pairs={{0,5},{1,4},{2,7},{3,6},{4,1},{5,0},{6,3},{7,2},{8,13},{9,12},{10,... | collective-permute-start | bytes 344072 | tf_op jit(solution)/shard_map/ppermute | solution.py:389
  98.1 6.9 %collective-permute-start.33 = (bf16[2,64,448]{2,1,0:T(8,128)(2,1)S(1)}, bf16[2,64,448]{2,1,0:T(8,128)(2,1)S(1)}, u32[]{:S(2)}, u32[]{:S(2)}) collective-permute-start(bf16[2,64,448]{2,1,0:T(8,128)(2,1)S(1)} %get-tuple-element.91), channel_id=1, source_target_pairs={{0,0},{8,128},{128,8},{136,136},{1,1},{9,129},{129,9},{137,137},{2... | collective-permute-start | bytes 344072 | tf_op jit(solution)/shard_map/ppermute | solution.py:497
  102.0 5.0 %collective-permute-start.34 = (bf16[2,64,448]{2,1,0:T(8,128)(2,1)S(1)}, bf16[2,64,448]{2,1,0:T(8,128)(2,1)S(1)}, u32[]{:S(2)}, u32[]{:S(2)}) collective-permute-start(bf16[2,64,448]{2,1,0:T(8,128)(2,1)S(1)} %get-tuple-element.92), channel_id=1, source_target_pairs={{0,128},{128,136},{8,0},{136,8},{1,129},{129,137},{9,1},{137,9},{2... | collective-permute-start | bytes 344072 | tf_op jit(solution)/shard_map/ppermute | solution.py:498

commit v6 on v5

--- a/solution.py
+++ b/solution.py
@@ -494,7 +494,8 @@
     other_seq += [to_partner(parts[2 * k + 3], X_PAIRS[k], 1) for k in range(3)]
     own_seq = [parts[0]] + [to_partner(parts[2 * k + 2], X_PAIRS[k], 0) for k in range(3)]
     first, second = sums(own_seq, other_seq)
-    first = lax.ppermute(first, ("yl", "yh"), [(0, 0), (1, 2), (2, 1), (3, 3)])
+    kept = lax.axis_index("yl") == lax.axis_index("yh")
+    first = jnp.where(kept, first, lax.ppermute(first, ("yl", "yh"), [(1, 2), (2, 1)]))
     second = lax.ppermute(second, ("yl", "yh"), [(0, 2), (2, 3), (1, 0), (3, 1)])
     return (first.astype(f32) + second.astype(f32)).astype(bf16)
 

time: 108 us -> 108 us (level)
  no operation moved by 1% of the time
where the time goes in v6:
time: 108 us
  starting transfers between devices  45.5 us (42%)
  waiting for transfers between devices  42.9 us (40%)
  Pallas kernels  18.4 us (17%)
    ppermute x16, starting transfers between devices, step(): return (lax.ppermute(a, 'z', UP), lax.ppermute(b, 'z', DOWN))  29.4 us
    ppermute x16, waiting for transfers between devices, step(): return (lax.ppermute(a, 'z', UP), lax.ppermute(b, 'z', DOWN))  26.1 us
    ppermute x6, waiting for transfers between devices, to_partner(): return lax.ppermute(x, ('x', 'core'), moves)  8.06 us
    ppermute x6, starting transfers between devices, to_partner(): return lax.ppermute(x, ('x', 'core'), moves)  7.49 us
    pallas_call x2, Pallas kernels, attention_second(): pl.pallas_call(functools.partial(second_kernel, rows, heads, half, slots)...  6.09 us
    pallas_call x2, Pallas kernels, attention_first(): pl.pallas_call(functools.partial(first_kernel, rows, heads, half, slots),...  5.17 us
    ppermute x11, starting transfers between devices, swap(): return lax.ppermute(x, axis, [(0, 1), (1, 0)])  4.7 us
    ppermute x1, starting transfers between devices, local(): lax.ppermute(first, ('yl', 'yh'), [(1, 2), (2, 1)])  3.84 us
  transfers between devices with their start and end apart: 35, of which 18 were waited for; matrix products, arithmetic and copies ran while one was open for 0% of the time, Pallas kernels for 15%

profile of v6, /device:TPU:8, one launch (start us, length us, event | category | flops | bytes accessed | tf_op | source)
XLA Modules:
  0.0 107.7 jit_solution(5079590046427098795)
XLA Ops:
  0.0 0.5 collective-permute-start.4
  0.5 1.6 %shard_map.91 = (bf16[128,576]{1,0:T(8,128)(2,1)S(1)}, bf16[64,1536]{1,0:T(8,128)(2,1)S(1)}, bf16[64,1536]{1,0:T(8,128)(2,1)S(1)}, bf16[512,1024]{1,0:T(8,128)(2,1)S(1)}) custom-call(bf16[2,64,1024]{2,1,0:T(8,128)(2,1)} %q_nope.1, bf16[2,64,512]{2,1,0:T(8,128)(2,1)} %q_rope.1, bf16[2,64,576]{2,1,0:T(8,128)(2,1)} %cache.1, bf16[2,64,576]{2,1,0:T(8,128)(2,1)} %stretch.1, ...), custom_call_target="tpu_custom_call" | custom-call | tf_op jit(solution)/shard_map/pallas_call | solution.py:414
  2.1 0.2 collective-permute-start.2
  2.3 1.9 %collective-permute-start = (bf16[128,576]{1,0:T(8,128)(2,1)S(1)}, bf16[128,576]{1,0:T(8,128)(2,1)S(1)}, u32[]{:S(2)}, u32[]{:S(2)}) collective-permute-start(bf16[128,576]{1,0:T(8,128)(2,1)S(1)} %get-tuple-element.49.refs_4_), channel_id=1, source_target_pairs={{0,16},{16,32},{32,48},{48,64},{64,80},{80,96},{96,112},{112,0},{1... | collective-permute-start | bytes 442376 | tf_op jit(solution)/shard_map/ppermute | solution.py:376
  4.2 4.0 %collective-permute-start.1 = (bf16[128,576]{1,0:T(8,128)(2,1)S(1)}, bf16[128,576]{1,0:T(8,128)(2,1)S(1)}, u32[]{:S(2)}, u32[]{:S(2)}) collective-permute-start(bf16[128,576]{1,0:T(8,128)(2,1)S(1)} %get-tuple-element.49.refs_4_), channel_id=1, source_target_pairs={{0,112},{16,0},{32,16},{48,32},{64,48},{80,64},{96,80},{112,96},{1... | collective-permute-start | bytes 442376 | tf_op jit(solution)/shard_map/ppermute | solution.py:376
  8.2 4.7 %collective-permute-done.refs_0_ = bf16[128,576]{1,0:T(8,128)(2,1)S(1)} collective-permute-done((bf16[128,576]{1,0:T(8,128)(2,1)S(1)}, bf16[128,576]{1,0:T(8,128)(2,1)S(1)}, u32[]{:S(2)}, u32[]{:S(2)}) %collective-permute-start) | collective-permute-done | bytes 147488 | tf_op jit(solution)/shard_map/ppermute | solution.py:376
  12.9 0.0 collective-permute-done.1.refs_1_
  12.9 0.0 collective-permute-done.2.refs_2_
  12.9 0.1 collective-permute-start.5
  13.0 0.5 collective-permute-start.9
  13.5 3.1 %collective-permute-start.6 = (bf16[128,576]{1,0:T(8,128)(2,1)S(1)}, bf16[128,576]{1,0:T(8,128)(2,1)S(1)}, u32[]{:S(2)}, u32[]{:S(2)}) collective-permute-start(bf16[128,576]{1,0:T(8,128)(2,1)S(1)} %get-tuple-element.53.refs_7_), channel_id=1, source_target_pairs={{0,112},{16,0},{32,16},{48,32},{64,48},{80,64},{96,80},{112,96},{1... | collective-permute-start | bytes 442376 | tf_op jit(solution)/shard_map/ppermute | solution.py:376
  16.7 3.5 %collective-permute-done.5.refs_0_ = bf16[128,576]{1,0:T(8,128)(2,1)S(1)} collective-permute-done((bf16[128,576]{1,0:T(8,128)(2,1)S(1)}, bf16[128,576]{1,0:T(8,128)(2,1)S(1)}, u32[]{:S(2)}, u32[]{:S(2)}) %collective-permute-start.5) | collective-permute-done | bytes 147488 | tf_op jit(solution)/shard_map/ppermute | solution.py:376
  20.1 0.4 collective-permute-start.3
  20.6 1.8 %collective-permute-start.7 = (bf16[128,576]{1,0:T(8,128)(2,1)S(1)}, bf16[128,576]{1,0:T(8,128)(2,1)S(1)}, u32[]{:S(2)}, u32[]{:S(2)}) collective-permute-start(bf16[128,576]{1,0:T(8,128)(2,1)S(1)} %get-tuple-element.54.refs_6_), channel_id=1, source_target_pairs={{0,16},{16,32},{32,48},{48,64},{64,80},{80,96},{96,112},{112,0},{1... | collective-permute-start | bytes 442376 | tf_op jit(solution)/shard_map/ppermute | solution.py:376
  22.4 1.5 %collective-permute-start.8 = (bf16[128,576]{1,0:T(8,128)(2,1)S(1)}, bf16[128,576]{1,0:T(8,128)(2,1)S(1)}, u32[]{:S(2)}, u32[]{:S(2)}) collective-permute-start(bf16[128,576]{1,0:T(8,128)(2,1)S(1)} %get-tuple-element.55.refs_5_), channel_id=1, source_target_pairs={{0,112},{16,0},{32,16},{48,32},{64,48},{80,64},{96,80},{112,96},{1... | collective-permute-start | bytes 442376 | tf_op jit(solution)/shard_map/ppermute | solution.py:376
  23.8 2.6 %shard_map.94 = (bf16[1024,640]{1,0:T(8,128)(2,1)S(1)}, f32[1024,512]{1,0:T(8,128)S(1)}, f32[1024,256]{1,0:T(8,128)S(1)}, bf16[448,1024]{1,0:T(8,128)(2,1)S(1)}) custom-call(s32[2]{0:T(128)S(1)} %copy-done.2, bf16[64,1536]{1,0:T(8,128)(2,1)S(1)} %get-tuple-element.56.refs_1_, bf16[64,1536]{1,0:T(8,128)(2,1)S(1)} %collective-permute-done.9.refs_2_, ...), custom_call_target="tpu_custom_call" | custom-call | flops 1207959552 | bytes 4194304 | tf_op jit(solution)/shard_map/pallas_call | solution.py:178
  26.5 0.7 collective-permute-done.7.refs_0_
  27.1 0.6 collective-permute-done.8.refs_1_
  27.7 0.1 collective-permute-start.13
  27.8 2.1 %collective-permute-start.11 = (bf16[64,576]{1,0:T(8,128)(2,1)S(1)}, bf16[64,576]{1,0:T(8,128)(2,1)S(1)}, u32[]{:S(2)}, u32[]{:S(2)}) collective-permute-start(bf16[64,576]{1,0:T(8,128)(2,1)S(1)} %slice.12), channel_id=1, source_target_pairs={{0,16},{16,32},{32,48},{48,64},{64,80},{80,96},{96,112},{112,0},{1... | collective-permute-start | bytes 221192 | tf_op jit(solution)/shard_map/ppermute | solution.py:376
  29.9 0.0 copy-start
  29.9 1.5 %collective-permute-start.12 = (bf16[64,576]{1,0:T(8,128)(2,1)S(1)}, bf16[64,576]{1,0:T(8,128)(2,1)S(1)}, u32[]{:S(2)}, u32[]{:S(2)}) collective-permute-start(bf16[64,576]{1,0:T(8,128)(2,1)S(1)} %slice.13), channel_id=1, source_target_pairs={{0,112},{16,0},{32,16},{48,32},{64,48},{80,64},{96,80},{112,96},{1... | collective-permute-start | bytes 221192 | tf_op jit(solution)/shard_map/ppermute | solution.py:376
  31.4 2.6 %shard_map.96 = (bf16[1024,640]{1,0:T(8,128)(2,1)S(1)}, f32[1024,512]{1,0:T(8,128)S(1)}, f32[1024,256]{1,0:T(8,128)S(1)}) custom-call(s32[2]{0:T(128)S(1)} %copy-done.2, bf16[64,1536]{1,0:T(8,128)(2,1)S(1)} %get-tuple-element.51.refs_1_, bf16[64,1536]{1,0:T(8,128)(2,1)S(1)} %collective-permute-done.3.refs_3_.refs_2_, ...), custom_call_target="tpu_custom_call" | custom-call | flops 1207959552 | bytes 4194304 | tf_op jit(solution)/shard_map/pallas_call | solution.py:178
  34.0 0.9 collective-permute-done.12.refs_9_
  34.9 3.0 %shard_map.97 = (f32[64,1024]{1,0:T(8,128)S(1)}, f32[64,128]{1,0:T(8,128)S(1)}, bf16[64,1152]{1,0:T(8,128)(2,1)S(1)}) custom-call(s32[2]{0:T(128)S(1)} %copy-done.2, bf16[1024,640]{1,0:T(8,128)(2,1)S(1)} %get-tuple-element.65.refs_1_, f32[1024,512]{1,0:T(8,128)S(1)} %get-tuple-element.66.refs_2_, f32[1024,256]{1,0:T(8,128)S(1)} %get-tuple-element.59.refs_6_.refs_3_, ...), custom_call_target="tpu_custom_call" | custom-call | flops 1207959552 | bytes 4194304 | tf_op jit(solution)/shard_map/pallas_call | solution.py:204
  37.9 1.5 %collective-permute-start.15 = (bf16[64,1152]{1,0:T(8,128)(2,1)S(1)}, bf16[64,1152]{1,0:T(8,128)(2,1)S(1)}, u32[]{:S(2)}, u32[]{:S(2)}) collective-permute-start(bf16[64,1152]{1,0:T(8,128)(2,1)S(1)} %get-tuple-element.73), channel_id=1, source_target_pairs={{0,128},{128,0},{1,129},{129,1},{2,130},{130,2},{3,131},{131,3},{4... | collective-permute-start | bytes 442376 | tf_op jit(solution)/shard_map/ppermute | solution.py:368
  39.5 3.0 %shard_map.98 = (f32[64,1024]{1,0:T(8,128)S(1)}, f32[64,128]{1,0:T(8,128)S(1)}, bf16[64,1152]{1,0:T(8,128)(2,1)S(1)}) custom-call(s32[2]{0:T(128)S(1)} %copy-done.2, bf16[1024,640]{1,0:T(8,128)(2,1)S(1)} %get-tuple-element.61.refs_1_, f32[1024,512]{1,0:T(8,128)S(1)} %get-tuple-element.62.refs_2_, f32[1024,256]{1,0:T(8,128)S(1)} %get-tuple-element.63.refs_10_.refs_3_, ...), custom_call_target="tpu_custom_call" | custom-call | flops 1207959552 | bytes 4194304 | tf_op jit(solution)/shard_map/pallas_call | solution.py:204
  42.5 0.7 collective-permute-start.14
  43.2 0.1 collective-permute-done.15.got
  43.3 0.8 shard_map.99.refs_0_
  44.1 3.6 %collective-permute-done.14.got = bf16[64,1152]{1,0:T(8,128)(2,1)S(1)} collective-permute-done((bf16[64,1152]{1,0:T(8,128)(2,1)S(1)}, bf16[64,1152]{1,0:T(8,128)(2,1)S(1)}, u32[]{:S(2)}, u32[]{:S(2)}) %collective-permute-start.14) | collective-permute-done | bytes 147488 | tf_op jit(solution)/shard_map/ppermute | solution.py:368
  47.8 1.1 %shard_map.100 = (bf16[64,2048]{1,0:T(8,128)(2,1)S(1)}, bf16[448,1024]{1,0:T(8,128)(2,1)S(1)}) custom-call(s32[2]{0:T(128)S(1)} %copy-done.2, s32[2]{0:T(128)S(1)} %copy-done.3, f32[64,1024]{1,0:T(8,128)S(1)} %get-tuple-element.69.own, f32[64,128]{1,0:T(8,128)S(1)} %get-tuple-element.70.refs_0_.lse, ...), custom_call_target="tpu_custom_call", output_to_operand_aliasing={{0}: (5, {})} | custom-call | flops 524288 | bytes 4194304 | tf_op jit(solution)/shard_map/pallas_call | solution.py:263
  48.9 0.7 collective-permute-start.22
  49.5 1.7 %collective-permute-start.16 = (bf16[64,2048]{1,0:T(8,128)(2,1)S(1)}, bf16[64,2048]{1,0:T(8,128)(2,1)S(1)}, u32[]{:S(2)}, u32[]{:S(2)}) collective-permute-start(bf16[64,2048]{1,0:T(8,128)(2,1)S(1)} %get-tuple-element.74.refs_0_), channel_id=1, source_target_pairs={{0,16},{16,32},{32,48},{48,64},{64,80},{80,96},{96,112},{112,0},{1... | collective-permute-start | bytes 786440 | tf_op jit(solution)/shard_map/ppermute | solution.py:376
  51.3 1.5 %collective-permute-start.17 = (bf16[64,2048]{1,0:T(8,128)(2,1)S(1)}, bf16[64,2048]{1,0:T(8,128)(2,1)S(1)}, u32[]{:S(2)}, u32[]{:S(2)}) collective-permute-start(bf16[64,2048]{1,0:T(8,128)(2,1)S(1)} %get-tuple-element.74.refs_0_), channel_id=1, source_target_pairs={{0,112},{16,0},{32,16},{48,32},{64,48},{80,64},{96,80},{112,96},{1... | collective-permute-start | bytes 786440 | tf_op jit(solution)/shard_map/ppermute | solution.py:376
  52.8 4.3 %collective-permute-done.16.refs_0_ = bf16[64,2048]{1,0:T(8,128)(2,1)S(1)} collective-permute-done((bf16[64,2048]{1,0:T(8,128)(2,1)S(1)}, bf16[64,2048]{1,0:T(8,128)(2,1)S(1)}, u32[]{:S(2)}, u32[]{:S(2)}) %collective-permute-start.16) | collective-permute-done | bytes 262176 | tf_op jit(solution)/shard_map/ppermute | solution.py:376
  57.1 0.5 collective-permute-done.17.refs_1_
  57.6 1.4 %collective-permute-start.18 = (bf16[64,2048]{1,0:T(8,128)(2,1)S(1)}, bf16[64,2048]{1,0:T(8,128)(2,1)S(1)}, u32[]{:S(2)}, u32[]{:S(2)}) collective-permute-start(bf16[64,2048]{1,0:T(8,128)(2,1)S(1)} %get-tuple-element.75.refs_1_), channel_id=1, source_target_pairs={{0,16},{16,32},{32,48},{48,64},{64,80},{80,96},{96,112},{112,0},{1... | collective-permute-start | bytes 786440 | tf_op jit(solution)/shard_map/ppermute | solution.py:376
  59.0 1.9 %collective-permute-start.19 = (bf16[64,2048]{1,0:T(8,128)(2,1)S(1)}, bf16[64,2048]{1,0:T(8,128)(2,1)S(1)}, u32[]{:S(2)}, u32[]{:S(2)}) collective-permute-start(bf16[64,2048]{1,0:T(8,128)(2,1)S(1)} %get-tuple-element.76.refs_6_), channel_id=1, source_target_pairs={{0,112},{16,0},{32,16},{48,32},{64,48},{80,64},{96,80},{112,96},{1... | collective-permute-start | bytes 786440 | tf_op jit(solution)/shard_map/ppermute | solution.py:376
  60.9 4.8 %collective-permute-done.18.refs_0_ = bf16[64,2048]{1,0:T(8,128)(2,1)S(1)} collective-permute-done((bf16[64,2048]{1,0:T(8,128)(2,1)S(1)}, bf16[64,2048]{1,0:T(8,128)(2,1)S(1)}, u32[]{:S(2)}, u32[]{:S(2)}) %collective-permute-start.18) | collective-permute-done | bytes 262176 | tf_op jit(solution)/shard_map/ppermute | solution.py:376
  65.7 1.2 %collective-permute-start.20 = (bf16[64,2048]{1,0:T(8,128)(2,1)S(1)}, bf16[64,2048]{1,0:T(8,128)(2,1)S(1)}, u32[]{:S(2)}, u32[]{:S(2)}) collective-permute-start(bf16[64,2048]{1,0:T(8,128)(2,1)S(1)} %get-tuple-element.77.refs_2_), channel_id=1, source_target_pairs={{0,16},{16,32},{32,48},{48,64},{64,80},{80,96},{96,112},{112,0},{1... | collective-permute-start | bytes 786440 | tf_op jit(solution)/shard_map/ppermute | solution.py:376
  66.9 2.3 %collective-permute-start.21 = (bf16[64,2048]{1,0:T(8,128)(2,1)S(1)}, bf16[64,2048]{1,0:T(8,128)(2,1)S(1)}, u32[]{:S(2)}, u32[]{:S(2)}) collective-permute-start(bf16[64,2048]{1,0:T(8,128)(2,1)S(1)} %get-tuple-element.78.refs_5_), channel_id=1, source_target_pairs={{0,112},{16,0},{32,16},{48,32},{64,48},{80,64},{96,80},{112,96},{1... | collective-permute-start | bytes 786440 | tf_op jit(solution)/shard_map/ppermute | solution.py:376
  69.2 4.3 %collective-permute-done.20.refs_0_ = bf16[64,2048]{1,0:T(8,128)(2,1)S(1)} collective-permute-done((bf16[64,2048]{1,0:T(8,128)(2,1)S(1)}, bf16[64,2048]{1,0:T(8,128)(2,1)S(1)}, u32[]{:S(2)}, u32[]{:S(2)}) %collective-permute-start.20) | collective-permute-done | bytes 262176 | tf_op jit(solution)/shard_map/ppermute | solution.py:376
  73.6 0.1 collective-permute-start.25
  73.7 1.3 %collective-permute-start.23 = (bf16[32,2048]{1,0:T(8,128)(2,1)S(1)}, bf16[32,2048]{1,0:T(8,128)(2,1)S(1)}, u32[]{:S(2)}, u32[]{:S(2)}) collective-permute-start(bf16[32,2048]{1,0:T(8,128)(2,1)S(1)} %slice.14), channel_id=1, source_target_pairs={{0,16},{16,32},{32,48},{48,64},{64,80},{80,96},{96,112},{112,0},{1... | collective-permute-start | bytes 393224 | tf_op jit(solution)/shard_map/ppermute | solution.py:376
  75.0 2.0 %collective-permute-start.24 = (bf16[32,2048]{1,0:T(8,128)(2,1)S(1)}, bf16[32,2048]{1,0:T(8,128)(2,1)S(1)}, u32[]{:S(2)}, u32[]{:S(2)}) collective-permute-start(bf16[32,2048]{1,0:T(8,128)(2,1)S(1)} %slice.15), channel_id=1, source_target_pairs={{0,112},{16,0},{32,16},{48,32},{64,48},{80,64},{96,80},{112,96},{1... | collective-permute-start | bytes 393224 | tf_op jit(solution)/shard_map/ppermute | solution.py:376
  77.1 2.2 %shard_map.104.refs_6_ = bf16[512,896]{1,0:T(8,128)(2,1)S(1)} custom-call(bf16[64,2048]{1,0:T(8,128)(2,1)S(1)} %get-tuple-element.74.refs_0_, bf16[64,2048]{1,0:T(8,128)(2,1)S(1)} %get-tuple-element.75.refs_1_, bf16[64,2048]{1,0:T(8,128)(2,1)S(1)} %get-tuple-element.77.refs_2_, bf16[64,2048]{1,0:T(8,128)(2,1)S(1)} %get-tuple-element.80.refs_3_, ...), custom_call_target="tpu_custom_call" | custom-call | flops 1644167168 | bytes 4194304 | tf_op jit(solution)/shard_map/pallas_call | solution.py:323
  79.3 1.8 %collective-permute-done.23.refs_0_ = bf16[32,2048]{1,0:T(8,128)(2,1)S(1)} collective-permute-done((bf16[32,2048]{1,0:T(8,128)(2,1)S(1)}, bf16[32,2048]{1,0:T(8,128)(2,1)S(1)}, u32[]{:S(2)}, u32[]{:S(2)}) %collective-permute-start.23) | collective-permute-done | bytes 131104 | tf_op jit(solution)/shard_map/ppermute | solution.py:376
  81.1 1.3 %shard_map.105 = (bf16[64,896]{1,0:T(8,128)(2,1)S(1)}, bf16[64,896]{1,0:T(8,128)(2,1)S(1)}, bf16[64,896]{1,0:T(8,128)(2,1)S(1)}, bf16[64,896]{1,0:T(8,128)(2,1)S...) custom-call(bf16[32,2048]{1,0:T(8,128)(2,1)S(1)} %collective-permute, ...), custom_call_target="tpu_custom_call", output_to_operand_aliasing={{8}: (6, {})} | custom-call | flops 234881024 | bytes 4194304 | tf_op jit(solution)/shard_map/pallas_call | solution.py:339
  82.4 1.6 %collective-permute-start.26 = (bf16[64,896]{1,0:T(8,128)(2,1)S(1)}, bf16[64,896]{1,0:T(8,128)(2,1)S(1)}, u32[]{:S(2)}, u32[]{:S(2)}) collective-permute-start(bf16[64,896]{1,0:T(8,128)(2,1)S(1)} %get-tuple-element.84), channel_id=1, source_target_pairs={{0,2},{1,3},{2,0},{3,1},{4,6},{5,7},{6,4},{7,5},{8,10},{9,11},{10,... | collective-permute-start | bytes 344072 | tf_op jit(solution)/shard_map/ppermute | solution.py:389
  84.0 2.1 %collective-permute-start.27 = (bf16[64,896]{1,0:T(8,128)(2,1)S(1)}, bf16[64,896]{1,0:T(8,128)(2,1)S(1)}, u32[]{:S(2)}, u32[]{:S(2)}) collective-permute-start(bf16[64,896]{1,0:T(8,128)(2,1)S(1)} %get-tuple-element.85), channel_id=1, source_target_pairs={{0,6},{1,7},{2,4},{3,5},{4,2},{5,3},{6,0},{7,1},{8,14},{9,15},{10,... | collective-permute-start | bytes 344072 | tf_op jit(solution)/shard_map/ppermute | solution.py:389
  86.1 0.6 collective-permute-start.28
  86.7 1.5 %collective-permute-start.30 = (bf16[64,896]{1,0:T(8,128)(2,1)S(1)}, bf16[64,896]{1,0:T(8,128)(2,1)S(1)}, u32[]{:S(2)}, u32[]{:S(2)}) collective-permute-start(bf16[64,896]{1,0:T(8,128)(2,1)S(1)} %get-tuple-element.88), channel_id=1, source_target_pairs={{0,3},{1,2},{2,1},{3,0},{4,7},{5,6},{6,5},{7,4},{8,11},{9,10},{10,... | collective-permute-start | bytes 344072 | tf_op jit(solution)/shard_map/ppermute | solution.py:389
  88.2 1.7 %collective-permute-start.31 = (bf16[64,896]{1,0:T(8,128)(2,1)S(1)}, bf16[64,896]{1,0:T(8,128)(2,1)S(1)}, u32[]{:S(2)}, u32[]{:S(2)}) collective-permute-start(bf16[64,896]{1,0:T(8,128)(2,1)S(1)} %get-tuple-element.89), channel_id=1, source_target_pairs={{0,7},{1,6},{2,5},{3,4},{4,3},{5,2},{6,1},{7,0},{8,15},{9,14},{10,... | collective-permute-start | bytes 344072 | tf_op jit(solution)/shard_map/ppermute | solution.py:389
  89.9 2.0 %collective-permute-done.27.refs_2_ = bf16[64,896]{1,0:T(8,128)(2,1)S(1)} collective-permute-done((bf16[64,896]{1,0:T(8,128)(2,1)S(1)}, bf16[64,896]{1,0:T(8,128)(2,1)S(1)}, u32[]{:S(2)}, u32[]{:S(2)}) %collective-permute-start.27) | collective-permute-done | bytes 114720 | tf_op jit(solution)/shard_map/ppermute | solution.py:389
  91.8 1.2 %collective-permute-done.28.refs_3_ = bf16[64,896]{1,0:T(8,128)(2,1)S(1)} collective-permute-done((bf16[64,896]{1,0:T(8,128)(2,1)S(1)}, bf16[64,896]{1,0:T(8,128)(2,1)S(1)}, u32[]{:S(2)}, u32[]{:S(2)}) %collective-permute-start.28) | collective-permute-done | bytes 114720 | tf_op jit(solution)/shard_map/ppermute | solution.py:389
  93.0 2.0 %collective-permute-done.31.refs_6_ = bf16[64,896]{1,0:T(8,128)(2,1)S(1)} collective-permute-done((bf16[64,896]{1,0:T(8,128)(2,1)S(1)}, bf16[64,896]{1,0:T(8,128)(2,1)S(1)}, u32[]{:S(2)}, u32[]{:S(2)}) %collective-permute-start.31) | collective-permute-done | bytes 114720 | tf_op jit(solution)/shard_map/ppermute | solution.py:389
  95.1 2.9 %collective-permute-done.32.refs_7_ = bf16[64,896]{1,0:T(8,128)(2,1)S(1)} collective-permute-done((bf16[64,896]{1,0:T(8,128)(2,1)S(1)}, bf16[64,896]{1,0:T(8,128)(2,1)S(1)}, u32[]{:S(2)}, u32[]{:S(2)}) %collective-permute-start.32) | collective-permute-done | bytes 114720 | tf_op jit(solution)/shard_map/ppermute | solution.py:389
  97.9 0.2 shard_map.106
  98.1 3.8 %collective-permute-start.33 = (bf16[2,64,448]{2,1,0:T(8,128)(2,1)S(1)}, bf16[2,64,448]{2,1,0:T(8,128)(2,1)S(1)}, u32[]{:S(2)}, u32[]{:S(2)}) collective-permute-start(bf16[2,64,448]{2,1,0:T(8,128)(2,1)S(1)} %get-tuple-element.91), channel_id=1, source_target_pairs={{8,128},{128,8},{9,129},{129,9},{10,130},{130,10},{11,131},{131,11... | collective-permute-start | bytes 344072 | tf_op jit(solution)/shard_map/ppermute | solution.py:498
  102.0 0.1 collective-permute-start.34
  102.1 2.9 %collective-permute-done.33 = bf16[2,64,448]{2,1,0:T(8,128)(2,1)S(1)} collective-permute-done((bf16[2,64,448]{2,1,0:T(8,128)(2,1)S(1)}, bf16[2,64,448]{2,1,0:T(8,128)(2,1)S(1)}, u32[]{:S(2)}, u32[]{:S(2)}) %collective-permute-start.33) | collective-permute-done | bytes 114720 | tf_op jit(solution)/shard_map/ppermute | solution.py:498
  105.0 2.0 %collective-permute-done.34 = bf16[2,64,448]{2,1,0:T(8,128)(2,1)S(1)} collective-permute-done((bf16[2,64,448]{2,1,0:T(8,128)(2,1)S(1)}, bf16[2,64,448]{2,1,0:T(8,128)(2,1)S(1)}, u32[]{:S(2)}, u32[]{:S(2)}) %collective-permute-start.34) | collective-permute-done | bytes 114720 | tf_op jit(solution)/shard_map/ppermute | solution.py:499
  107.0 0.7 add_convert_fusion
  (35 shorter events, 0.1 us)
Async XLA Ops:
  0.0 23.8 %copy-start.2 = (s32[2]{0:T(128)S(1)}, s32[2]{0:T(128)}, u32[]{:S(2)}) copy-start(s32[2]{0:T(128)} %starts.3) | copy-start | bytes 28
  0.0 27.7 %collective-permute-start.10 = (bf16[512,1024]{1,0:T(8,128)(2,1)}, bf16[512,1024]{1,0:T(8,128)(2,1)S(1)}, u32[]{:S(2)}, u32[]{:S(2)}) collective-permute-start(bf16[512,1024]{1,0:T(8,128)(2,1)} %refs_4_.1), channel_id=1, source_target_pairs={{0,1},{1,0},{2,3},{3,2},{4,5},{5,4},{6,7},{7,6},{8,9},{9,8},{10,11... | collective-permute-start | bytes 3145736 | tf_op jit(solution)/shard_map/ppermute | solution.py:368
  0.0 27.7 %collective-permute-start.4 = (bf16[512,1024]{1,0:T(8,128)(2,1)}, bf16[512,1024]{1,0:T(8,128)(2,1)S(1)}, u32[]{:S(2)}, u32[]{:S(2)}) collective-permute-start(bf16[512,1024]{1,0:T(8,128)(2,1)} %w.1), channel_id=1, source_target_pairs={{0,1},{1,0},{2,3},{3,2},{4,5},{5,4},{6,7},{7,6},{8,9},{9,8},{10,11... | collective-permute-start | bytes 3145736 | tf_op jit(solution)/shard_map/ppermute | solution.py:368
  2.1 10.8 %collective-permute-start.2 = (bf16[64,1536]{1,0:T(8,128)(2,1)S(1)}, bf16[64,1536]{1,0:T(8,128)(2,1)S(1)}, u32[]{:S(2)}, u32[]{:S(2)}) collective-permute-start(bf16[64,1536]{1,0:T(8,128)(2,1)S(1)} %get-tuple-element.50), channel_id=1, source_target_pairs={{0,1},{1,0},{2,3},{3,2},{4,5},{5,4},{6,7},{7,6},{8,9},{9,8},{10,11... | collective-permute-start | bytes 589832 | tf_op jit(solution)/shard_map/ppermute | solution.py:368
  2.3 10.6 %collective-permute-start = (bf16[128,576]{1,0:T(8,128)(2,1)S(1)}, bf16[128,576]{1,0:T(8,128)(2,1)S(1)}, u32[]{:S(2)}, u32[]{:S(2)}) collective-permute-start(bf16[128,576]{1,0:T(8,128)(2,1)S(1)} %get-tuple-element.49.refs_4_), channel_id=1, source_target_pairs={{0,16},{16,32},{32,48},{48,64},{64,80},{80,96},{96,112},{112,0},{1... | collective-permute-start | bytes 442376 | tf_op jit(solution)/shard_map/ppermute | solution.py:376
  4.2 8.7 %collective-permute-start.1 = (bf16[128,576]{1,0:T(8,128)(2,1)S(1)}, bf16[128,576]{1,0:T(8,128)(2,1)S(1)}, u32[]{:S(2)}, u32[]{:S(2)}) collective-permute-start(bf16[128,576]{1,0:T(8,128)(2,1)S(1)} %get-tuple-element.49.refs_4_), channel_id=1, source_target_pairs={{0,112},{16,0},{32,16},{48,32},{64,48},{80,64},{96,80},{112,96},{1... | collective-permute-start | bytes 442376 | tf_op jit(solution)/shard_map/ppermute | solution.py:376
  12.9 7.2 %collective-permute-start.5 = (bf16[128,576]{1,0:T(8,128)(2,1)S(1)}, bf16[128,576]{1,0:T(8,128)(2,1)S(1)}, u32[]{:S(2)}, u32[]{:S(2)}) collective-permute-start(bf16[128,576]{1,0:T(8,128)(2,1)S(1)} %get-tuple-element.52.refs_5_.refs_8_), channel_id=1, source_target_pairs={{0,16},{16,32},{32,48},{48,64},{64,80},{80,96},{96,112},{112,0},{1... | collective-permute-start | bytes 442376 | tf_op jit(solution)/shard_map/ppermute | solution.py:376
  13.0 9.4 %collective-permute-start.9 = (bf16[64,1536]{1,0:T(8,128)(2,1)S(1)}, bf16[64,1536]{1,0:T(8,128)(2,1)S(1)}, u32[]{:S(2)}, u32[]{:S(2)}) collective-permute-start(bf16[64,1536]{1,0:T(8,128)(2,1)S(1)} %get-tuple-element.56.refs_1_), channel_id=1, source_target_pairs={{0,128},{128,0},{1,129},{129,1},{2,130},{130,2},{3,131},{131,3},{4... | collective-permute-start | bytes 589832 | tf_op jit(solution)/shard_map/ppermute | solution.py:368
  13.5 7.1 %collective-permute-start.6 = (bf16[128,576]{1,0:T(8,128)(2,1)S(1)}, bf16[128,576]{1,0:T(8,128)(2,1)S(1)}, u32[]{:S(2)}, u32[]{:S(2)}) collective-permute-start(bf16[128,576]{1,0:T(8,128)(2,1)S(1)} %get-tuple-element.53.refs_7_), channel_id=1, source_target_pairs={{0,112},{16,0},{32,16},{48,32},{64,48},{80,64},{96,80},{112,96},{1... | collective-permute-start | bytes 442376 | tf_op jit(solution)/shard_map/ppermute | solution.py:376
  20.1 6.3 %collective-permute-start.3 = (bf16[64,1536]{1,0:T(8,128)(2,1)S(1)}, bf16[64,1536]{1,0:T(8,128)(2,1)S(1)}, u32[]{:S(2)}, u32[]{:S(2)}) collective-permute-start(bf16[64,1536]{1,0:T(8,128)(2,1)S(1)} %get-tuple-element.51.refs_1_), channel_id=1, source_target_pairs={{0,128},{128,0},{1,129},{129,1},{2,130},{130,2},{3,131},{131,3},{4... | collective-permute-start | bytes 589832 | tf_op jit(solution)/shard_map/ppermute | solution.py:368
  20.6 6.5 %collective-permute-start.7 = (bf16[128,576]{1,0:T(8,128)(2,1)S(1)}, bf16[128,576]{1,0:T(8,128)(2,1)S(1)}, u32[]{:S(2)}, u32[]{:S(2)}) collective-permute-start(bf16[128,576]{1,0:T(8,128)(2,1)S(1)} %get-tuple-element.54.refs_6_), channel_id=1, source_target_pairs={{0,16},{16,32},{32,48},{48,64},{64,80},{80,96},{96,112},{112,0},{1... | collective-permute-start | bytes 442376 | tf_op jit(solution)/shard_map/ppermute | solution.py:376
  22.4 5.3 %collective-permute-start.8 = (bf16[128,576]{1,0:T(8,128)(2,1)S(1)}, bf16[128,576]{1,0:T(8,128)(2,1)S(1)}, u32[]{:S(2)}, u32[]{:S(2)}) collective-permute-start(bf16[128,576]{1,0:T(8,128)(2,1)S(1)} %get-tuple-element.55.refs_5_), channel_id=1, source_target_pairs={{0,112},{16,0},{32,16},{48,32},{64,48},{80,64},{96,80},{112,96},{1... | collective-permute-start | bytes 442376 | tf_op jit(solution)/shard_map/ppermute | solution.py:376
  27.7 11.8 %collective-permute-start.13 = (bf16[448,1024]{1,0:T(8,128)(2,1)S(1)}, bf16[448,1024]{1,0:T(8,128)(2,1)S(1)}, u32[]{:S(2)}, u32[]{:S(2)}) collective-permute-start(bf16[448,1024]{1,0:T(8,128)(2,1)S(1)} %get-tuple-element.68), channel_id=1, source_target_pairs={{0,1},{1,0},{2,3},{3,2},{4,5},{5,4},{6,7},{7,6},{8,9},{9,8},{10,11... | collective-permute-start | bytes 2752520 | tf_op jit(solution)/shard_map/ppermute | solution.py:368
  27.8 6.2 %collective-permute-start.11 = (bf16[64,576]{1,0:T(8,128)(2,1)S(1)}, bf16[64,576]{1,0:T(8,128)(2,1)S(1)}, u32[]{:S(2)}, u32[]{:S(2)}) collective-permute-start(bf16[64,576]{1,0:T(8,128)(2,1)S(1)} %slice.12), channel_id=1, source_target_pairs={{0,16},{16,32},{32,48},{48,64},{64,80},{80,96},{96,112},{112,0},{1... | collective-permute-start | bytes 221192 | tf_op jit(solution)/shard_map/ppermute | solution.py:376
  29.9 4.9 %copy-start = (bf16[512,1024]{1,0:T(8,128)(2,1)S(1)}, bf16[512,1024]{1,0:T(8,128)(2,1)}, u32[]{:S(2)}) copy-start(bf16[512,1024]{1,0:T(8,128)(2,1)} %refs_4_.1) | copy-start | bytes 3145732
  29.9 4.9 %collective-permute-start.12 = (bf16[64,576]{1,0:T(8,128)(2,1)S(1)}, bf16[64,576]{1,0:T(8,128)(2,1)S(1)}, u32[]{:S(2)}, u32[]{:S(2)}) collective-permute-start(bf16[64,576]{1,0:T(8,128)(2,1)S(1)} %slice.13), channel_id=1, source_target_pairs={{0,112},{16,0},{32,16},{48,32},{64,48},{80,64},{96,80},{112,96},{1... | collective-permute-start | bytes 221192 | tf_op jit(solution)/shard_map/ppermute | solution.py:376
  37.9 5.4 %collective-permute-start.15 = (bf16[64,1152]{1,0:T(8,128)(2,1)S(1)}, bf16[64,1152]{1,0:T(8,128)(2,1)S(1)}, u32[]{:S(2)}, u32[]{:S(2)}) collective-permute-start(bf16[64,1152]{1,0:T(8,128)(2,1)S(1)} %get-tuple-element.73), channel_id=1, source_target_pairs={{0,128},{128,0},{1,129},{129,1},{2,130},{130,2},{3,131},{131,3},{4... | collective-permute-start | bytes 442376 | tf_op jit(solution)/shard_map/ppermute | solution.py:368
  39.5 3.8 %copy-start.3 = (s32[2]{0:T(128)S(1)}, s32[2]{0:T(128)}, u32[]{:S(2)}) copy-start(s32[2]{0:T(128)} %lens.3) | copy-start | bytes 28
  39.5 8.3 %copy-start.1 = (bf16[1024,448]{0,1:T(8,128)(2,1)S(1)}, bf16[1024,448]{0,1:T(8,128)(2,1)}, u32[]{:S(2)}) copy-start(bf16[1024,448]{0,1:T(8,128)(2,1)} %param.15) | copy-start | bytes 2752516
  42.5 5.2 %collective-permute-start.14 = (bf16[64,1152]{1,0:T(8,128)(2,1)S(1)}, bf16[64,1152]{1,0:T(8,128)(2,1)S(1)}, u32[]{:S(2)}, u32[]{:S(2)}) collective-permute-start(bf16[64,1152]{1,0:T(8,128)(2,1)S(1)} %get-tuple-element.71), channel_id=1, source_target_pairs={{0,128},{128,0},{1,129},{129,1},{2,130},{130,2},{3,131},{131,3},{4... | collective-permute-start | bytes 442376 | tf_op jit(solution)/shard_map/ppermute | solution.py:368
  48.9 24.7 %collective-permute-start.22 = (bf16[448,1024]{1,0:T(8,128)(2,1)S(1)}, bf16[448,1024]{1,0:T(8,128)(2,1)S(1)}, u32[]{:S(2)}, u32[]{:S(2)}) collective-permute-start(bf16[448,1024]{1,0:T(8,128)(2,1)S(1)} %get-tuple-element.79.refs_7_.refs_2_), channel_id=1, source_target_pairs={{0,128},{128,0},{1,129},{129,1},{2,130},{130,2},{3,131},{131,3},{4... | collective-permute-start | bytes 2752520 | tf_op jit(solution)/shard_map/ppermute | solution.py:368
  49.5 7.6 %collective-permute-start.16 = (bf16[64,2048]{1,0:T(8,128)(2,1)S(1)}, bf16[64,2048]{1,0:T(8,128)(2,1)S(1)}, u32[]{:S(2)}, u32[]{:S(2)}) collective-permute-start(bf16[64,2048]{1,0:T(8,128)(2,1)S(1)} %get-tuple-element.74.refs_0_), channel_id=1, source_target_pairs={{0,16},{16,32},{32,48},{48,64},{64,80},{80,96},{96,112},{112,0},{1... | collective-permute-start | bytes 786440 | tf_op jit(solution)/shard_map/ppermute | solution.py:376
  51.3 6.4 %collective-permute-start.17 = (bf16[64,2048]{1,0:T(8,128)(2,1)S(1)}, bf16[64,2048]{1,0:T(8,128)(2,1)S(1)}, u32[]{:S(2)}, u32[]{:S(2)}) collective-permute-start(bf16[64,2048]{1,0:T(8,128)(2,1)S(1)} %get-tuple-element.74.refs_0_), channel_id=1, source_target_pairs={{0,112},{16,0},{32,16},{48,32},{64,48},{80,64},{96,80},{112,96},{1... | collective-permute-start | bytes 786440 | tf_op jit(solution)/shard_map/ppermute | solution.py:376
  57.6 8.1 %collective-permute-start.18 = (bf16[64,2048]{1,0:T(8,128)(2,1)S(1)}, bf16[64,2048]{1,0:T(8,128)(2,1)S(1)}, u32[]{:S(2)}, u32[]{:S(2)}) collective-permute-start(bf16[64,2048]{1,0:T(8,128)(2,1)S(1)} %get-tuple-element.75.refs_1_), channel_id=1, source_target_pairs={{0,16},{16,32},{32,48},{48,64},{64,80},{80,96},{96,112},{112,0},{1... | collective-permute-start | bytes 786440 | tf_op jit(solution)/shard_map/ppermute | solution.py:376
  59.0 6.7 %collective-permute-start.19 = (bf16[64,2048]{1,0:T(8,128)(2,1)S(1)}, bf16[64,2048]{1,0:T(8,128)(2,1)S(1)}, u32[]{:S(2)}, u32[]{:S(2)}) collective-permute-start(bf16[64,2048]{1,0:T(8,128)(2,1)S(1)} %get-tuple-element.76.refs_6_), channel_id=1, source_target_pairs={{0,112},{16,0},{32,16},{48,32},{64,48},{80,64},{96,80},{112,96},{1... | collective-permute-start | bytes 786440 | tf_op jit(solution)/shard_map/ppermute | solution.py:376
  65.7 7.9 %collective-permute-start.20 = (bf16[64,2048]{1,0:T(8,128)(2,1)S(1)}, bf16[64,2048]{1,0:T(8,128)(2,1)S(1)}, u32[]{:S(2)}, u32[]{:S(2)}) collective-permute-start(bf16[64,2048]{1,0:T(8,128)(2,1)S(1)} %get-tuple-element.77.refs_2_), channel_id=1, source_target_pairs={{0,16},{16,32},{32,48},{48,64},{64,80},{80,96},{96,112},{112,0},{1... | collective-permute-start | bytes 786440 | tf_op jit(solution)/shard_map/ppermute | solution.py:376
  66.9 6.7 %collective-permute-start.21 = (bf16[64,2048]{1,0:T(8,128)(2,1)S(1)}, bf16[64,2048]{1,0:T(8,128)(2,1)S(1)}, u32[]{:S(2)}, u32[]{:S(2)}) collective-permute-start(bf16[64,2048]{1,0:T(8,128)(2,1)S(1)} %get-tuple-element.78.refs_5_), channel_id=1, source_target_pairs={{0,112},{16,0},{32,16},{48,32},{64,48},{80,64},{96,80},{112,96},{1... | collective-permute-start | bytes 786440 | tf_op jit(solution)/shard_map/ppermute | solution.py:376
  73.6 3.5 %collective-permute-start.25 = (bf16[448,1024]{1,0:T(8,128)(2,1)S(1)}, bf16[448,1024]{1,0:T(8,128)(2,1)S(1)}, u32[]{:S(2)}, u32[]{:S(2)}) collective-permute-start(bf16[448,1024]{1,0:T(8,128)(2,1)S(1)} %get-tuple-element.82.refs_8_.refs_3_), channel_id=1, source_target_pairs={{0,1},{1,0},{2,3},{3,2},{4,5},{5,4},{6,7},{7,6},{8,9},{9,8},{10,11... | collective-permute-start | bytes 2752520 | tf_op jit(solution)/shard_map/ppermute | solution.py:368
  73.7 7.4 %collective-permute-start.23 = (bf16[32,2048]{1,0:T(8,128)(2,1)S(1)}, bf16[32,2048]{1,0:T(8,128)(2,1)S(1)}, u32[]{:S(2)}, u32[]{:S(2)}) collective-permute-start(bf16[32,2048]{1,0:T(8,128)(2,1)S(1)} %slice.14), channel_id=1, source_target_pairs={{0,16},{16,32},{32,48},{48,64},{64,80},{80,96},{96,112},{112,0},{1... | collective-permute-start | bytes 393224 | tf_op jit(solution)/shard_map/ppermute | solution.py:376
  75.0 6.0 %collective-permute-start.24 = (bf16[32,2048]{1,0:T(8,128)(2,1)S(1)}, bf16[32,2048]{1,0:T(8,128)(2,1)S(1)}, u32[]{:S(2)}, u32[]{:S(2)}) collective-permute-start(bf16[32,2048]{1,0:T(8,128)(2,1)S(1)} %slice.15), channel_id=1, source_target_pairs={{0,112},{16,0},{32,16},{48,32},{64,48},{80,64},{96,80},{112,96},{1... | collective-permute-start | bytes 393224 | tf_op jit(solution)/shard_map/ppermute | solution.py:376
  82.4 5.8 %collective-permute-start.26 = (bf16[64,896]{1,0:T(8,128)(2,1)S(1)}, bf16[64,896]{1,0:T(8,128)(2,1)S(1)}, u32[]{:S(2)}, u32[]{:S(2)}) collective-permute-start(bf16[64,896]{1,0:T(8,128)(2,1)S(1)} %get-tuple-element.84), channel_id=1, source_target_pairs={{0,2},{1,3},{2,0},{3,1},{4,6},{5,7},{6,4},{7,5},{8,10},{9,11},{10,... | collective-permute-start | bytes 344072 | tf_op jit(solution)/shard_map/ppermute | solution.py:389
  84.0 7.9 %collective-permute-start.27 = (bf16[64,896]{1,0:T(8,128)(2,1)S(1)}, bf16[64,896]{1,0:T(8,128)(2,1)S(1)}, u32[]{:S(2)}, u32[]{:S(2)}) collective-permute-start(bf16[64,896]{1,0:T(8,128)(2,1)S(1)} %get-tuple-element.85), channel_id=1, source_target_pairs={{0,6},{1,7},{2,4},{3,5},{4,2},{5,3},{6,0},{7,1},{8,14},{9,15},{10,... | collective-permute-start | bytes 344072 | tf_op jit(solution)/shard_map/ppermute | solution.py:389
  86.1 6.9 %collective-permute-start.28 = (bf16[64,896]{1,0:T(8,128)(2,1)S(1)}, bf16[64,896]{1,0:T(8,128)(2,1)S(1)}, u32[]{:S(2)}, u32[]{:S(2)}) collective-permute-start(bf16[64,896]{1,0:T(8,128)(2,1)S(1)} %get-tuple-element.86), channel_id=1, source_target_pairs={{0,4},{1,5},{2,6},{3,7},{4,0},{5,1},{6,2},{7,3},{8,12},{9,13},{10,... | collective-permute-start | bytes 344072 | tf_op jit(solution)/shard_map/ppermute | solution.py:389
  86.7 6.3 %collective-permute-start.29 = (bf16[64,896]{1,0:T(8,128)(2,1)S(1)}, bf16[64,896]{1,0:T(8,128)(2,1)S(1)}, u32[]{:S(2)}, u32[]{:S(2)}) collective-permute-start(bf16[64,896]{1,0:T(8,128)(2,1)S(1)} %get-tuple-element.87), channel_id=1, source_target_pairs={{0,1},{1,0},{2,3},{3,2},{4,5},{5,4},{6,7},{7,6},{8,9},{9,8},{10,11... | collective-permute-start | bytes 344072 | tf_op jit(solution)/shard_map/ppermute | solution.py:368
  86.7 6.3 %collective-permute-start.30 = (bf16[64,896]{1,0:T(8,128)(2,1)S(1)}, bf16[64,896]{1,0:T(8,128)(2,1)S(1)}, u32[]{:S(2)}, u32[]{:S(2)}) collective-permute-start(bf16[64,896]{1,0:T(8,128)(2,1)S(1)} %get-tuple-element.88), channel_id=1, source_target_pairs={{0,3},{1,2},{2,1},{3,0},{4,7},{5,6},{6,5},{7,4},{8,11},{9,10},{10,... | collective-permute-start | bytes 344072 | tf_op jit(solution)/shard_map/ppermute | solution.py:389
  88.2 6.9 %collective-permute-start.31 = (bf16[64,896]{1,0:T(8,128)(2,1)S(1)}, bf16[64,896]{1,0:T(8,128)(2,1)S(1)}, u32[]{:S(2)}, u32[]{:S(2)}) collective-permute-start(bf16[64,896]{1,0:T(8,128)(2,1)S(1)} %get-tuple-element.89), channel_id=1, source_target_pairs={{0,7},{1,6},{2,5},{3,4},{4,3},{5,2},{6,1},{7,0},{8,15},{9,14},{10,... | collective-permute-start | bytes 344072 | tf_op jit(solution)/shard_map/ppermute | solution.py:389
  91.8 6.1 %collective-permute-start.32 = (bf16[64,896]{1,0:T(8,128)(2,1)S(1)}, bf16[64,896]{1,0:T(8,128)(2,1)S(1)}, u32[]{:S(2)}, u32[]{:S(2)}) collective-permute-start(bf16[64,896]{1,0:T(8,128)(2,1)S(1)} %get-tuple-element.90), channel_id=1, source_target_pairs={{0,5},{1,4},{2,7},{3,6},{4,1},{5,0},{6,3},{7,2},{8,13},{9,12},{10,... | collective-permute-start | bytes 344072 | tf_op jit(solution)/shard_map/ppermute | solution.py:389
  98.1 6.9 %collective-permute-start.33 = (bf16[2,64,448]{2,1,0:T(8,128)(2,1)S(1)}, bf16[2,64,448]{2,1,0:T(8,128)(2,1)S(1)}, u32[]{:S(2)}, u32[]{:S(2)}) collective-permute-start(bf16[2,64,448]{2,1,0:T(8,128)(2,1)S(1)} %get-tuple-element.91), channel_id=1, source_target_pairs={{8,128},{128,8},{9,129},{129,9},{10,130},{130,10},{11,131},{131,11... | collective-permute-start | bytes 344072 | tf_op jit(solution)/shard_map/ppermute | solution.py:498
  102.0 5.0 %collective-permute-start.34 = (bf16[2,64,448]{2,1,0:T(8,128)(2,1)S(1)}, bf16[2,64,448]{2,1,0:T(8,128)(2,1)S(1)}, u32[]{:S(2)}, u32[]{:S(2)}) collective-permute-start(bf16[2,64,448]{2,1,0:T(8,128)(2,1)S(1)} %get-tuple-element.92), channel_id=1, source_target_pairs={{0,128},{128,136},{8,0},{136,8},{1,129},{129,137},{9,1},{137,9},{2... | collective-permute-start | bytes 344072 | tf_op jit(solution)/shard_map/ppermute | solution.py:499
